TPU v7x, 32 devices: a whole 2x2x4 slice. The times are simulated.
32 devices in a mesh: height: 2 (over core), plane: 16 (over z, y, x).
Axes of the slice: x: 2, y: 2, z: 4, core: 2. Of those that a mesh axis runs over, the one named last changes fastest.
Arguments:
- cotangent: float32 [32, 128, 128], P('height', 'plane'), may hold values from -36 to 36
- conductivity: float32 [4, 16, 16], P('height', 'plane'), may hold values from 0.2 to 5
- capacity: float32 [4, 16, 16], P('height', 'plane'), may hold values from 0.5 to 2
- sources: int32 [2, 128], replicated, may hold values from 0 to 1023
Outputs:
- adjoint_second: float32 [32, 128, 128], P('height', 'plane')
- adjoint_first: float32 [32, 128, 128], P('height', 'plane')
- source_grad: float32 [2, 128], replicated
Inputs may be any that keep to these rules, and one draw needn't show every extreme that they name: `sources`: element numbers; element (ez, ex, ey) has number (ez * 16 + ex) * 16 + ey, and a number may repeat.
All inputs are finite; a program needn't handle non-finite values.
Results may differ from a plain program's by a relative error of at most 0.0001.
Values sent between devices are 32-bit elements; how exact they have to be, the bound alone decides.
No kernel may reach another device: no remote copies, remote signals or barrier semaphores. Data moves between devices by JAX's collectives and lax.ppermute only.
A program may use at most 64 MiB of HBM per device.

v0:
```python
import functools

import jax
import jax.numpy as jnp
import ml_dtypes
import numpy as np
from jax import lax
from jax.experimental import pallas as pl
from jax.experimental.pallas import tpu as pltpu
from jax.sharding import PartitionSpec as P

INV_STEP = 20.0
SHIFTS = (0.5, 1.5)
GROUP = 4
REACH = 4
TERMS = ((0, 0), (0, 1), (0, 2), (1, 0), (1, 1), (2, 0))
PAIRS = ((0, 0), (0, 1), (0, 2), (1, 1), (1, 2), (2, 2))
HIGHEST = lax.Precision.HIGHEST
F32 = jnp.float32


def gll_tables():
    points = np.array([-1.0, -0.8717401485096066, -0.5917001814331423, -0.2092992179024789, 0.2092992179024789, 0.5917001814331423, 0.8717401485096066, 1.0])
    weights = np.array([1.0 / 28.0, 0.2107042271435061, 0.3411226924835044, 0.4124587946587038, 0.4124587946587038, 0.3411226924835044, 0.2107042271435061, 1.0 / 28.0])
    product = np.array([np.prod([points[col] - points[others] for others in range(8) if others != col]) for col in range(8)])
    derivative = np.zeros((8, 8))
    for row in range(8):
        for col in range(8):
            if row != col:
                derivative[row, col] = product[row] / (product[col] * (points[row] - points[col]))
        derivative[row, row] = -np.sum(derivative[row])
    return derivative, weights, np.sum(derivative**2 * weights[:, None], axis=0)


def pieces(matrix):
    out, rest = [], matrix
    for _ in range(3):
        piece = rest.astype(ml_dtypes.bfloat16)
        out.append(piece)
        rest = rest - piece.astype(np.float64)
    return out


def tables(span):
    derivative, weights, stiff = gll_tables()
    line = (derivative.T * weights) @ derivative / weights[:, None]
    eye = np.eye(8)
    face = pieces(np.kron(line, eye) + np.kron(eye, line))
    face_mat = np.concatenate([face[m] for m, _ in TERMS], axis=1)
    row = pieces(np.kron(np.eye(span // 8), line.T))
    row_a = np.concatenate([np.concatenate([row[0], row[1]], 1)] * 2, axis=0)
    row_b = np.concatenate([row[2], row[0]], axis=0)
    tile = np.tile(weights, span // 8)
    ratio = stiff / weights
    omega = weights[:, None, None] * weights[None, :, None] * tile[None, None, :]
    quot = ratio[:, None, None] + ratio[None, :, None] + np.tile(ratio, span // 8)[None, None, :]
    return face_mat, row_a, row_b, omega.astype(np.float32), quot.astype(np.float32)


def swap(value, axis, pairs):
    if not pairs:
        return None
    return lax.ppermute(value, axis, [*pairs, *((b, a) for a, b in pairs)])


def pack_kernel(cot_ref, kap_ref, cap_ref, out_ref):
    depth, _, span = cot_ref.shape
    elems, _, parts = kap_ref.shape
    out_ref[: depth * 8, :] = cot_ref[...].reshape(depth * 8, span)
    spread = (lax.broadcasted_iota(jnp.int32, (parts, span), 1) // 8 == lax.broadcasted_iota(jnp.int32, (parts, span), 0)).astype(F32)
    coef = jnp.concatenate([kap_ref[...].reshape(elems, parts), cap_ref[...].reshape(elems, parts)], axis=0)
    rows = out_ref.shape[0] - depth * 8
    if rows > 2 * elems:
        coef = jnp.concatenate([coef, jnp.zeros((rows - 2 * elems, parts), F32)], axis=0)
    out_ref[depth * 8 :, :] = jnp.dot(coef, spread, precision=HIGHEST, preferred_element_type=F32)


class Layout:
    def __init__(self):
        wide = 2 * REACH + 1
        self.wide = wide
        self.cot = 0
        self.sums = self.cot + 3 * GROUP + 2
        self.minv = self.sums + wide + 2
        self.ratio = self.minv + wide
        self.basis = self.ratio + 5
        self.second = self.basis + 3 * wide
        self.total = self.second + wide


def basis_kernel(counts, sent, *refs):
    height, plane = counts
    lay = Layout()
    wide = lay.wide
    n_in = sum(1 for arr in sent if arr is not None) * height
    msgs = refs[:n_in]
    face_ref, row_a_ref, row_b_ref, omega_ref, quot_ref = refs[n_in : n_in + 5]
    fields_ref, info_ref = refs[n_in + 5 : n_in + 7]
    pool, coef, weigh = refs[n_in + 7 :]
    depth, _, span = pool.shape[1:]
    own_depth = depth // height
    elems = depth // 8
    own_elems = elems // height
    height_pos = lax.axis_index("height")
    plane_pos = lax.axis_index("plane")
    member = lax.rem(plane_pos, GROUP)
    group = plane_pos // GROUP
    even = lax.rem(group, 2) == 0
    early = lax.rem(group // 2, 2) == 0

    def stage(msg, piece, slot, block):
        rows = own_depth * 8 + (-(-(2 * own_elems) // 8)) * 8
        top = piece * rows
        pool[lay.cot + slot, pl.ds(block * own_depth, own_depth)] = msg[top : top + own_depth * 8, :].reshape(own_depth, 8, span)
        for kind in range(2):
            for elem in range(own_elems):
                at = top + own_depth * 8 + kind * own_elems + elem
                coef[slot, kind, block * own_elems + elem] = jnp.broadcast_to(msg[at : at + 1, :], (8, span))

    def blank(slot):
        pool[lay.cot + slot] = jnp.zeros((depth, 8, span), F32)
        coef[slot] = jnp.zeros(coef.shape[1:], F32)

    present = [name for name, arr in zip(("own", "pair", "cross", "far1", "far2"), sent) if arr is not None]
    for missing, slot in (("pair", None), ("cross", None)):
        if missing not in present:
            for piece in range(GROUP):
                base = jnp.where(even, 1 + 2 * GROUP, 1) if missing == "pair" else jnp.where(even, 1, 1 + 2 * GROUP)
                blank(base + piece)
    if "far1" not in present or "far2" not in present:
        if "far1" in present:
            blank(jnp.where(early, 0, 3 * GROUP + 1))
        else:
            blank(0)
            blank(3 * GROUP + 1)
    step = len(present)
    for turn in range(height):
        block = lax.rem(height_pos - turn + height, height)
        for pos, name in enumerate(present):
            msg = msgs[turn * step + pos]
            if name in ("own", "pair", "cross"):
                if name == "own":
                    base = 1 + GROUP
                elif name == "pair":
                    base = jnp.where(even, 1 + 2 * GROUP, 1)
                else:
                    base = jnp.where(even, 1, 1 + 2 * GROUP)
                for piece in range(GROUP):
                    stage(msg, piece, base + jnp.bitwise_xor(member, piece), block)
            else:
                first = early if name == "far1" else jnp.logical_not(early)
                stage(msg, 0, jnp.where(first, 3 * GROUP + 1, 0), block)

    lane = lax.broadcasted_iota(jnp.int32, (8, span), 1)
    sub = lax.broadcasted_iota(jnp.int32, (8, span), 0)
    opens = (lane % 8 == 0) & (lane > 0)
    closes = (lane % 8 == 7) & (lane < span - 1)

    def join_span(values):
        return values + jnp.where(opens, pltpu.roll(values, 1, 2), jnp.where(closes, pltpu.roll(values, span - 1, 2), 0.0))

    def join_depth(values):
        planes = []
        for elem in range(elems):
            first, last = values[elem * 8], values[elem * 8 + 7]
            if elem > 0:
                first = first + values[elem * 8 - 1]
            if elem < elems - 1:
                last = last + values[elem * 8 + 8]
            planes += [first[None], values[elem * 8 + 1 : elem * 8 + 7], last[None]]
        return jnp.concatenate(planes, axis=0)

    def join_width(base, at):
        low = pltpu.roll(pool[base + at - 1], 1, 1)
        high = pltpu.roll(pool[base + at + 1], 7, 1)
        return pool[base + at] + jnp.where(sub == 0, low, jnp.where(sub == 7, high, 0.0))

    def per_elem(slot, kind, count=elems, start=0):
        return jnp.concatenate([jnp.broadcast_to(coef[slot, kind, start + e][None], (8, 8, span)) for e in range(count)], axis=0)

    def omega(count=elems):
        return jnp.concatenate([omega_ref[...]] * count, axis=0)

    def operator(values, slot, start=0):
        count = values.shape[0] // 8
        flat = values.reshape(count * 64, span)
        one = flat.astype(jnp.bfloat16)
        rest = flat - one.astype(F32)
        two = rest.astype(jnp.bfloat16)
        three = (rest - two.astype(F32)).astype(jnp.bfloat16)
        split = (one, two, three)
        both = jnp.dot(jnp.concatenate([one, two], axis=1), row_a_ref[...], preferred_element_type=F32)
        lin = both[:, :span] + both[:, span:] + jnp.dot(jnp.concatenate([one, three], axis=1), row_b_ref[...], preferred_element_type=F32)
        blocks = []
        for e in range(count):
            stack = jnp.concatenate([split[f][e * 64 : e * 64 + 64] for _, f in TERMS], axis=0)
            blocks.append(jnp.dot(face_ref[...], stack, preferred_element_type=F32))
        lin = (lin + jnp.concatenate(blocks, axis=0)).reshape(values.shape)
        return omega(count) * ((INV_STEP * per_elem(slot, 1, count, start)) * values + per_elem(slot, 0, count, start) * lin)

    def loop(start, stop, body):
        lax.fori_loop(start, stop, lambda at, carry: (body(at), carry)[1], 0)

    diag_at, mass_at = lay.basis + wide, lay.second - 1

    def start_slab(at):
        slot = member + at
        heavy = omega() * (INV_STEP * per_elem(slot, 1))
        pool[lay.sums + at] = join_depth(join_span(heavy * pool[lay.cot + slot]))
        quot = jnp.concatenate([quot_ref[...]] * elems, axis=0)
        pool[diag_at + at] = join_depth(join_span(heavy + omega() * per_elem(slot, 0) * quot))

    def mass_slab(at):
        pool[mass_at + at - 1] = join_depth(join_span(omega() * (INV_STEP * per_elem(member + at, 1))))

    def first_slab(at):
        diag = join_width(diag_at, at)
        inverse = jnp.where(diag > 0.0, 1.0 / jnp.where(diag > 0.0, diag, 1.0), 0.0)
        pool[lay.minv + at - 1] = inverse
        pool[lay.basis + at - 1] = inverse * join_width(lay.sums, at)

    def ratio_slab(at):
        pool[lay.ratio + at - 3] = pool[lay.minv + at - 1] * join_width(mass_at - 1, at)

    loop(0, wide + 2, start_slab)
    loop(2, wide, mass_slab)
    loop(1, wide + 1, first_slab)
    loop(3, wide - 1, ratio_slab)

    mid = REACH + 1
    own = pl.ds(height_pos * own_depth, own_depth)
    zpos = lax.broadcasted_iota(jnp.int32, (own_depth, 8, span), 0) + height_pos * own_depth
    xpos = lax.broadcasted_iota(jnp.int32, (own_depth, 8, span), 1) + plane_pos * 8

    def copies(pos, extent):
        return jnp.where(((pos % 8 == 7) & (pos < extent - 1)) | ((pos % 8 == 0) & (pos > 0)), 0.5, 1.0)

    share = copies(zpos, depth) * copies(xpos, plane * 8) * jnp.where(opens | closes, 0.5, 1.0)
    weigh[...] = share / pool[lay.minv + REACH, own]

    for level in range(2):
        def apply(at, level=level):
            pool[lay.sums + at] = join_depth(join_span(operator(pool[lay.basis + level * wide + at - 1], member + at)))

        def advance(at, level=level):
            pool[lay.basis + (level + 1) * wide + at - 1] = (
                pool[lay.minv + at - 1] * join_width(lay.sums, at) - SHIFTS[level] * pool[lay.basis + level * wide + at - 1]
            )

        loop(1 + level, wide + 1 - level, apply)
        loop(2 + level, wide - level, advance)

    def second(vec):
        def begin(at):
            pool[lay.second + at - 3] = pool[lay.ratio + at - 3] * pool[lay.basis + vec * wide + at - 1]

        loop(3, 8, begin)
        for level in range(2):
            here = lay.second + (0, 5, 8)[level] - 3 - level
            after = lay.second + (0, 5, 8)[level + 1] - 4 - level

            def apply(at, here=here):
                pool[lay.sums + at] = join_depth(join_span(operator(pool[here + at], member + at)))

            def advance(at, here=here, after=after, level=level):
                pool[after + at] = pool[lay.minv + at - 1] * join_width(lay.sums, at) - SHIFTS[level] * pool[here + at]

            loop(3 + level, 8 - level, apply)
            loop(4 + level, 7 - level, advance)
        fields_ref[3 + vec] = pool[lay.second + 2, own]
        fields_ref[6 + vec] = pool[lay.second + 6, own]
        fields_ref[9 + vec] = pool[lay.second + 8, own]

    for vec in range(3):
        fields_ref[vec] = pool[lay.basis + vec * wide + REACH, own]
    loop(0, 3, second)

    slot = member + mid
    start = height_pos * own_elems

    def total(values):
        return jnp.sum(values, axis=0)

    def weighted(index):
        return weigh[...] * fields_ref[index]

    parts = []
    left = [weighted(i) for i in range(3)]
    parts += [total(left[i] * fields_ref[j]) for i, j in PAIRS]
    parts.append(total(fields_ref[2] * operator(fields_ref[2], slot, start)))
    for k, l in PAIRS:
        pairs = PAIRS if k == l else [(i, j) for i in range(3) for j in range(3)]
        left = [weighted(3 + 3 * k + i) for i in range(3)]
        parts += [total(left[i] * fields_ref[3 + 3 * l + j]) for i, j in pairs]
    energy = [operator(fields_ref[9 + j], slot, start) for j in range(3)]
    parts += [total(fields_ref[9 + i] * energy[j]) for i, j in PAIRS]
    lines = [jnp.sum(part, axis=0, keepdims=True) for part in parts]
    lines.append(jnp.zeros((span - len(lines), span), F32))
    sums = lax.dot_general(jnp.ones((8, span), F32), jnp.concatenate(lines, axis=0), (((1,), (1,)), ((), ())), precision=HIGHEST, preferred_element_type=F32)

    heavy = omega(own_elems) * (INV_STEP * per_elem(slot, 1, own_elems, start))
    rows = []
    for index in range(12):
        mass = heavy * fields_ref[index]
        for elem in range(own_elems):
            rows.append(jnp.sum(jnp.sum(mass[elem * 8 : elem * 8 + 8], axis=0), axis=0, keepdims=True))
    rows = jnp.concatenate(rows, axis=0)
    cells = span // 8
    per_row = span // cells
    spread = (lax.broadcasted_iota(jnp.int32, (span, span), 0) // 8 == lax.broadcasted_iota(jnp.int32, (span, span), 1) % cells).astype(F32)
    rows = jnp.dot(rows, spread, precision=HIGHEST, preferred_element_type=F32)
    place = lax.broadcasted_iota(jnp.int32, rows.shape, 0) % per_row == lax.broadcasted_iota(jnp.int32, rows.shape, 1) // cells
    rows = jnp.where(place, rows, 0.0).reshape(rows.shape[0] // per_row, per_row, span)
    packed = jnp.sum(rows, axis=1)
    info_ref[...] = jnp.concatenate([packed, sums[:1]], axis=0)


def galerkin(gram, energy):
    n00, n01, n02, n11, n12, n22 = gram
    h00, h01, h02 = n01 + SHIFTS[0] * n00, n11 + SHIFTS[0] * n01, n12 + SHIFTS[0] * n02
    h11, h12 = n12 + SHIFTS[1] * n11, n22 + SHIFTS[1] * n12
    low10, low20 = h01 / h00, h02 / h00
    piv1 = h11 - low10 * h01
    off12 = h12 - low10 * h02
    low21 = off12 / piv1
    piv2 = energy - low20 * h02 - low21 * off12
    y0 = n00
    y1 = n01 - low10 * y0
    y2 = n02 - low20 * y0 - low21 * y1
    c2 = y2 / piv2
    c1 = y1 / piv1 - low21 * c2
    c0 = y0 / h00 - low10 * c1 - low20 * c2
    return c0, c1, c2


def combine_kernel(info_ref, fields_ref, owner_ref, place_ref, second_ref, first_ref, grad_ref):
    devices, lines, span = info_ref.shape
    ones = jnp.ones((devices, span), F32)
    contract = (((0,), (0,)), ((), ()))
    wide = lax.dot_general(info_ref[:, lines - 1, :], ones, contract, precision=HIGHEST, preferred_element_type=F32)
    take = [wide[i : i + 1, :] for i in range(7 + 45 + 6)]
    coef = galerkin(take[:6], take[6])
    at = 7
    double = [(2.0 if i != j else 1.0) * coef[i] * coef[j] for i, j in PAIRS]
    every = [coef[i] * coef[j] for i in range(3) for j in range(3)]
    gram = []
    for k, l in PAIRS:
        factors = double if k == l else every
        gram.append(sum(f * t for f, t in zip(factors, take[at : at + len(factors)])))
        at += len(factors)
    energy = sum(f * t for f, t in zip(double, take[at : at + 6]))
    outer = galerkin(gram, energy)
    factors = list(coef) + [d * c for d in outer for c in coef]

    second_ref[...] = factors[0] * fields_ref[0] + factors[1] * fields_ref[1] + factors[2] * fields_ref[2]
    first = factors[3] * fields_ref[3]
    for i in range(4, 12):
        first = first + factors[i] * fields_ref[i]
    first_ref[...] = first

    per_line = 12 // (lines - 1)
    cells = span // per_line
    row = lax.broadcasted_iota(jnp.int32, (span, span), 0)
    for step in range(2):
        holder = (owner_ref[step : step + 1, :] == lax.broadcasted_iota(jnp.int32, (devices, span), 0)).astype(F32)
        here = place_ref[step : step + 1, :] == row % cells
        result = jnp.zeros((1, span), F32)
        for line in range(lines - 1):
            fields = [f for f in range(line * per_line, (line + 1) * per_line) if (f >= 3) == (step == 0)]
            if not fields:
                continue
            picked = lax.dot_general(info_ref[:, line, :], holder, contract, precision=HIGHEST, preferred_element_type=F32)
            picked = jnp.where(here, picked, 0.0)
            for f in fields:
                lo = (f - line * per_line) * cells
                result = result + factors[f] * jnp.sum(picked[lo : lo + cells], axis=0, keepdims=True)
        grad_ref[step : step + 1, :] = result * (1.0 / (8.0 * INV_STEP))


def per_device(counts, cotangent, conductivity, capacity, sources):
    height, plane = counts
    depth, _, span = cotangent.shape
    elems = depth // 8
    cells = span // 8
    vmem = pl.BlockSpec(memory_space=pltpu.VMEM)

    rows = depth * 8 + -(-(2 * elems) // 8) * 8
    message = pl.pallas_call(
        pack_kernel,
        out_shape=jax.ShapeDtypeStruct((rows, span), F32),
        in_specs=[vmem] * 3,
        out_specs=vmem,
    )(cotangent, conductivity, capacity)

    member = lax.axis_index("plane") % GROUP
    group = lax.axis_index("plane") // GROUP
    groups = plane // GROUP
    gathered = message
    width = 1
    while width < GROUP:
        other = swap(gathered, "plane", [(p, p ^ width) for p in range(plane) if p & width == 0])
        gathered = jnp.concatenate([gathered, other], axis=0)
        width *= 2

    def group_pairs(first, gap):
        return [(g * GROUP + m, (g + gap) * GROUP + m) for g in range(groups - gap) if first(g) for m in range(GROUP)]

    pair = swap(gathered, "plane", group_pairs(lambda g: g % 2 == 0, 1))
    cross = swap(gathered, "plane", group_pairs(lambda g: g % 2 == 1, 1))
    slabs = gathered.reshape(GROUP, rows, span)
    far = []
    for turn in range(2):
        pairs = group_pairs(lambda g, turn=turn: (g // 2) % 2 == turn, 2)
        if pairs:
            ends = jnp.where((group // 2) % 2 == turn, GROUP - 1, 0)
            edge = lax.dynamic_index_in_dim(slabs, jnp.bitwise_xor(member, ends), 0, keepdims=False)
            far.append(swap(edge, "plane", pairs))
        else:
            far.append(None)
    sent = (gathered, pair, cross, *far)
    blocks = [arr for arr in sent if arr is not None]
    operands = list(blocks)
    for turn in range(1, height):
        operands += [lax.ppermute(arr, "height", [(h, (h + turn) % height) for h in range(height)]) for arr in blocks]

    lay = Layout()
    consts = tables(span)
    slots = 3 * GROUP + 2
    fields, info = pl.pallas_call(
        functools.partial(basis_kernel, counts, tuple(None if arr is None else 0 for arr in sent)),
        out_shape=(jax.ShapeDtypeStruct((12, depth, 8, span), F32), jax.ShapeDtypeStruct((12 * elems * cells // span + 1, span), F32)),
        in_specs=[vmem] * (len(operands) + len(consts)),
        out_specs=(vmem, vmem),
        scratch_shapes=[
            pltpu.VMEM((lay.total, depth * height, 8, span), F32),
            pltpu.VMEM((slots, 2, elems * height, 8, span), F32),
            pltpu.VMEM((depth, 8, span), F32),
        ],
        compiler_params=pltpu.CompilerParams(vmem_limit_bytes=56 * 1024 * 1024),
    )(*operands, *[jnp.asarray(c) for c in consts])

    devices = height * plane
    shared = lax.all_to_all(jnp.broadcast_to(info[None], (devices, *info.shape)), ("height", "plane"), 0, 0, tiled=True)

    cell = sources % cells
    column = sources // cells
    wide_elem = column % plane
    deep_elem = column // plane
    owner = (deep_elem // elems) * plane + wide_elem
    place = (deep_elem % elems) * cells + cell
    return pl.pallas_call(
        combine_kernel,
        out_shape=(
            jax.ShapeDtypeStruct(cotangent.shape, F32),
            jax.ShapeDtypeStruct(cotangent.shape, F32),
            jax.ShapeDtypeStruct(sources.shape, F32),
        ),
        in_specs=[vmem] * 4,
        out_specs=(vmem, vmem, vmem),
        compiler_params=pltpu.CompilerParams(vmem_limit_bytes=32 * 1024 * 1024),
    )(shared, fields, owner, place)


def solution(mesh):
    counts = (mesh.shape["height"], mesh.shape["plane"])
    field = P("height", "plane", None)
    return jax.shard_map(
        functools.partial(per_device, counts),
        mesh=mesh,
        in_specs=(field, field, field, P()),
        out_specs=(field, field, P()),
        check_vma=False,
    )
```

profile of v0, /device:TPU:0, one launch (start us, length us, event | category | flops | bytes accessed | tf_op | source)
XLA Modules:
  0.0 69.6 jit_solution(11381572028400759084)
XLA Ops:
  0.6 1.6 %shard_map.112 = f32[136,128]{1,0:T(8,128)} custom-call(f32[16,8,128]{2,1,0:T(8,128)} %cot_ref.1, f32[2,1,16]{2,1,0:T(1,128)} %kap_ref.1, f32[2,1,16]{2,1,0:T(1,128)} %cap_ref.1), custom_call_target="tpu_custom_call" | custom-call | tf_op jit(solution)/shard_map/pallas_call | solution.py:388
  2.2 2.9 %collective-permute-start = (f32[136,128]{1,0:T(8,128)}, f32[136,128]{1,0:T(8,128)S(1)}, u32[]{:S(2)}, u32[]{:S(2)}) collective-permute-start(f32[136,128]{1,0:T(8,128)} %shard_map.112), channel_id=1, source_target_pairs={{0,1},{2,3},{4,5},{6,7},{8,9},{10,11},{12,13},{14,15},{1,0},{3,2},... | collective-permute-start | bytes 208904 | tf_op jit(solution)/shard_map/ppermute | solution.py:63
  5.2 2.6 %collective-permute-done = f32[136,128]{1,0:T(8,128)S(1)} collective-permute-done((f32[136,128]{1,0:T(8,128)}, f32[136,128]{1,0:T(8,128)S(1)}, u32[]{:S(2)}, u32[]{:S(2)}) %collective-permute-start) | collective-permute-done | bytes 69664 | tf_op jit(solution)/shard_map/ppermute | solution.py:63
  7.8 0.9 %pad_maximum_fusion.1 = f32[272,128]{1,0:T(8,128)S(1)} fusion(f32[136,128]{1,0:T(8,128)S(1)} %collective-permute-done, f32[136,128]{1,0:T(8,128)} %shard_map.112), kind=kLoop, calls=%fused_computation.1 | loop fusion | flops 34816 | bytes 278528 | tf_op jit(solution)/shard_map/concatenate | solution.py:402
  8.7 2.0 %collective-permute-start.1 = (f32[272,128]{1,0:T(8,128)S(1)}, f32[272,128]{1,0:T(8,128)S(1)}, u32[]{:S(2)}, u32[]{:S(2)}) collective-permute-start(f32[272,128]{1,0:T(8,128)S(1)} %pad_maximum_fusion.1), channel_id=1, source_target_pairs={{0,2},{1,3},{4,6},{5,7},{8,10},{9,11},{12,14},{13,15},{2,0},{3,1},... | collective-permute-start | bytes 417800 | tf_op jit(solution)/shard_map/ppermute | solution.py:63
  10.7 3.1 %collective-permute-done.1 = f32[272,128]{1,0:T(8,128)S(1)} collective-permute-done((f32[272,128]{1,0:T(8,128)S(1)}, f32[272,128]{1,0:T(8,128)S(1)}, u32[]{:S(2)}, u32[]{:S(2)}) %collective-permute-start.1) | collective-permute-done | bytes 139296 | tf_op jit(solution)/shard_map/ppermute | solution.py:63
  13.8 2.1 %collective-permute-start.2 = (f32[544,128]{1,0:T(8,128)S(1)}, f32[544,128]{1,0:T(8,128)S(1)}, u32[]{:S(2)}, u32[]{:S(2)}) collective-permute-start(f32[544,128]{1,0:T(8,128)S(1)} %pad_maximum_fusion.refs_0_), channel_id=1, source_target_pairs={{0,4},{1,5},{2,6},{3,7},{8,12},{9,13},{10,14},{11,15},{4,0},{5,1},... | collective-permute-start | bytes 835592 | tf_op jit(solution)/shard_map/ppermute | solution.py:63
  15.9 0.7 collective-permute-start.3
  16.7 3.9 %collective-permute-start.4 = (f32[136,128]{1,0:T(8,128)S(1)}, f32[136,128]{1,0:T(8,128)S(1)}, u32[]{:S(2)}, u32[]{:S(2)}) collective-permute-start(f32[136,128]{1,0:T(8,128)S(1)} %dynamic-slice_bitcast_fusion), channel_id=1, source_target_pairs={{0,8},{1,9},{2,10},{3,11},{4,12},{5,13},{6,14},{7,15},{8,0},{9,1},... | collective-permute-start | bytes 208904 | tf_op jit(solution)/shard_map/ppermute | solution.py:63
  20.6 0.1 collective-permute-done.2.refs_1_
  20.7 0.4 collective-permute-start.6
  21.1 0.1 collective-permute-start.7
  21.2 6.2 %collective-permute-done.4.refs_3_ = f32[136,128]{1,0:T(8,128)S(1)} collective-permute-done((f32[136,128]{1,0:T(8,128)S(1)}, f32[136,128]{1,0:T(8,128)S(1)}, u32[]{:S(2)}, u32[]{:S(2)}) %collective-permute-start.4) | collective-permute-done | bytes 69664 | tf_op jit(solution)/shard_map/ppermute | solution.py:63
  27.5 1.2 %collective-permute-done.8.refs_7_ = f32[136,128]{1,0:T(8,128)S(1)} collective-permute-done((f32[136,128]{1,0:T(8,128)S(1)}, f32[136,128]{1,0:T(8,128)S(1)}, u32[]{:S(2)}, u32[]{:S(2)}) %collective-permute-start.8) | collective-permute-done | bytes 69664 | tf_op jit(solution)/shard_map/ppermute | solution.py:424
  28.8 0.5 copy-done.9
  29.3 0.1 copy-done.5
  29.5 0.1 copy-done.6
  29.5 0.7 %copy-done.7 = f32[544,128]{1,0:T(8,128)} copy-done((f32[544,128]{1,0:T(8,128)}, f32[544,128]{1,0:T(8,128)S(1)}, u32[]{:S(2)}) %copy-start.7) | copy-done | bytes 278552
  30.2 23.6 %shard_map.113 = (f32[12,16,8,128]{3,2,1,0:T(8,128)}, f32[4,128]{1,0:T(4,128)}) custom-call(f32[544,128]{1,0:T(8,128)} %copy-done.1, f32[544,128]{1,0:T(8,128)} %copy-done.3, f32[544,128]{1,0:T(8,128)} %copy-done.4, f32[136,128]{1,0:T(8,128)} %copy-done.8, f32[544,128]{1,0:T(8,128)} %copy-done.5, f32[544,128]{1,0:T(8,128)} %copy-done.6, ...), custom_call_target="tpu_custom_call" | custom-call | tf_op jit(solution)/shard_map/pallas_call | solution.py:429
  53.8 1.3 %broadcast_in_dim.2 = f32[32,4,128]{2,1,0:T(4,128)} broadcast(f32[4,128]{1,0:T(4,128)} %get-tuple-element.5), dimensions={1,2} | broadcast | bytes 67584 | tf_op jit(solution)/shard_map/broadcast_in_dim | solution.py:443
  55.2 4.9 %all-to-all-start = ((f32[32,4,128]{2,1,0:T(4,128)}), f32[32,4,128]{2,1,0:T(4,128)S(1)}, u32[]{:S(2)}, u32[]{:S(2)}) async-start(f32[32,4,128]{2,1,0:T(4,128)} %broadcast_in_dim.2), calls=%async_computation | async-start | bytes 131072 | tf_op jit(solution)/shard_map/all_to_all | solution.py:443
  60.1 7.3 %all-to-all-done.info_ref = f32[32,4,128]{2,1,0:T(4,128)S(1)} async-done(((f32[32,4,128]{2,1,0:T(4,128)}), f32[32,4,128]{2,1,0:T(4,128)S(1)}, u32[]{:S(2)}, u32[]{:S(2)}) %all-to-all-start) | async-done | bytes 65568 | tf_op jit(solution)/shard_map/all_to_all | solution.py:443
  67.4 1.1 %copy-done = f32[12,16,8,128]{3,2,1,0:T(8,128)S(1)} copy-done((f32[12,16,8,128]{3,2,1,0:T(8,128)S(1)}, f32[12,16,8,128]{3,2,1,0:T(8,128)}, u32[]{:S(2)}) %copy-start) | copy-done | bytes 786456
  68.5 1.0 %shard_map.114 = (f32[16,8,128]{2,1,0:T(8,128)}, f32[16,8,128]{2,1,0:T(8,128)}, f32[2,128]{1,0:T(2,128)}) custom-call(f32[32,4,128]{2,1,0:T(4,128)S(1)} %all-to-all-done.info_ref, f32[12,16,8,128]{3,2,1,0:T(8,128)S(1)} %copy-done, s32[2,128]{1,0:T(2,128)S(1)} %fusion.owner_ref, s32[2,128]{1,0:T(2,128)S(1)} %get-tuple-element.7.place_ref), custom_call_target="tpu_custom_call" | custom-call | tf_op jit(solution)/shard_map/pallas_call | solution.py:451
  (27 shorter events, 0.1 us)
Async XLA Ops:
  2.2 11.5 %copy-start.2 = (f32[136,128]{1,0:T(8,128)S(1)}, f32[136,128]{1,0:T(8,128)}, u32[]{:S(2)}) copy-start(f32[136,128]{1,0:T(8,128)} %shard_map.112) | copy-start | bytes 208900
  2.2 5.5 %collective-permute-start = (f32[136,128]{1,0:T(8,128)}, f32[136,128]{1,0:T(8,128)S(1)}, u32[]{:S(2)}, u32[]{:S(2)}) collective-permute-start(f32[136,128]{1,0:T(8,128)} %shard_map.112), channel_id=1, source_target_pairs={{0,1},{2,3},{4,5},{6,7},{8,9},{10,11},{12,13},{14,15},{1,0},{3,2},... | collective-permute-start | bytes 208904 | tf_op jit(solution)/shard_map/ppermute | solution.py:63
  8.7 5.1 %collective-permute-start.1 = (f32[272,128]{1,0:T(8,128)S(1)}, f32[272,128]{1,0:T(8,128)S(1)}, u32[]{:S(2)}, u32[]{:S(2)}) collective-permute-start(f32[272,128]{1,0:T(8,128)S(1)} %pad_maximum_fusion.1), channel_id=1, source_target_pairs={{0,2},{1,3},{4,6},{5,7},{8,10},{9,11},{12,14},{13,15},{2,0},{3,1},... | collective-permute-start | bytes 417800 | tf_op jit(solution)/shard_map/ppermute | solution.py:63
  13.8 15.0 %copy-start.1 = (f32[544,128]{1,0:T(8,128)}, f32[544,128]{1,0:T(8,128)S(1)}, u32[]{:S(2)}) copy-start(f32[544,128]{1,0:T(8,128)S(1)} %pad_maximum_fusion.refs_0_) | copy-start | bytes 835588
  13.8 6.9 %collective-permute-start.2 = (f32[544,128]{1,0:T(8,128)S(1)}, f32[544,128]{1,0:T(8,128)S(1)}, u32[]{:S(2)}, u32[]{:S(2)}) collective-permute-start(f32[544,128]{1,0:T(8,128)S(1)} %pad_maximum_fusion.refs_0_), channel_id=1, source_target_pairs={{0,4},{1,5},{2,6},{3,7},{8,12},{9,13},{10,14},{11,15},{4,0},{5,1},... | collective-permute-start | bytes 835592 | tf_op jit(solution)/shard_map/ppermute | solution.py:63
  15.9 5.2 %collective-permute-start.3 = (f32[544,128]{1,0:T(8,128)S(1)}, f32[544,128]{1,0:T(8,128)S(1)}, u32[]{:S(2)}, u32[]{:S(2)}) collective-permute-start(f32[544,128]{1,0:T(8,128)S(1)} %pad_maximum_fusion.refs_0_), channel_id=1, source_target_pairs={{4,8},{5,9},{6,10},{7,11},{8,4},{9,5},{10,6},{11,7},{20,24},{21,25... | collective-permute-start | bytes 835592 | tf_op jit(solution)/shard_map/ppermute | solution.py:63
  16.6 10.8 %copy-start.10 = (s32[2,128]{1,0:T(2,128)S(1)}, s32[2,128]{1,0:T(2,128)}, u32[]{:S(2)}) copy-start(s32[2,128]{1,0:T(2,128)} %param.12) | copy-start | bytes 3076
  16.7 10.8 %collective-permute-start.4 = (f32[136,128]{1,0:T(8,128)S(1)}, f32[136,128]{1,0:T(8,128)S(1)}, u32[]{:S(2)}, u32[]{:S(2)}) collective-permute-start(f32[136,128]{1,0:T(8,128)S(1)} %dynamic-slice_bitcast_fusion), channel_id=1, source_target_pairs={{0,8},{1,9},{2,10},{3,11},{4,12},{5,13},{6,14},{7,15},{8,0},{9,1},... | collective-permute-start | bytes 208904 | tf_op jit(solution)/shard_map/ppermute | solution.py:63
  20.6 8.1 %collective-permute-start.5 = (f32[544,128]{1,0:T(8,128)S(1)}, f32[544,128]{1,0:T(8,128)S(1)}, u32[]{:S(2)}, u32[]{:S(2)}) collective-permute-start(f32[544,128]{1,0:T(8,128)S(1)} %pad_maximum_fusion.refs_0_), channel_id=1, source_target_pairs={{0,16},{16,0},{1,17},{17,1},{2,18},{18,2},{3,19},{19,3},{4,20},{20... | collective-permute-start | bytes 835592 | tf_op jit(solution)/shard_map/ppermute | solution.py:424
  20.7 8.0 %copy-start.3 = (f32[544,128]{1,0:T(8,128)}, f32[544,128]{1,0:T(8,128)S(1)}, u32[]{:S(2)}) copy-start(f32[544,128]{1,0:T(8,128)S(1)} %collective-permute-done.2.refs_1_) | copy-start | bytes 835588
  20.7 8.0 %collective-permute-start.6 = (f32[544,128]{1,0:T(8,128)S(1)}, f32[544,128]{1,0:T(8,128)S(1)}, u32[]{:S(2)}, u32[]{:S(2)}) collective-permute-start(f32[544,128]{1,0:T(8,128)S(1)} %collective-permute-done.2.refs_1_), channel_id=1, source_target_pairs={{0,16},{16,0},{1,17},{17,1},{2,18},{18,2},{3,19},{19,3},{4,20},{20... | collective-permute-start | bytes 835592 | tf_op jit(solution)/shard_map/ppermute | solution.py:424
  21.1 7.7 %copy-start.4 = (f32[544,128]{1,0:T(8,128)}, f32[544,128]{1,0:T(8,128)S(1)}, u32[]{:S(2)}) copy-start(f32[544,128]{1,0:T(8,128)S(1)} %collective-permute-done.3.refs_2_) | copy-start | bytes 835588
  21.1 7.6 %collective-permute-start.7 = (f32[544,128]{1,0:T(8,128)S(1)}, f32[544,128]{1,0:T(8,128)S(1)}, u32[]{:S(2)}, u32[]{:S(2)}) collective-permute-start(f32[544,128]{1,0:T(8,128)S(1)} %collective-permute-done.3.refs_2_), channel_id=1, source_target_pairs={{0,16},{16,0},{1,17},{17,1},{2,18},{18,2},{3,19},{19,3},{4,20},{20... | collective-permute-start | bytes 835592 | tf_op jit(solution)/shard_map/ppermute | solution.py:424
  27.5 1.3 %copy-start.8 = (f32[136,128]{1,0:T(8,128)}, f32[136,128]{1,0:T(8,128)S(1)}, u32[]{:S(2)}) copy-start(f32[136,128]{1,0:T(8,128)S(1)} %collective-permute-done.4.refs_3_) | copy-start | bytes 208900
  27.5 1.3 %collective-permute-start.8 = (f32[136,128]{1,0:T(8,128)S(1)}, f32[136,128]{1,0:T(8,128)S(1)}, u32[]{:S(2)}, u32[]{:S(2)}) collective-permute-start(f32[136,128]{1,0:T(8,128)S(1)} %collective-permute-done.4.refs_3_), channel_id=1, source_target_pairs={{0,16},{16,0},{1,17},{17,1},{2,18},{18,2},{3,19},{19,3},{4,20},{20... | collective-permute-start | bytes 208904 | tf_op jit(solution)/shard_map/ppermute | solution.py:424
  28.7 0.6 copy-start.9
  28.7 0.7 %copy-start.5 = (f32[544,128]{1,0:T(8,128)}, f32[544,128]{1,0:T(8,128)S(1)}, u32[]{:S(2)}) copy-start(f32[544,128]{1,0:T(8,128)S(1)} %collective-permute-done.5.refs_4_) | copy-start | bytes 835588
  28.7 0.8 %copy-start.6 = (f32[544,128]{1,0:T(8,128)}, f32[544,128]{1,0:T(8,128)S(1)}, u32[]{:S(2)}) copy-start(f32[544,128]{1,0:T(8,128)S(1)} %collective-permute-done.6.refs_5_) | copy-start | bytes 835588
  29.5 0.7 %copy-start.7 = (f32[544,128]{1,0:T(8,128)}, f32[544,128]{1,0:T(8,128)S(1)}, u32[]{:S(2)}) copy-start(f32[544,128]{1,0:T(8,128)S(1)} %collective-permute-done.7.refs_6_) | copy-start | bytes 835588
  55.2 12.2 %all-to-all-start = ((f32[32,4,128]{2,1,0:T(4,128)}), f32[32,4,128]{2,1,0:T(4,128)S(1)}, u32[]{:S(2)}, u32[]{:S(2)}) async-start(f32[32,4,128]{2,1,0:T(4,128)} %broadcast_in_dim.2), calls=%async_computation | async-start | bytes 131072 | tf_op jit(solution)/shard_map/all_to_all | solution.py:443
  67.4 1.1 %copy-start = (f32[12,16,8,128]{3,2,1,0:T(8,128)S(1)}, f32[12,16,8,128]{3,2,1,0:T(8,128)}, u32[]{:S(2)}) copy-start(f32[12,16,8,128]{3,2,1,0:T(8,128)} %get-tuple-element.6.fields_ref) | copy-start | bytes 2359300
where the time goes:
time: 69.9 us; the launch traced here: 69.6 us
  Pallas kernels  26.3 us (38%)
  waiting for transfers between devices  20.5 us (29%)
  starting transfers between devices  17 us (24%)
  local copies, waits for them, and re-layouts  3.93 us (6%)
  other arithmetic  0.95 us (1%)
  between operations  0.82 us (1%)
    pallas_call x1, Pallas kernels, per_device(): pl.pallas_call(functools.partial(basis_kernel, counts, tuple((None if arr...  23.6 us
    ppermute x5, waiting for transfers between devices, swap(): return lax.ppermute(value, axis, [*pairs, *((b, a) for a, b in pairs)])  12 us
    ppermute x5, starting transfers between devices, swap(): return lax.ppermute(value, axis, [*pairs, *((b, a) for a, b in pairs)])  11.6 us
    all_to_all x1, waiting for transfers between devices, per_device(): lax.all_to_all(jnp.broadcast_to(info[None], (devices, *info.shape)), ('he...  7.3 us
    all_to_all x1, starting transfers between devices, per_device(): lax.all_to_all(jnp.broadcast_to(info[None], (devices, *info.shape)), ('he...  4.88 us
    unnamed x22, local copies, waits for them, and re-layouts  2.6 us
    pallas_call x1, Pallas kernels, per_device(): pl.pallas_call(pack_kernel, out_shape=jax.ShapeDtypeStruct((rows, span),...  1.62 us
  transfers between devices with their start and end apart: 10, of which 6 were waited for; matrix products, arithmetic and copies ran while one was open for 0% of the time, Pallas kernels for 0%

commit v1 on v0

--- a/solution.py
+++ b/solution.py
@@ -199,7 +199,11 @@
         return omega(count) * ((INV_STEP * per_elem(slot, 1, count, start)) * values + per_elem(slot, 0, count, start) * lin)
 
     def loop(start, stop, body):
-        lax.fori_loop(start, stop, lambda at, carry: (body(at), carry)[1], 0)
+        if elems > 4:
+            lax.fori_loop(start, stop, lambda at, carry: (body(at), carry)[1], 0)
+        else:
+            for at in range(start, stop):
+                body(at)
 
     diag_at, mass_at = lay.basis + wide, lay.second - 1
 

time: 69.9 us -> 57.3 us (0.82)
  Pallas kernels: 26.3 us -> 13.7 us
    pallas_call x1, Pallas kernels: 23.6 us -> 11 us  [per_device(): pl.pallas_call(functools.partial(basis_kernel, counts, tuple((None if arr...]
where the time goes in v1:
time: 57.3 us; the launch traced here: 57 us
  waiting for transfers between devices  20.5 us (36%)
  starting transfers between devices  17 us (30%)
  Pallas kernels  13.7 us (24%)
  local copies, waits for them, and re-layouts  3.93 us (7%)
  other arithmetic  0.95 us (2%)
  between operations  0.82 us (1%)
    ppermute x5, waiting for transfers between devices, swap(): return lax.ppermute(value, axis, [*pairs, *((b, a) for a, b in pairs)])  12 us
    ppermute x5, starting transfers between devices, swap(): return lax.ppermute(value, axis, [*pairs, *((b, a) for a, b in pairs)])  11.6 us
    pallas_call x1, Pallas kernels, per_device(): pl.pallas_call(functools.partial(basis_kernel, counts, tuple((None if arr...  11 us
    all_to_all x1, waiting for transfers between devices, per_device(): lax.all_to_all(jnp.broadcast_to(info[None], (devices, *info.shape)), ('he...  7.3 us
    all_to_all x1, starting transfers between devices, per_device(): lax.all_to_all(jnp.broadcast_to(info[None], (devices, *info.shape)), ('he...  4.88 us
    unnamed x22, local copies, waits for them, and re-layouts  2.6 us
    pallas_call x1, Pallas kernels, per_device(): pl.pallas_call(pack_kernel, out_shape=jax.ShapeDtypeStruct((rows, span),...  1.62 us
    broadcast_in_dim x1, local copies, waits for them, and re-layouts, per_device(): jnp.broadcast_to(info[None], (devices, *info.shape))  1.32 us
  transfers between devices with their start and end apart: 10, of which 6 were waited for; matrix products, arithmetic and copies ran while one was open for 0% of the time, Pallas kernels for 0%

profile of v1, /device:TPU:0, one launch (start us, length us, event | category | flops | bytes accessed | tf_op | source)
XLA Modules:
  0.0 57.0 jit_solution(13596474042889491924)
XLA Ops:
  0.6 1.6 %shard_map.112 = f32[136,128]{1,0:T(8,128)} custom-call(f32[16,8,128]{2,1,0:T(8,128)} %cot_ref.1, f32[2,1,16]{2,1,0:T(1,128)} %kap_ref.1, f32[2,1,16]{2,1,0:T(1,128)} %cap_ref.1), custom_call_target="tpu_custom_call" | custom-call | tf_op jit(solution)/shard_map/pallas_call | solution.py:392
  2.2 2.9 %collective-permute-start = (f32[136,128]{1,0:T(8,128)}, f32[136,128]{1,0:T(8,128)S(1)}, u32[]{:S(2)}, u32[]{:S(2)}) collective-permute-start(f32[136,128]{1,0:T(8,128)} %shard_map.112), channel_id=1, source_target_pairs={{0,1},{2,3},{4,5},{6,7},{8,9},{10,11},{12,13},{14,15},{1,0},{3,2},... | collective-permute-start | bytes 208904 | tf_op jit(solution)/shard_map/ppermute | solution.py:63
  5.2 2.6 %collective-permute-done = f32[136,128]{1,0:T(8,128)S(1)} collective-permute-done((f32[136,128]{1,0:T(8,128)}, f32[136,128]{1,0:T(8,128)S(1)}, u32[]{:S(2)}, u32[]{:S(2)}) %collective-permute-start) | collective-permute-done | bytes 69664 | tf_op jit(solution)/shard_map/ppermute | solution.py:63
  7.8 0.9 %pad_maximum_fusion.1 = f32[272,128]{1,0:T(8,128)S(1)} fusion(f32[136,128]{1,0:T(8,128)S(1)} %collective-permute-done, f32[136,128]{1,0:T(8,128)} %shard_map.112), kind=kLoop, calls=%fused_computation.1 | loop fusion | flops 34816 | bytes 278528 | tf_op jit(solution)/shard_map/concatenate | solution.py:406
  8.7 2.0 %collective-permute-start.1 = (f32[272,128]{1,0:T(8,128)S(1)}, f32[272,128]{1,0:T(8,128)S(1)}, u32[]{:S(2)}, u32[]{:S(2)}) collective-permute-start(f32[272,128]{1,0:T(8,128)S(1)} %pad_maximum_fusion.1), channel_id=1, source_target_pairs={{0,2},{1,3},{4,6},{5,7},{8,10},{9,11},{12,14},{13,15},{2,0},{3,1},... | collective-permute-start | bytes 417800 | tf_op jit(solution)/shard_map/ppermute | solution.py:63
  10.7 3.1 %collective-permute-done.1 = f32[272,128]{1,0:T(8,128)S(1)} collective-permute-done((f32[272,128]{1,0:T(8,128)S(1)}, f32[272,128]{1,0:T(8,128)S(1)}, u32[]{:S(2)}, u32[]{:S(2)}) %collective-permute-start.1) | collective-permute-done | bytes 139296 | tf_op jit(solution)/shard_map/ppermute | solution.py:63
  13.8 2.1 %collective-permute-start.2 = (f32[544,128]{1,0:T(8,128)S(1)}, f32[544,128]{1,0:T(8,128)S(1)}, u32[]{:S(2)}, u32[]{:S(2)}) collective-permute-start(f32[544,128]{1,0:T(8,128)S(1)} %pad_maximum_fusion.refs_0_), channel_id=1, source_target_pairs={{0,4},{1,5},{2,6},{3,7},{8,12},{9,13},{10,14},{11,15},{4,0},{5,1},... | collective-permute-start | bytes 835592 | tf_op jit(solution)/shard_map/ppermute | solution.py:63
  15.9 0.7 %collective-permute-start.3 = (f32[544,128]{1,0:T(8,128)S(1)}, f32[544,128]{1,0:T(8,128)S(1)}, u32[]{:S(2)}, u32[]{:S(2)}) collective-permute-start(f32[544,128]{1,0:T(8,128)S(1)} %pad_maximum_fusion.refs_0_), channel_id=1, source_target_pairs={{4,8},{5,9},{6,10},{7,11},{8,4},{9,5},{10,6},{11,7},{20,24},{21,25... | collective-permute-start | bytes 835592 | tf_op jit(solution)/shard_map/ppermute | solution.py:63
  16.7 3.9 %collective-permute-start.4 = (f32[136,128]{1,0:T(8,128)S(1)}, f32[136,128]{1,0:T(8,128)S(1)}, u32[]{:S(2)}, u32[]{:S(2)}) collective-permute-start(f32[136,128]{1,0:T(8,128)S(1)} %dynamic-slice_bitcast_fusion), channel_id=1, source_target_pairs={{0,8},{1,9},{2,10},{3,11},{4,12},{5,13},{6,14},{7,15},{8,0},{9,1},... | collective-permute-start | bytes 208904 | tf_op jit(solution)/shard_map/ppermute | solution.py:63
  20.6 0.1 collective-permute-done.2.refs_1_
  20.7 0.4 collective-permute-start.6
  21.1 0.1 collective-permute-start.7
  21.2 6.2 %collective-permute-done.4.refs_3_ = f32[136,128]{1,0:T(8,128)S(1)} collective-permute-done((f32[136,128]{1,0:T(8,128)S(1)}, f32[136,128]{1,0:T(8,128)S(1)}, u32[]{:S(2)}, u32[]{:S(2)}) %collective-permute-start.4) | collective-permute-done | bytes 69664 | tf_op jit(solution)/shard_map/ppermute | solution.py:63
  27.5 1.2 %collective-permute-done.8.refs_7_ = f32[136,128]{1,0:T(8,128)S(1)} collective-permute-done((f32[136,128]{1,0:T(8,128)S(1)}, f32[136,128]{1,0:T(8,128)S(1)}, u32[]{:S(2)}, u32[]{:S(2)}) %collective-permute-start.8) | collective-permute-done | bytes 69664 | tf_op jit(solution)/shard_map/ppermute | solution.py:428
  28.8 0.5 copy-done.9
  29.3 0.1 copy-done.5
  29.5 0.1 copy-done.6
  29.5 0.7 %copy-done.7 = f32[544,128]{1,0:T(8,128)} copy-done((f32[544,128]{1,0:T(8,128)}, f32[544,128]{1,0:T(8,128)S(1)}, u32[]{:S(2)}) %copy-start.7) | copy-done | bytes 278552
  30.2 11.0 %shard_map.113 = (f32[12,16,8,128]{3,2,1,0:T(8,128)}, f32[4,128]{1,0:T(4,128)}) custom-call(f32[544,128]{1,0:T(8,128)} %copy-done.1, f32[544,128]{1,0:T(8,128)} %copy-done.3, f32[544,128]{1,0:T(8,128)} %copy-done.4, f32[136,128]{1,0:T(8,128)} %copy-done.8, f32[544,128]{1,0:T(8,128)} %copy-done.5, f32[544,128]{1,0:T(8,128)} %copy-done.6, ...), custom_call_target="tpu_custom_call" | custom-call | tf_op jit(solution)/shard_map/pallas_call | solution.py:433
  41.3 1.3 %broadcast_in_dim.2 = f32[32,4,128]{2,1,0:T(4,128)} broadcast(f32[4,128]{1,0:T(4,128)} %get-tuple-element.5), dimensions={1,2} | broadcast | bytes 67584 | tf_op jit(solution)/shard_map/broadcast_in_dim | solution.py:447
  42.6 4.9 %all-to-all-start = ((f32[32,4,128]{2,1,0:T(4,128)}), f32[32,4,128]{2,1,0:T(4,128)S(1)}, u32[]{:S(2)}, u32[]{:S(2)}) async-start(f32[32,4,128]{2,1,0:T(4,128)} %broadcast_in_dim.2), calls=%async_computation | async-start | bytes 131072 | tf_op jit(solution)/shard_map/all_to_all | solution.py:447
  47.5 7.3 %all-to-all-done.info_ref = f32[32,4,128]{2,1,0:T(4,128)S(1)} async-done(((f32[32,4,128]{2,1,0:T(4,128)}), f32[32,4,128]{2,1,0:T(4,128)S(1)}, u32[]{:S(2)}, u32[]{:S(2)}) %all-to-all-start) | async-done | bytes 65568 | tf_op jit(solution)/shard_map/all_to_all | solution.py:447
  54.8 1.1 %copy-done = f32[12,16,8,128]{3,2,1,0:T(8,128)S(1)} copy-done((f32[12,16,8,128]{3,2,1,0:T(8,128)S(1)}, f32[12,16,8,128]{3,2,1,0:T(8,128)}, u32[]{:S(2)}) %copy-start) | copy-done | bytes 786456
  55.9 1.0 %shard_map.114 = (f32[16,8,128]{2,1,0:T(8,128)}, f32[16,8,128]{2,1,0:T(8,128)}, f32[2,128]{1,0:T(2,128)}) custom-call(f32[32,4,128]{2,1,0:T(4,128)S(1)} %all-to-all-done.info_ref, f32[12,16,8,128]{3,2,1,0:T(8,128)S(1)} %copy-done, s32[2,128]{1,0:T(2,128)S(1)} %fusion.owner_ref, s32[2,128]{1,0:T(2,128)S(1)} %get-tuple-element.7.place_ref), custom_call_target="tpu_custom_call" | custom-call | tf_op jit(solution)/shard_map/pallas_call | solution.py:455
  (27 shorter events, 0.1 us)
Async XLA Ops:
  2.2 11.5 %copy-start.2 = (f32[136,128]{1,0:T(8,128)S(1)}, f32[136,128]{1,0:T(8,128)}, u32[]{:S(2)}) copy-start(f32[136,128]{1,0:T(8,128)} %shard_map.112) | copy-start | bytes 208900
  2.2 5.5 %collective-permute-start = (f32[136,128]{1,0:T(8,128)}, f32[136,128]{1,0:T(8,128)S(1)}, u32[]{:S(2)}, u32[]{:S(2)}) collective-permute-start(f32[136,128]{1,0:T(8,128)} %shard_map.112), channel_id=1, source_target_pairs={{0,1},{2,3},{4,5},{6,7},{8,9},{10,11},{12,13},{14,15},{1,0},{3,2},... | collective-permute-start | bytes 208904 | tf_op jit(solution)/shard_map/ppermute | solution.py:63
  8.7 5.1 %collective-permute-start.1 = (f32[272,128]{1,0:T(8,128)S(1)}, f32[272,128]{1,0:T(8,128)S(1)}, u32[]{:S(2)}, u32[]{:S(2)}) collective-permute-start(f32[272,128]{1,0:T(8,128)S(1)} %pad_maximum_fusion.1), channel_id=1, source_target_pairs={{0,2},{1,3},{4,6},{5,7},{8,10},{9,11},{12,14},{13,15},{2,0},{3,1},... | collective-permute-start | bytes 417800 | tf_op jit(solution)/shard_map/ppermute | solution.py:63
  13.8 15.0 %copy-start.1 = (f32[544,128]{1,0:T(8,128)}, f32[544,128]{1,0:T(8,128)S(1)}, u32[]{:S(2)}) copy-start(f32[544,128]{1,0:T(8,128)S(1)} %pad_maximum_fusion.refs_0_) | copy-start | bytes 835588
  13.8 6.9 %collective-permute-start.2 = (f32[544,128]{1,0:T(8,128)S(1)}, f32[544,128]{1,0:T(8,128)S(1)}, u32[]{:S(2)}, u32[]{:S(2)}) collective-permute-start(f32[544,128]{1,0:T(8,128)S(1)} %pad_maximum_fusion.refs_0_), channel_id=1, source_target_pairs={{0,4},{1,5},{2,6},{3,7},{8,12},{9,13},{10,14},{11,15},{4,0},{5,1},... | collective-permute-start | bytes 835592 | tf_op jit(solution)/shard_map/ppermute | solution.py:63
  15.9 5.2 %collective-permute-start.3 = (f32[544,128]{1,0:T(8,128)S(1)}, f32[544,128]{1,0:T(8,128)S(1)}, u32[]{:S(2)}, u32[]{:S(2)}) collective-permute-start(f32[544,128]{1,0:T(8,128)S(1)} %pad_maximum_fusion.refs_0_), channel_id=1, source_target_pairs={{4,8},{5,9},{6,10},{7,11},{8,4},{9,5},{10,6},{11,7},{20,24},{21,25... | collective-permute-start | bytes 835592 | tf_op jit(solution)/shard_map/ppermute | solution.py:63
  16.6 10.8 %copy-start.10 = (s32[2,128]{1,0:T(2,128)S(1)}, s32[2,128]{1,0:T(2,128)}, u32[]{:S(2)}) copy-start(s32[2,128]{1,0:T(2,128)} %param.12) | copy-start | bytes 3076
  16.7 10.8 %collective-permute-start.4 = (f32[136,128]{1,0:T(8,128)S(1)}, f32[136,128]{1,0:T(8,128)S(1)}, u32[]{:S(2)}, u32[]{:S(2)}) collective-permute-start(f32[136,128]{1,0:T(8,128)S(1)} %dynamic-slice_bitcast_fusion), channel_id=1, source_target_pairs={{0,8},{1,9},{2,10},{3,11},{4,12},{5,13},{6,14},{7,15},{8,0},{9,1},... | collective-permute-start | bytes 208904 | tf_op jit(solution)/shard_map/ppermute | solution.py:63
  20.6 8.1 %collective-permute-start.5 = (f32[544,128]{1,0:T(8,128)S(1)}, f32[544,128]{1,0:T(8,128)S(1)}, u32[]{:S(2)}, u32[]{:S(2)}) collective-permute-start(f32[544,128]{1,0:T(8,128)S(1)} %pad_maximum_fusion.refs_0_), channel_id=1, source_target_pairs={{0,16},{16,0},{1,17},{17,1},{2,18},{18,2},{3,19},{19,3},{4,20},{20... | collective-permute-start | bytes 835592 | tf_op jit(solution)/shard_map/ppermute | solution.py:428
  20.7 8.0 %copy-start.3 = (f32[544,128]{1,0:T(8,128)}, f32[544,128]{1,0:T(8,128)S(1)}, u32[]{:S(2)}) copy-start(f32[544,128]{1,0:T(8,128)S(1)} %collective-permute-done.2.refs_1_) | copy-start | bytes 835588
  20.7 8.0 %collective-permute-start.6 = (f32[544,128]{1,0:T(8,128)S(1)}, f32[544,128]{1,0:T(8,128)S(1)}, u32[]{:S(2)}, u32[]{:S(2)}) collective-permute-start(f32[544,128]{1,0:T(8,128)S(1)} %collective-permute-done.2.refs_1_), channel_id=1, source_target_pairs={{0,16},{16,0},{1,17},{17,1},{2,18},{18,2},{3,19},{19,3},{4,20},{20... | collective-permute-start | bytes 835592 | tf_op jit(solution)/shard_map/ppermute | solution.py:428
  21.1 7.7 %copy-start.4 = (f32[544,128]{1,0:T(8,128)}, f32[544,128]{1,0:T(8,128)S(1)}, u32[]{:S(2)}) copy-start(f32[544,128]{1,0:T(8,128)S(1)} %collective-permute-done.3.refs_2_) | copy-start | bytes 835588
  21.1 7.6 %collective-permute-start.7 = (f32[544,128]{1,0:T(8,128)S(1)}, f32[544,128]{1,0:T(8,128)S(1)}, u32[]{:S(2)}, u32[]{:S(2)}) collective-permute-start(f32[544,128]{1,0:T(8,128)S(1)} %collective-permute-done.3.refs_2_), channel_id=1, source_target_pairs={{0,16},{16,0},{1,17},{17,1},{2,18},{18,2},{3,19},{19,3},{4,20},{20... | collective-permute-start | bytes 835592 | tf_op jit(solution)/shard_map/ppermute | solution.py:428
  27.5 1.3 %copy-start.8 = (f32[136,128]{1,0:T(8,128)}, f32[136,128]{1,0:T(8,128)S(1)}, u32[]{:S(2)}) copy-start(f32[136,128]{1,0:T(8,128)S(1)} %collective-permute-done.4.refs_3_) | copy-start | bytes 208900
  27.5 1.3 %collective-permute-start.8 = (f32[136,128]{1,0:T(8,128)S(1)}, f32[136,128]{1,0:T(8,128)S(1)}, u32[]{:S(2)}, u32[]{:S(2)}) collective-permute-start(f32[136,128]{1,0:T(8,128)S(1)} %collective-permute-done.4.refs_3_), channel_id=1, source_target_pairs={{0,16},{16,0},{1,17},{17,1},{2,18},{18,2},{3,19},{19,3},{4,20},{20... | collective-permute-start | bytes 208904 | tf_op jit(solution)/shard_map/ppermute | solution.py:428
  28.7 0.6 %copy-start.9 = (f32[136,128]{1,0:T(8,128)}, f32[136,128]{1,0:T(8,128)S(1)}, u32[]{:S(2)}) copy-start(f32[136,128]{1,0:T(8,128)S(1)} %collective-permute-done.8.refs_7_) | copy-start | bytes 208900
  28.7 0.7 %copy-start.5 = (f32[544,128]{1,0:T(8,128)}, f32[544,128]{1,0:T(8,128)S(1)}, u32[]{:S(2)}) copy-start(f32[544,128]{1,0:T(8,128)S(1)} %collective-permute-done.5.refs_4_) | copy-start | bytes 835588
  28.7 0.8 %copy-start.6 = (f32[544,128]{1,0:T(8,128)}, f32[544,128]{1,0:T(8,128)S(1)}, u32[]{:S(2)}) copy-start(f32[544,128]{1,0:T(8,128)S(1)} %collective-permute-done.6.refs_5_) | copy-start | bytes 835588
  29.5 0.7 %copy-start.7 = (f32[544,128]{1,0:T(8,128)}, f32[544,128]{1,0:T(8,128)S(1)}, u32[]{:S(2)}) copy-start(f32[544,128]{1,0:T(8,128)S(1)} %collective-permute-done.7.refs_6_) | copy-start | bytes 835588
  42.6 12.2 %all-to-all-start = ((f32[32,4,128]{2,1,0:T(4,128)}), f32[32,4,128]{2,1,0:T(4,128)S(1)}, u32[]{:S(2)}, u32[]{:S(2)}) async-start(f32[32,4,128]{2,1,0:T(4,128)} %broadcast_in_dim.2), calls=%async_computation | async-start | bytes 131072 | tf_op jit(solution)/shard_map/all_to_all | solution.py:447
  54.8 1.1 %copy-start = (f32[12,16,8,128]{3,2,1,0:T(8,128)S(1)}, f32[12,16,8,128]{3,2,1,0:T(8,128)}, u32[]{:S(2)}) copy-start(f32[12,16,8,128]{3,2,1,0:T(8,128)} %get-tuple-element.6.fields_ref) | copy-start | bytes 2359300

commit v2 on v0

v2 whole, which is shorter than its diff:
```python
import functools

import jax
import jax.numpy as jnp
import ml_dtypes
import numpy as np
from jax import lax
from jax.experimental import pallas as pl
from jax.experimental.pallas import tpu as pltpu
from jax.sharding import PartitionSpec as P

INV_STEP = 20.0
SHIFTS = (0.5, 1.5)
GROUP = 4
REACH = 4
TERMS = ((0, 0), (0, 1), (1, 0), (1, 1), (2, 0))
PAIRS = ((0, 0), (0, 1), (0, 2), (1, 1), (1, 2), (2, 2))
TINY = 1e-30
HIGHEST = lax.Precision.HIGHEST
F32 = jnp.float32
BF16 = jnp.bfloat16


def gll_tables():
    points = np.array([-1.0, -0.8717401485096066, -0.5917001814331423, -0.2092992179024789, 0.2092992179024789, 0.5917001814331423, 0.8717401485096066, 1.0])
    weights = np.array([1.0 / 28.0, 0.2107042271435061, 0.3411226924835044, 0.4124587946587038, 0.4124587946587038, 0.3411226924835044, 0.2107042271435061, 1.0 / 28.0])
    product = np.array([np.prod([points[col] - points[others] for others in range(8) if others != col]) for col in range(8)])
    derivative = np.zeros((8, 8))
    for row in range(8):
        for col in range(8):
            if row != col:
                derivative[row, col] = product[row] / (product[col] * (points[row] - points[col]))
        derivative[row, row] = -np.sum(derivative[row])
    return derivative, weights, np.sum(derivative**2 * weights[:, None], axis=0)


def pieces(matrix):
    out, rest = [], matrix
    for _ in range(3):
        piece = rest.astype(ml_dtypes.bfloat16)
        out.append(piece)
        rest = rest - piece.astype(np.float64)
    return out


def tables(span):
    derivative, weights, stiff = gll_tables()
    line = (derivative.T * weights) @ derivative / weights[:, None]
    eye = np.eye(8)
    face = pieces(np.kron(line, eye) + np.kron(eye, line))
    face_mat = np.concatenate([face[m] for m, _ in TERMS], axis=1)
    ends_mat = np.concatenate([face_mat[0::8], face_mat[7::8]], axis=0)
    row = pieces(np.kron(np.eye(span // 8), line.T))
    row_a = np.concatenate([np.concatenate([row[0], row[1]], 1)] * 2, axis=0)
    none = np.zeros_like(row[2])
    row_b = np.concatenate([np.concatenate([row[2], none], 1), np.concatenate([none, row[2]], 1)], axis=0)
    tile = np.tile(weights, span // 8)
    ratio = stiff / weights
    omega = weights[:, None, None] * weights[None, :, None] * tile[None, None, :]
    quot = ratio[:, None, None] + ratio[None, :, None] + np.tile(ratio, span // 8)[None, None, :]
    return face_mat, ends_mat, row_a, row_b, omega.astype(np.float32), quot.astype(np.float32)


def swap(value, axis, pairs):
    if not pairs:
        return None
    return lax.ppermute(value, axis, [*pairs, *((b, a) for a, b in pairs)])


def coef_rows(elems):
    return -(-(2 * elems) // 8) * 8


def pack_kernel(cot_ref, kap_ref, cap_ref, out_ref, edge_ref):
    depth, _, span = cot_ref.shape
    elems, _, parts = kap_ref.shape
    out_ref[: depth * 8, :] = cot_ref[...].reshape(depth * 8, span)
    spread = (lax.broadcasted_iota(jnp.int32, (parts, span), 1) // 8 == lax.broadcasted_iota(jnp.int32, (parts, span), 0)).astype(F32)
    coef = jnp.concatenate([kap_ref[...].reshape(elems, parts) * (1.0 / INV_STEP), cap_ref[...].reshape(elems, parts)], axis=0)
    rows = coef_rows(elems)
    if rows > 2 * elems:
        coef = jnp.concatenate([coef, jnp.zeros((rows - 2 * elems, parts), F32)], axis=0)
    coef = jnp.dot(coef, spread, precision=HIGHEST, preferred_element_type=F32)
    out_ref[depth * 8 :, :] = coef
    last = lax.rem(lax.axis_index("plane"), GROUP) == GROUP - 1
    edge_ref[:depth, :] = jnp.where(last, cot_ref[:, 7, :], cot_ref[:, 0, :])
    edge_ref[depth:, :] = coef


class Layout:
    def __init__(self):
        wide = 2 * REACH + 1
        self.wide = wide
        self.cot = 0
        self.sums = self.cot + 3 * GROUP + 2
        self.minv = self.sums + wide + 2
        self.ratio = self.minv + wide
        self.basis = self.ratio + 5
        self.second = self.basis + 3 * wide
        self.total = self.second + wide


def basis_kernel(counts, present, *refs):
    height, plane = counts
    lay = Layout()
    wide = lay.wide
    n_in = len(present) * height
    msgs = refs[:n_in]
    face_ref, ends_ref, row_a_ref, row_b_ref, omega_ref, quot_ref = refs[n_in : n_in + 6]
    fields_ref, info_ref = refs[n_in + 6 : n_in + 8]
    pool, coef, weigh = refs[n_in + 8 :]
    rows, span = pool.shape[1:]
    depth = rows // 8
    own_depth = depth // height
    own_rows = own_depth * 8
    elems = depth // 8
    own_elems = elems // height
    height_pos = lax.axis_index("height")
    plane_pos = lax.axis_index("plane")
    member = lax.rem(plane_pos, GROUP)
    even = lax.rem(plane_pos // GROUP, 2) == 0
    slab_rows = own_rows + coef_rows(own_elems)
    whole = elems > 4

    def stage_coef(msg, top, slot, block):
        for kind in range(2):
            for elem in range(own_elems):
                at = top + kind * own_elems + elem
                coef[slot, kind, block * own_elems + elem] = jnp.broadcast_to(msg[at : at + 1, :], (8, span))

    def stage(msg, piece, slot, block):
        top = piece * slab_rows
        pool[lay.cot + slot, pl.ds(pl.multiple_of(block * own_rows, own_rows), own_rows)] = msg[top : top + own_rows, :]
        stage_coef(msg, top + own_rows, slot, block)

    def stage_face(msg, slot, block):
        top = GROUP * slab_rows
        face = msg[top : top + own_depth, :]
        spread = jnp.concatenate([jnp.broadcast_to(face[z : z + 1], (8, span)) for z in range(own_depth)], axis=0)
        pool[lay.cot + slot, pl.ds(pl.multiple_of(block * own_rows, own_rows), own_rows)] = spread
        stage_coef(msg, top + own_depth, slot, block)

    def sides(name):
        after = even if name == "pair" else jnp.logical_not(even)
        return jnp.where(after, 1 + 2 * GROUP, 1), jnp.where(after, 3 * GROUP + 1, 0)

    for name in ("pair", "cross"):
        if name not in present:
            base, beyond = sides(name)
            for slot in [base + piece for piece in range(GROUP)] + [beyond]:
                pool[lay.cot + slot] = jnp.zeros((rows, span), F32)
                coef[slot] = jnp.zeros(coef.shape[1:], F32)
    for turn in range(height):
        block = lax.rem(height_pos - turn + height, height)
        for pos, name in enumerate(present):
            msg = msgs[turn * len(present) + pos]
            if name == "own":
                base = 1 + GROUP
            else:
                base, beyond = sides(name)
                stage_face(msg, beyond, block)
            for piece in range(GROUP):
                stage(msg, piece, base + jnp.bitwise_xor(member, piece), block)

    lane = lax.broadcasted_iota(jnp.int32, (8, span), 1)
    sub = lax.broadcasted_iota(jnp.int32, (8, span), 0)
    opens = (lane % 8 == 0) & (lane > 0)
    closes = (lane % 8 == 7) & (lane < span - 1)

    def tall(mask, like):
        return jnp.concatenate([mask] * (like.shape[0] // 8), axis=0) if like.shape[0] > 8 else mask

    def join_span(values):
        up, down = pltpu.roll(values, 1, 1), pltpu.roll(values, span - 1, 1)
        return values + jnp.where(tall(opens, values), up, jnp.where(tall(closes, values), down, 0.0))

    def join_depth(values):
        planes = []
        for elem in range(elems):
            top = elem * 64
            first, last = values[top : top + 8], values[top + 56 : top + 64]
            if elem > 0:
                first = first + values[top - 8 : top]
            if elem < elems - 1:
                last = last + values[top + 64 : top + 72]
            planes += [first, values[top + 8 : top + 56], last]
        return jnp.concatenate(planes, axis=0)

    def face_at(at, width_node):
        return lay.sums + at, pl.ds(width_node, depth, stride=8)

    def join_width(at):
        low, high = face_at(at, 7), face_at(at + 1, 0)
        both = pool[low] + pool[high]
        pool[low] = both
        pool[high] = both

    def loop(start, stop, body, step=1):
        if whole:
            lax.fori_loop(start, stop, lambda at, carry: (body([at]), carry)[1], 0)
        else:
            for at in range(start, stop, step):
                body(list(range(at, min(at + step, stop))))

    def each(body):
        return lambda slabs: [body(at) for at in slabs]

    def split(values):
        one = values.astype(BF16)
        return one, (values - one.astype(F32)).astype(BF16)

    def along_span(halves):
        wides = [jnp.dot(jnp.concatenate(h, axis=1), row_a_ref[...], preferred_element_type=F32) for h in halves]
        if len(halves) == 2:
            extra = jnp.dot(jnp.concatenate([halves[0][0], halves[1][0]], axis=1), row_b_ref[...], preferred_element_type=F32)
            extras = [extra[:, :span], extra[:, span:]]
        else:
            extras = [jnp.dot(halves[0][0], row_b_ref[:span, :span], preferred_element_type=F32)]
        return [(w[:, :span] + w[:, span:]) + x for w, x in zip(wides, extras)]

    def along_face(matrix, halves, elem):
        top = elem * 64
        stacks = [jnp.concatenate([h[f][top : top + 64] for _, f in TERMS], axis=0) for h in halves]
        return jnp.dot(matrix, stacks[0] if len(stacks) == 1 else jnp.concatenate(stacks, axis=1), preferred_element_type=F32)

    def scaled(slot, kind, elem, scale):
        value = coef[slot, kind, elem]
        return value if scale == 1.0 else value * scale

    def operator(fields, slots, scale=1.0, start=0):
        halves = [split(v) for v in fields]
        lines = along_span(halves)
        out = [[] for _ in fields]
        for elem in range(fields[0].shape[0] // 64):
            top = elem * 64
            face = along_face(face_ref[...], halves, elem)
            for i, v in enumerate(fields):
                cap = tall(scaled(slots[i], 1, start + elem, scale), face)
                kap = tall(scaled(slots[i], 0, start + elem, scale), face)
                lin = lines[i][top : top + 64] + face[:, i * span : (i + 1) * span]
                out[i].append(cap * v[top : top + 64] + kap * lin)
        return [jnp.concatenate(o, axis=0) for o in out]

    def ends(sources, at, scale):
        halves = [split(pool[s]) for s in sources]
        edges = [pool[s, pl.ds(node, depth, stride=8)] for s, node in zip(sources, (7, 0))]
        lines = along_span([split(jnp.concatenate(edges, axis=0))])[0]
        both = [along_face(ends_ref[...], halves, elem) for elem in range(elems)]
        for i in range(2):
            joined = []
            for elem in range(elems):
                lin = lines[i * depth + elem * 8 : i * depth + elem * 8 + 8] + both[elem][8 * (1 - i) : 8 * (2 - i), i * span : (i + 1) * span]
                slot = member + at[i]
                joined.append(join_span(scaled(slot, 1, elem, scale) * edges[i][elem * 8 : elem * 8 + 8] + scaled(slot, 0, elem, scale) * lin))
            final = []
            for elem in range(elems):
                value = joined[elem]
                if elem > 0:
                    value = value + jnp.where(sub == 0, pltpu.roll(joined[elem - 1], 1, 0), 0.0)
                if elem < elems - 1:
                    value = value + jnp.where(sub == 7, pltpu.roll(joined[elem + 1], 7, 0), 0.0)
                final.append(value)
            pool[face_at(at[i], (7, 0)[i])] = jnp.concatenate(final, axis=0)

    def step(here, after, low, high, shift):
        def apply(slabs):
            made = operator([pool[here + at] for at in slabs], [member + at for at in slabs], 1.0 / shift)
            for at, value in zip(slabs, made):
                pool[lay.sums + at] = join_depth(join_span(value))

        def advance(at):
            pool[after + at] = pool[lay.minv + at - 1] * pool[lay.sums + at] - pool[here + at]

        ends((here + low, here + high), (low, high), 1.0 / shift)
        loop(low + 1, high, apply, 2)
        loop(low, high, each(join_width))
        loop(low + 1, high, each(advance))

    def constant(kind, at):
        layers = [[join_span(coef[member + at + side, kind, elem]) for elem in range(elems)] for side in (-1, 0, 1)]
        wide_sum = lambda low, mid, high: mid + jnp.where(sub == 0, low, jnp.where(sub == 7, high, 0.0))
        inside = [wide_sum(*(layers[side][elem] for side in range(3))) for elem in range(elems)]
        planes = []
        for elem in range(elems):
            first = inside[elem] if elem == 0 else inside[elem] + inside[elem - 1]
            last = inside[elem] if elem == elems - 1 else inside[elem] + inside[elem + 1]
            planes += [first] + [inside[elem]] * 6 + [last]
        return jnp.concatenate(planes, axis=0)

    def start_slab(at):
        cap = jnp.concatenate([tall(coef[member + at, 1, elem], face_ref) for elem in range(elems)], axis=0)
        pool[lay.sums + at] = join_depth(join_span(cap * pool[lay.cot + member + at]))

    def inverse_slab(at):
        quot = jnp.concatenate([quot_ref[...].reshape(64, span)] * elems, axis=0)
        mass = constant(1, at)
        inverse = 1.0 / jnp.maximum(mass + quot * constant(0, at), TINY)
        pool[lay.minv + at - 1] = inverse
        return inverse, mass

    def first_slab(at):
        inverse, _ = inverse_slab(at)
        pool[lay.basis + at - 1] = inverse * pool[lay.sums + at]

    def inner_slab(at):
        inverse, mass = inverse_slab(at)
        pool[lay.basis + at - 1] = inverse * pool[lay.sums + at]
        pool[lay.ratio + at - 3] = inverse * mass

    loop(0, wide + 2, each(start_slab))
    loop(0, wide + 1, each(join_width))
    loop(1, 3, each(first_slab))
    loop(3, wide - 1, each(inner_slab))
    loop(wide - 1, wide + 1, each(first_slab))

    mid = REACH + 1
    own = pl.ds(pl.multiple_of(height_pos * own_rows, own_rows), own_rows)
    shape = (own_depth, 8, span)
    zpos = lax.broadcasted_iota(jnp.int32, shape, 0) + height_pos * own_depth
    xpos = lax.broadcasted_iota(jnp.int32, shape, 1) + plane_pos * 8

    def copies(pos, extent):
        return jnp.where(((pos % 8 == 7) & (pos < extent - 1)) | ((pos % 8 == 0) & (pos > 0)), 0.5, 1.0)

    share = copies(zpos, depth) * copies(xpos, plane * 8) * jnp.where(opens | closes, 0.5, 1.0)
    omega = jnp.concatenate([omega_ref[...].reshape(64, span)] * own_elems, axis=0)
    weigh[...] = share.reshape(own_rows, span) * omega / pool[lay.minv + REACH, own]

    for level in range(2):
        step(lay.basis + level * wide - 1, lay.basis + (level + 1) * wide - 1, 1 + level, wide - level, SHIFTS[level])
    for vec in range(3):
        fields_ref[vec] = pool[lay.basis + vec * wide + REACH, own]

    def second(vec):
        def begin(at):
            pool[lay.second + at - 3] = pool[lay.ratio + at - 3] * pool[lay.basis + vec * wide + at - 1]

        loop(3, 8, each(begin))
        step(lay.second - 3, lay.second + 1, 3, 7, SHIFTS[0])
        step(lay.second + 1, lay.second + 3, 4, 6, SHIFTS[1])
        fields_ref[3 + vec] = pool[lay.second + 2, own]
        fields_ref[6 + vec] = pool[lay.second + 6, own]
        fields_ref[9 + vec] = pool[lay.second + 8, own]

    loop(0, 3, each(second))

    slot = member + mid
    start = height_pos * own_elems

    def total(values):
        return jnp.sum(values.reshape(shape), axis=0)

    parts = []
    left = [weigh[...] * fields_ref[i] for i in range(3)]
    parts += [total(left[i] * fields_ref[j]) for i, j in PAIRS]
    lasts = (2, 9, 10, 11)
    energy = []
    for k in (0, 2):
        energy += operator([fields_ref[i] for i in lasts[k : k + 2]], [slot] * 2, 1.0, start)
    energy = [omega * e for e in energy]
    parts.append(total(fields_ref[2] * energy[0]))
    for k, l in PAIRS:
        pairs = PAIRS if k == l else [(i, j) for i in range(3) for j in range(3)]
        left = [weigh[...] * fields_ref[3 + 3 * k + i] for i in range(3)]
        parts += [total(left[i] * fields_ref[3 + 3 * l + j]) for i, j in pairs]
    parts += [total(fields_ref[9 + i] * energy[1 + j]) for i, j in PAIRS]
    lines = [jnp.sum(part, axis=0, keepdims=True) for part in parts]
    lines.append(jnp.zeros((span - len(lines), span), F32))
    sums = lax.dot_general(jnp.ones((8, span), F32), jnp.concatenate(lines, axis=0), (((1,), (1,)), ((), ())), precision=HIGHEST, preferred_element_type=F32)

    heavy = jnp.concatenate([tall(coef[slot, 1, start + elem], face_ref) for elem in range(own_elems)], axis=0) * (omega * 0.125)
    rows_of = []
    for index in range(12):
        mass = heavy * fields_ref[index]
        for elem in range(own_elems):
            rows_of.append(jnp.sum(mass[elem * 64 : elem * 64 + 64], axis=0, keepdims=True))
    stack = jnp.concatenate(rows_of, axis=0)
    cells = span // 8
    per_row = span // cells
    spread = (lax.broadcasted_iota(jnp.int32, (span, span), 0) // 8 == lax.broadcasted_iota(jnp.int32, (span, span), 1) % cells).astype(F32)
    stack = jnp.dot(stack, spread, precision=HIGHEST, preferred_element_type=F32)
    place = lax.broadcasted_iota(jnp.int32, stack.shape, 0) % per_row == lax.broadcasted_iota(jnp.int32, stack.shape, 1) // cells
    stack = jnp.where(place, stack, 0.0).reshape(stack.shape[0] // per_row, per_row, span)
    info = jnp.concatenate([jnp.sum(stack, axis=1), sums[:1]], axis=0)
    info_ref[...] = jnp.broadcast_to(info[None], info_ref.shape)


def galerkin(gram, energy):
    n00, n01, n02, n11, n12, n22 = gram
    first, later = SHIFTS
    h00, h01, h02 = first * (n01 + n00), first * (n11 + n01), first * (n12 + n02)
    h11, h12 = later * (n12 + n11), later * (n22 + n12)
    low10, low20 = h01 / h00, h02 / h00
    piv1 = h11 - low10 * h01
    off12 = h12 - low10 * h02
    low21 = off12 / piv1
    piv2 = energy - low20 * h02 - low21 * off12
    y0 = n00
    y1 = n01 - low10 * y0
    y2 = n02 - low20 * y0 - low21 * y1
    c2 = y2 / piv2
    c1 = y1 / piv1 - low21 * c2
    c0 = y0 / h00 - low10 * c1 - low20 * c2
    return c0, c1, c2


def combine_kernel(info_ref, fields_ref, owner_ref, place_ref, second_ref, first_ref, grad_ref):
    devices, lines, span = info_ref.shape
    ones = jnp.ones((devices, span), F32)
    contract = (((0,), (0,)), ((), ()))
    wide = lax.dot_general(info_ref[:, lines - 1, :], ones, contract, precision=HIGHEST, preferred_element_type=F32)
    take = [wide[i : i + 1, :] for i in range(7 + 45 + 6)]
    coef = galerkin(take[:6], take[6])
    at = 7
    double = [(2.0 if i != j else 1.0) * coef[i] * coef[j] for i, j in PAIRS]
    every = [coef[i] * coef[j] for i in range(3) for j in range(3)]
    gram = []
    for k, l in PAIRS:
        factors = double if k == l else every
        gram.append(sum(f * t for f, t in zip(factors, take[at : at + len(factors)])))
        at += len(factors)
    energy = sum(f * t for f, t in zip(double, take[at : at + 6]))
    outer = galerkin(gram, energy)
    factors = list(coef) + [d * c for d in outer for c in coef]

    second = factors[0] * fields_ref[0] + factors[1] * fields_ref[1] + factors[2] * fields_ref[2]
    second_ref[...] = second.reshape(second_ref.shape)
    first = factors[3] * fields_ref[3]
    for i in range(4, 12):
        first = first + factors[i] * fields_ref[i]
    first_ref[...] = first.reshape(first_ref.shape)

    per_line = 12 // (lines - 1)
    cells = span // per_line
    row = lax.broadcasted_iota(jnp.int32, (span, span), 0)
    for step in range(2):
        holder = (owner_ref[step : step + 1, :] == lax.broadcasted_iota(jnp.int32, (devices, span), 0)).astype(F32)
        here = place_ref[step : step + 1, :] == row % cells
        result = jnp.zeros((1, span), F32)
        for line in range(lines - 1):
            fields = [f for f in range(line * per_line, (line + 1) * per_line) if (f >= 3) == (step == 0)]
            if not fields:
                continue
            picked = lax.dot_general(info_ref[:, line, :], holder, contract, precision=HIGHEST, preferred_element_type=F32)
            picked = jnp.where(here, picked, 0.0)
            for f in fields:
                lo = (f - line * per_line) * cells
                result = result + factors[f] * jnp.sum(picked[lo : lo + cells], axis=0, keepdims=True)
        grad_ref[step : step + 1, :] = result


def per_device(counts, cotangent, conductivity, capacity, sources):
    height, plane = counts
    depth, _, span = cotangent.shape
    elems = depth // 8
    cells = span // 8
    groups = plane // GROUP
    devices = height * plane
    vmem = pl.BlockSpec(memory_space=pltpu.VMEM)

    rows = depth * 8 + coef_rows(elems)
    message, edge = pl.pallas_call(
        pack_kernel,
        out_shape=(jax.ShapeDtypeStruct((rows, span), F32), jax.ShapeDtypeStruct((depth + coef_rows(elems), span), F32)),
        in_specs=[vmem] * 3,
        out_specs=(vmem, vmem),
    )(cotangent, conductivity, capacity)

    beyond = swap(edge, "plane", [(g * GROUP + GROUP - 1, (g + 1) * GROUP) for g in range(groups - 1)])
    gathered = message
    width = 1
    while width < GROUP:
        other = swap(gathered, "plane", [(p, p ^ width) for p in range(plane) if p & width == 0])
        gathered = jnp.concatenate([gathered, other], axis=0)
        width *= 2
    gathered = jnp.concatenate([gathered, edge if beyond is None else beyond], axis=0)

    def group_pairs(turn):
        return [(g * GROUP + m, (g + 1) * GROUP + m) for g in range(turn, groups - 1, 2) for m in range(GROUP)]

    sent = {"own": gathered, "pair": swap(gathered, "plane", group_pairs(0)), "cross": swap(gathered, "plane", group_pairs(1))}
    present = tuple(name for name, arr in sent.items() if arr is not None)
    operands = [sent[name] for name in present]
    for turn in range(1, height):
        operands += [lax.ppermute(sent[name], "height", [(h, (h + turn) % height) for h in range(height)]) for name in present]

    lay = Layout()
    consts = tables(span)
    slots = 3 * GROUP + 2
    fields, info = pl.pallas_call(
        functools.partial(basis_kernel, counts, present),
        out_shape=(jax.ShapeDtypeStruct((12, depth * 8, span), F32), jax.ShapeDtypeStruct((devices, 12 * elems * cells // span + 1, span), F32)),
        in_specs=[vmem] * (len(operands) + len(consts)),
        out_specs=(vmem, vmem),
        scratch_shapes=[
            pltpu.VMEM((lay.total, depth * 8 * height, span), F32),
            pltpu.VMEM((slots, 2, elems * height, 8, span), F32),
            pltpu.VMEM((depth * 8, span), F32),
        ],
        compiler_params=pltpu.CompilerParams(vmem_limit_bytes=56 * 1024 * 1024),
    )(*operands, *[jnp.asarray(c) for c in consts])

    shared = lax.all_to_all(info, ("height", "plane"), 0, 0, tiled=True)

    cell = sources % cells
    column = sources // cells
    wide_elem = column % plane
    deep_elem = column // plane
    owner = (deep_elem // elems) * plane + wide_elem
    place = (deep_elem % elems) * cells + cell
    return pl.pallas_call(
        combine_kernel,
        out_shape=(
            jax.ShapeDtypeStruct(cotangent.shape, F32),
            jax.ShapeDtypeStruct(cotangent.shape, F32),
            jax.ShapeDtypeStruct(sources.shape, F32),
        ),
        in_specs=[vmem] * 4,
        out_specs=(vmem, vmem, vmem),
        compiler_params=pltpu.CompilerParams(vmem_limit_bytes=32 * 1024 * 1024),
    )(shared, fields, owner, place)


def solution(mesh):
    counts = (mesh.shape["height"], mesh.shape["plane"])
    field = P("height", "plane", None)
    return jax.shard_map(
        functools.partial(per_device, counts),
        mesh=mesh,
        in_specs=(field, field, field, P()),
        out_specs=(field, field, P()),
        check_vma=False,
    )
```

time: 69.9 us -> 51 us (0.73)
  Pallas kernels: 26.3 us -> 12.2 us
  waiting for transfers between devices: 20.5 us -> 18.2 us
  local copies, waits for them, and re-layouts: 3.93 us -> 2.18 us
    pallas_call x2, Pallas kernels: 25.2 us -> 11.1 us  [the longest x1 9.51 us: per_device(): pl.pallas_call(functools.partial(basis_kernel, counts, present), out_shap...]
    ppermute x5, starting transfers between devices: 11.6 us -> 9.04 us  [swap(): return lax.ppermute(value, axis, [*pairs, *((b, a) for a, b in pairs)])]
    ppermute x5, waiting for transfers between devices: 12 us -> 9.44 us  [swap(): return lax.ppermute(value, axis, [*pairs, *((b, a) for a, b in pairs)])]
    all_to_all x1, starting transfers between devices: 4.88 us -> 6.81 us  [per_device(): shared = lax.all_to_all(info, ('height', 'plane'), 0, 0, tiled=True)]
    broadcast_in_dim x1 -> x0, local copies, waits for them, and re-layouts: 1.32 us -> none  [per_device(): jnp.broadcast_to(info[None], (devices, *info.shape))]
    unnamed x22 -> x21, local copies, waits for them, and re-layouts: 2.6 us -> 2.18 us
    ppermute x4 -> x3, waiting for transfers between devices: 1.23 us -> 1.43 us  [per_device(): lax.ppermute(sent[name], 'height', [(h, (h + turn) % height) for h in ran...]
  transfers between devices with their start and end apart: 10 -> 9, of which waited for: 6 -> 6; matrix products, arithmetic and copies ran while one was open for 0% -> 2% of each run, Pallas kernels for 0% -> 0%
where the time goes in v2:
time: 51 us; the launch traced here: 50.7 us
  waiting for transfers between devices  18.2 us (36%)
  starting transfers between devices  16.4 us (32%)
  Pallas kernels  12.2 us (24%)
  local copies, waits for them, and re-layouts  2.18 us (4%)
  other arithmetic  0.93 us (2%)
  between operations  0.77 us (2%)
    pallas_call x1, Pallas kernels, per_device(): pl.pallas_call(functools.partial(basis_kernel, counts, present), out_shap...  9.51 us
    ppermute x5, waiting for transfers between devices, swap(): return lax.ppermute(value, axis, [*pairs, *((b, a) for a, b in pairs)])  9.44 us
    ppermute x5, starting transfers between devices, swap(): return lax.ppermute(value, axis, [*pairs, *((b, a) for a, b in pairs)])  9.04 us
    all_to_all x1, waiting for transfers between devices, per_device(): shared = lax.all_to_all(info, ('height', 'plane'), 0, 0, tiled=True)  7.3 us
    all_to_all x1, starting transfers between devices, per_device(): shared = lax.all_to_all(info, ('height', 'plane'), 0, 0, tiled=True)  6.81 us
    unnamed x21, local copies, waits for them, and re-layouts  2.18 us
    pallas_call x1, Pallas kernels, per_device(): pl.pallas_call(pack_kernel, out_shape=(jax.ShapeDtypeStruct((rows, span),...  1.62 us
    ppermute x3, waiting for transfers between devices, per_device(): lax.ppermute(sent[name], 'height', [(h, (h + turn) % height) for h in ran...  1.43 us
  transfers between devices with their start and end apart: 9, of which 6 were waited for; matrix products, arithmetic and copies ran while one was open for 2% of the time, Pallas kernels for 0%

profile of v2, /device:TPU:0, one launch (start us, length us, event | category | flops | bytes accessed | tf_op | source)
XLA Modules:
  0.0 50.7 jit_solution(9240506665951583502)
XLA Ops:
  0.6 1.6 %shard_map.121 = (f32[136,128]{1,0:T(8,128)}, f32[24,128]{1,0:T(8,128)}) custom-call(f32[16,8,128]{2,1,0:T(8,128)} %cot_ref.1, f32[2,1,16]{2,1,0:T(1,128)} %kap_ref.1, f32[2,1,16]{2,1,0:T(1,128)} %cap_ref.1), custom_call_target="tpu_custom_call" | custom-call | tf_op jit(solution)/shard_map/pallas_call | solution.py:462
  2.3 2.9 %collective-permute-start = (f32[136,128]{1,0:T(8,128)}, f32[136,128]{1,0:T(8,128)S(1)}, u32[]{:S(2)}, u32[]{:S(2)}) collective-permute-start(f32[136,128]{1,0:T(8,128)} %get-tuple-element.7), channel_id=1, source_target_pairs={{0,1},{2,3},{4,5},{6,7},{8,9},{10,11},{12,13},{14,15},{1,0},{3,2},... | collective-permute-start | bytes 208904 | tf_op jit(solution)/shard_map/ppermute | solution.py:67
  5.2 0.8 %collective-permute-start.2 = (f32[24,128]{1,0:T(8,128)}, f32[24,128]{1,0:T(8,128)S(1)}, u32[]{:S(2)}, u32[]{:S(2)}) collective-permute-start(f32[24,128]{1,0:T(8,128)} %get-tuple-element.8), channel_id=1, source_target_pairs={{3,4},{7,8},{11,12},{4,3},{8,7},{12,11},{19,20},{23,24},{27,28},{2... | collective-permute-start | bytes 36872 | tf_op jit(solution)/shard_map/ppermute | solution.py:67
  6.0 1.7 %collective-permute-done = f32[136,128]{1,0:T(8,128)S(1)} collective-permute-done((f32[136,128]{1,0:T(8,128)}, f32[136,128]{1,0:T(8,128)S(1)}, u32[]{:S(2)}, u32[]{:S(2)}) %collective-permute-start) | collective-permute-done | bytes 69664 | tf_op jit(solution)/shard_map/ppermute | solution.py:67
  7.7 0.9 %pad_maximum_fusion = f32[272,128]{1,0:T(8,128)S(1)} fusion(f32[136,128]{1,0:T(8,128)S(1)} %collective-permute-done, f32[136,128]{1,0:T(8,128)} %get-tuple-element.7), kind=kLoop, calls=%fused_computation | loop fusion | flops 34816 | bytes 278528 | tf_op jit(solution)/shard_map/concatenate | solution.py:474
  8.6 2.1 %collective-permute-start.1 = (f32[272,128]{1,0:T(8,128)S(1)}, f32[272,128]{1,0:T(8,128)S(1)}, u32[]{:S(2)}, u32[]{:S(2)}) collective-permute-start(f32[272,128]{1,0:T(8,128)S(1)} %pad_maximum_fusion), channel_id=1, source_target_pairs={{0,2},{1,3},{4,6},{5,7},{8,10},{9,11},{12,14},{13,15},{2,0},{3,1},... | collective-permute-start | bytes 417800 | tf_op jit(solution)/shard_map/ppermute | solution.py:67
  10.7 3.0 %collective-permute-done.1 = f32[272,128]{1,0:T(8,128)S(1)} collective-permute-done((f32[272,128]{1,0:T(8,128)S(1)}, f32[272,128]{1,0:T(8,128)S(1)}, u32[]{:S(2)}, u32[]{:S(2)}) %collective-permute-start.1) | collective-permute-done | bytes 139296 | tf_op jit(solution)/shard_map/ppermute | solution.py:67
  13.8 0.0 copy-start.8
  13.8 2.5 %collective-permute-start.3 = (f32[568,128]{1,0:T(8,128)S(1)}, f32[568,128]{1,0:T(8,128)S(1)}, u32[]{:S(2)}, u32[]{:S(2)}) collective-permute-start(f32[568,128]{1,0:T(8,128)S(1)} %constant_dynamic-update-slice_fusion.refs_0_), channel_id=1, source_target_pairs={{0,4},{1,5},{2,6},{3,7},{8,12},{9,13},{10,14},{11,15},{4,0},{5,1},... | collective-permute-start | bytes 872456 | tf_op jit(solution)/shard_map/ppermute | solution.py:67
  16.3 0.7 %collective-permute-start.4 = (f32[568,128]{1,0:T(8,128)S(1)}, f32[568,128]{1,0:T(8,128)S(1)}, u32[]{:S(2)}, u32[]{:S(2)}) collective-permute-start(f32[568,128]{1,0:T(8,128)S(1)} %constant_dynamic-update-slice_fusion.refs_0_), channel_id=1, source_target_pairs={{4,8},{5,9},{6,10},{7,11},{8,4},{9,5},{10,6},{11,7},{20,24},{21,25... | collective-permute-start | bytes 872456 | tf_op jit(solution)/shard_map/ppermute | solution.py:67
  17.0 0.1 collective-permute-start.5
  17.1 4.7 %collective-permute-done.3.refs_1_ = f32[568,128]{1,0:T(8,128)S(1)} collective-permute-done((f32[568,128]{1,0:T(8,128)S(1)}, f32[568,128]{1,0:T(8,128)S(1)}, u32[]{:S(2)}, u32[]{:S(2)}) %collective-permute-start.3) | collective-permute-done | bytes 290848 | tf_op jit(solution)/shard_map/ppermute | solution.py:67
  21.8 0.0 collective-permute-start.6
  21.8 0.0 collective-permute-done.4.refs_2_
  21.8 0.5 collective-permute-start.7
  22.4 1.0 %collective-permute-done.6.refs_4_ = f32[568,128]{1,0:T(8,128)S(1)} collective-permute-done((f32[568,128]{1,0:T(8,128)S(1)}, f32[568,128]{1,0:T(8,128)S(1)}, u32[]{:S(2)}, u32[]{:S(2)}) %collective-permute-start.6) | collective-permute-done | bytes 290848 | tf_op jit(solution)/shard_map/ppermute | solution.py:485
  23.4 0.4 collective-permute-done.7.refs_5_
  23.8 0.3 copy-done.5
  24.1 0.7 %copy-done.6 = f32[568,128]{1,0:T(8,128)} copy-done((f32[568,128]{1,0:T(8,128)}, f32[568,128]{1,0:T(8,128)S(1)}, u32[]{:S(2)}) %copy-start.6) | copy-done | bytes 290840
  24.8 9.5 %shard_map.122 = (f32[12,128,128]{2,1,0:T(8,128)}, f32[32,4,128]{2,1,0:T(4,128)}) custom-call(f32[568,128]{1,0:T(8,128)} %copy-done.1, f32[568,128]{1,0:T(8,128)} %copy-done.2, f32[568,128]{1,0:T(8,128)} %copy-done.3, f32[568,128]{1,0:T(8,128)} %copy-done.4, f32[568,128]{1,0:T(8,128)} %copy-done.5, f32[568,128]{1,0:T(8,128)} %copy-done.6, ...), custom_call_target="tpu_custom_call" | custom-call | tf_op jit(solution)/shard_map/pallas_call | solution.py:490
  34.3 6.8 %all-to-all-start = ((f32[32,4,128]{2,1,0:T(4,128)}), f32[32,4,128]{2,1,0:T(4,128)S(1)}, u32[]{:S(2)}, u32[]{:S(2)}) async-start(f32[32,4,128]{2,1,0:T(4,128)} %get-tuple-element.9), calls=%async_computation | async-start | bytes 131072 | tf_op jit(solution)/shard_map/all_to_all | solution.py:503
  41.2 7.3 %all-to-all-done.info_ref = f32[32,4,128]{2,1,0:T(4,128)S(1)} async-done(((f32[32,4,128]{2,1,0:T(4,128)}), f32[32,4,128]{2,1,0:T(4,128)S(1)}, u32[]{:S(2)}, u32[]{:S(2)}) %all-to-all-start) | async-done | bytes 65568 | tf_op jit(solution)/shard_map/all_to_all | solution.py:503
  48.5 1.1 %copy-done = f32[12,128,128]{2,1,0:T(8,128)S(1)} copy-done((f32[12,128,128]{2,1,0:T(8,128)S(1)}, f32[12,128,128]{2,1,0:T(8,128)}, u32[]{:S(2)}) %copy-start) | copy-done | bytes 786456
  49.6 1.0 %shard_map.123 = (f32[16,8,128]{2,1,0:T(8,128)}, f32[16,8,128]{2,1,0:T(8,128)}, f32[2,128]{1,0:T(2,128)}) custom-call(f32[32,4,128]{2,1,0:T(4,128)S(1)} %all-to-all-done.info_ref, f32[12,128,128]{2,1,0:T(8,128)S(1)} %copy-done, s32[2,128]{1,0:T(2,128)S(1)} %fusion.owner_ref, s32[2,128]{1,0:T(2,128)S(1)} %get-tuple-element.11.place_ref), custom_call_target="tpu_custom_call" | custom-call | tf_op jit(solution)/shard_map/pallas_call | solution.py:511
  (22 shorter events, 0.1 us)
Async XLA Ops:
  2.3 5.4 %collective-permute-start = (f32[136,128]{1,0:T(8,128)}, f32[136,128]{1,0:T(8,128)S(1)}, u32[]{:S(2)}, u32[]{:S(2)}) collective-permute-start(f32[136,128]{1,0:T(8,128)} %get-tuple-element.7), channel_id=1, source_target_pairs={{0,1},{2,3},{4,5},{6,7},{8,9},{10,11},{12,13},{14,15},{1,0},{3,2},... | collective-permute-start | bytes 208904 | tf_op jit(solution)/shard_map/ppermute | solution.py:67
  5.2 5.5 %copy-start.7 = (f32[136,128]{1,0:T(8,128)S(1)}, f32[136,128]{1,0:T(8,128)}, u32[]{:S(2)}) copy-start(f32[136,128]{1,0:T(8,128)} %get-tuple-element.7) | copy-start | bytes 208900
  5.2 8.6 %collective-permute-start.2 = (f32[24,128]{1,0:T(8,128)}, f32[24,128]{1,0:T(8,128)S(1)}, u32[]{:S(2)}, u32[]{:S(2)}) collective-permute-start(f32[24,128]{1,0:T(8,128)} %get-tuple-element.8), channel_id=1, source_target_pairs={{3,4},{7,8},{11,12},{4,3},{8,7},{12,11},{19,20},{23,24},{27,28},{2... | collective-permute-start | bytes 36872 | tf_op jit(solution)/shard_map/ppermute | solution.py:67
  8.6 5.2 %collective-permute-start.1 = (f32[272,128]{1,0:T(8,128)S(1)}, f32[272,128]{1,0:T(8,128)S(1)}, u32[]{:S(2)}, u32[]{:S(2)}) collective-permute-start(f32[272,128]{1,0:T(8,128)S(1)} %pad_maximum_fusion), channel_id=1, source_target_pairs={{0,2},{1,3},{4,6},{5,7},{8,10},{9,11},{12,14},{13,15},{2,0},{3,1},... | collective-permute-start | bytes 417800 | tf_op jit(solution)/shard_map/ppermute | solution.py:67
  13.8 8.6 %copy-start.8 = (s32[2,128]{1,0:T(2,128)S(1)}, s32[2,128]{1,0:T(2,128)}, u32[]{:S(2)}) copy-start(s32[2,128]{1,0:T(2,128)} %param.13) | copy-start | bytes 3076
  13.8 10.0 %copy-start.1 = (f32[568,128]{1,0:T(8,128)}, f32[568,128]{1,0:T(8,128)S(1)}, u32[]{:S(2)}) copy-start(f32[568,128]{1,0:T(8,128)S(1)} %constant_dynamic-update-slice_fusion.refs_0_) | copy-start | bytes 872452
  13.8 8.0 %collective-permute-start.3 = (f32[568,128]{1,0:T(8,128)S(1)}, f32[568,128]{1,0:T(8,128)S(1)}, u32[]{:S(2)}, u32[]{:S(2)}) collective-permute-start(f32[568,128]{1,0:T(8,128)S(1)} %constant_dynamic-update-slice_fusion.refs_0_), channel_id=1, source_target_pairs={{0,4},{1,5},{2,6},{3,7},{8,12},{9,13},{10,14},{11,15},{4,0},{5,1},... | collective-permute-start | bytes 872456 | tf_op jit(solution)/shard_map/ppermute | solution.py:67
  16.3 5.5 %collective-permute-start.4 = (f32[568,128]{1,0:T(8,128)S(1)}, f32[568,128]{1,0:T(8,128)S(1)}, u32[]{:S(2)}, u32[]{:S(2)}) collective-permute-start(f32[568,128]{1,0:T(8,128)S(1)} %constant_dynamic-update-slice_fusion.refs_0_), channel_id=1, source_target_pairs={{4,8},{5,9},{6,10},{7,11},{8,4},{9,5},{10,6},{11,7},{20,24},{21,25... | collective-permute-start | bytes 872456 | tf_op jit(solution)/shard_map/ppermute | solution.py:67
  17.0 5.4 %collective-permute-start.5 = (f32[568,128]{1,0:T(8,128)S(1)}, f32[568,128]{1,0:T(8,128)S(1)}, u32[]{:S(2)}, u32[]{:S(2)}) collective-permute-start(f32[568,128]{1,0:T(8,128)S(1)} %constant_dynamic-update-slice_fusion.refs_0_), channel_id=1, source_target_pairs={{0,16},{16,0},{1,17},{17,1},{2,18},{18,2},{3,19},{19,3},{4,20},{20... | collective-permute-start | bytes 872456 | tf_op jit(solution)/shard_map/ppermute | solution.py:485
  21.8 2.0 %copy-start.2 = (f32[568,128]{1,0:T(8,128)}, f32[568,128]{1,0:T(8,128)S(1)}, u32[]{:S(2)}) copy-start(f32[568,128]{1,0:T(8,128)S(1)} %collective-permute-done.3.refs_1_) | copy-start | bytes 872452
  21.8 1.6 %collective-permute-start.6 = (f32[568,128]{1,0:T(8,128)S(1)}, f32[568,128]{1,0:T(8,128)S(1)}, u32[]{:S(2)}, u32[]{:S(2)}) collective-permute-start(f32[568,128]{1,0:T(8,128)S(1)} %collective-permute-done.3.refs_1_), channel_id=1, source_target_pairs={{0,16},{16,0},{1,17},{17,1},{2,18},{18,2},{3,19},{19,3},{4,20},{20... | collective-permute-start | bytes 872456 | tf_op jit(solution)/shard_map/ppermute | solution.py:485
  21.8 2.0 %copy-start.3 = (f32[568,128]{1,0:T(8,128)}, f32[568,128]{1,0:T(8,128)S(1)}, u32[]{:S(2)}) copy-start(f32[568,128]{1,0:T(8,128)S(1)} %collective-permute-done.4.refs_2_) | copy-start | bytes 872452
  21.8 2.0 %collective-permute-start.7 = (f32[568,128]{1,0:T(8,128)S(1)}, f32[568,128]{1,0:T(8,128)S(1)}, u32[]{:S(2)}, u32[]{:S(2)}) collective-permute-start(f32[568,128]{1,0:T(8,128)S(1)} %collective-permute-done.4.refs_2_), channel_id=1, source_target_pairs={{0,16},{16,0},{1,17},{17,1},{2,18},{18,2},{3,19},{19,3},{4,20},{20... | collective-permute-start | bytes 872456 | tf_op jit(solution)/shard_map/ppermute | solution.py:485
  22.4 1.5 %copy-start.4 = (f32[568,128]{1,0:T(8,128)}, f32[568,128]{1,0:T(8,128)S(1)}, u32[]{:S(2)}) copy-start(f32[568,128]{1,0:T(8,128)S(1)} %collective-permute-done.5.refs_3_) | copy-start | bytes 872452
  23.4 0.7 %copy-start.5 = (f32[568,128]{1,0:T(8,128)}, f32[568,128]{1,0:T(8,128)S(1)}, u32[]{:S(2)}) copy-start(f32[568,128]{1,0:T(8,128)S(1)} %collective-permute-done.6.refs_4_) | copy-start | bytes 872452
  24.1 0.7 %copy-start.6 = (f32[568,128]{1,0:T(8,128)}, f32[568,128]{1,0:T(8,128)S(1)}, u32[]{:S(2)}) copy-start(f32[568,128]{1,0:T(8,128)S(1)} %collective-permute-done.7.refs_5_) | copy-start | bytes 872452
  34.3 14.1 %all-to-all-start = ((f32[32,4,128]{2,1,0:T(4,128)}), f32[32,4,128]{2,1,0:T(4,128)S(1)}, u32[]{:S(2)}, u32[]{:S(2)}) async-start(f32[32,4,128]{2,1,0:T(4,128)} %get-tuple-element.9), calls=%async_computation | async-start | bytes 131072 | tf_op jit(solution)/shard_map/all_to_all | solution.py:503
  48.5 1.1 %copy-start = (f32[12,128,128]{2,1,0:T(8,128)S(1)}, f32[12,128,128]{2,1,0:T(8,128)}, u32[]{:S(2)}) copy-start(f32[12,128,128]{2,1,0:T(8,128)} %get-tuple-element.10.fields_ref) | copy-start | bytes 2359300

commit v3 on v2

--- a/solution.py
+++ b/solution.py
@@ -88,27 +88,25 @@
 
 
 class Layout:
-    def __init__(self):
+    def __init__(self, tall):
         wide = 2 * REACH + 1
         self.wide = wide
-        self.cot = 0
-        self.sums = self.cot + 3 * GROUP + 2
-        self.minv = self.sums + wide + 2
+        self.at_once = 1 if tall else 3
+        self.sums = 0
+        self.minv = max(wide, 5 * self.at_once)
         self.ratio = self.minv + wide
         self.basis = self.ratio + 5
         self.second = self.basis + 3 * wide
-        self.total = self.second + wide
+        self.total = self.second + wide * self.at_once
 
 
 def basis_kernel(counts, present, *refs):
     height, plane = counts
-    lay = Layout()
-    wide = lay.wide
     n_in = len(present) * height
     msgs = refs[:n_in]
     face_ref, ends_ref, row_a_ref, row_b_ref, omega_ref, quot_ref = refs[n_in : n_in + 6]
     fields_ref, info_ref = refs[n_in + 6 : n_in + 8]
-    pool, coef, weigh = refs[n_in + 8 :]
+    pool, raw, coef, weigh = refs[n_in + 8 :]
     rows, span = pool.shape[1:]
     depth = rows // 8
     own_depth = depth // height
@@ -121,6 +119,33 @@
     even = lax.rem(plane_pos // GROUP, 2) == 0
     slab_rows = own_rows + coef_rows(own_elems)
     whole = elems > 4
+    lay = Layout(whole)
+    wide = lay.wide
+
+    lane = lax.broadcasted_iota(jnp.int32, (8, span), 1)
+    sub = lax.broadcasted_iota(jnp.int32, (8, span), 0)
+    opens = (lane % 8 == 0) & (lane > 0)
+    closes = (lane % 8 == 7) & (lane < span - 1)
+
+    def tall(mask, like):
+        return jnp.concatenate([mask] * (like.shape[0] // 8), axis=0) if like.shape[0] > 8 else mask
+
+    def join_span(values):
+        up, down = pltpu.roll(values, 1, 1), pltpu.roll(values, span - 1, 1)
+        return values + jnp.where(tall(opens, values), up, jnp.where(tall(closes, values), down, 0.0))
+
+    def join_depth(values):
+        planes = []
+        layers = values.shape[0] // 64
+        for elem in range(layers):
+            top = elem * 64
+            first, last = values[top : top + 8], values[top + 56 : top + 64]
+            if elem > 0:
+                first = first + values[top - 8 : top]
+            if elem < layers - 1:
+                last = last + values[top + 64 : top + 72]
+            planes += [first, values[top + 8 : top + 56], last]
+        return jnp.concatenate(planes, axis=0)
 
     def stage_coef(msg, top, slot, block):
         for kind in range(2):
@@ -128,16 +153,22 @@
                 at = top + kind * own_elems + elem
                 coef[slot, kind, block * own_elems + elem] = jnp.broadcast_to(msg[at : at + 1, :], (8, span))
 
+    def caps(msg, top):
+        return [jnp.broadcast_to(msg[at : at + 1, :], (8, span)) for at in range(top + own_elems, top + 2 * own_elems)]
+
     def stage(msg, piece, slot, block):
         top = piece * slab_rows
-        pool[lay.cot + slot, pl.ds(pl.multiple_of(block * own_rows, own_rows), own_rows)] = msg[top : top + own_rows, :]
+        heavy = jnp.concatenate([c for c in caps(msg, top + own_rows) for _ in range(8)], axis=0)
+        value = join_depth(join_span(heavy * msg[top : top + own_rows, :]))
+        raw[slot, pl.ds(pl.multiple_of(block * own_rows, own_rows), own_rows)] = value
         stage_coef(msg, top + own_rows, slot, block)
 
     def stage_face(msg, slot, block):
         top = GROUP * slab_rows
-        face = msg[top : top + own_depth, :]
-        spread = jnp.concatenate([jnp.broadcast_to(face[z : z + 1], (8, span)) for z in range(own_depth)], axis=0)
-        pool[lay.cot + slot, pl.ds(pl.multiple_of(block * own_rows, own_rows), own_rows)] = spread
+        heavy = jnp.concatenate(caps(msg, top + own_depth), axis=0)
+        face = join_span(heavy * msg[top : top + own_depth, :])
+        value = join_depth(jnp.concatenate([jnp.broadcast_to(face[z : z + 1], (8, span)) for z in range(own_depth)], axis=0))
+        raw[slot, pl.ds(pl.multiple_of(block * own_rows, own_rows), own_rows)] = value
         stage_coef(msg, top + own_depth, slot, block)
 
     def sides(name):
@@ -148,7 +179,7 @@
         if name not in present:
             base, beyond = sides(name)
             for slot in [base + piece for piece in range(GROUP)] + [beyond]:
-                pool[lay.cot + slot] = jnp.zeros((rows, span), F32)
+                raw[slot] = jnp.zeros((rows, span), F32)
                 coef[slot] = jnp.zeros(coef.shape[1:], F32)
     for turn in range(height):
         block = lax.rem(height_pos - turn + height, height)
@@ -162,38 +193,14 @@
             for piece in range(GROUP):
                 stage(msg, piece, base + jnp.bitwise_xor(member, piece), block)
 
-    lane = lax.broadcasted_iota(jnp.int32, (8, span), 1)
-    sub = lax.broadcasted_iota(jnp.int32, (8, span), 0)
-    opens = (lane % 8 == 0) & (lane > 0)
-    closes = (lane % 8 == 7) & (lane < span - 1)
-
-    def tall(mask, like):
-        return jnp.concatenate([mask] * (like.shape[0] // 8), axis=0) if like.shape[0] > 8 else mask
-
-    def join_span(values):
-        up, down = pltpu.roll(values, 1, 1), pltpu.roll(values, span - 1, 1)
-        return values + jnp.where(tall(opens, values), up, jnp.where(tall(closes, values), down, 0.0))
-
-    def join_depth(values):
-        planes = []
-        for elem in range(elems):
-            top = elem * 64
-            first, last = values[top : top + 8], values[top + 56 : top + 64]
-            if elem > 0:
-                first = first + values[top - 8 : top]
-            if elem < elems - 1:
-                last = last + values[top + 64 : top + 72]
-            planes += [first, values[top + 8 : top + 56], last]
-        return jnp.concatenate(planes, axis=0)
-
-    def face_at(at, width_node):
-        return lay.sums + at, pl.ds(width_node, depth, stride=8)
-
-    def join_width(at):
-        low, high = face_at(at, 7), face_at(at + 1, 0)
-        both = pool[low] + pool[high]
-        pool[low] = both
-        pool[high] = both
+    def face_at(slot, width_node):
+        return slot, pl.ds(width_node, depth, stride=8)
+
+    def join_width(store, slot):
+        low, high = face_at(slot, 7), face_at(slot + 1, 0)
+        both = store[low] + store[high]
+        store[low] = both
+        store[high] = both
 
     def loop(start, stop, body, step=1):
         if whole:
@@ -241,7 +248,7 @@
                 out[i].append(cap * v[top : top + 64] + kap * lin)
         return [jnp.concatenate(o, axis=0) for o in out]
 
-    def ends(sources, at, scale):
+    def ends(sources, targets, at, scale):
         halves = [split(pool[s]) for s in sources]
         edges = [pool[s, pl.ds(node, depth, stride=8)] for s, node in zip(sources, (7, 0))]
         lines = along_span([split(jnp.concatenate(edges, axis=0))])[0]
@@ -260,21 +267,30 @@
                 if elem < elems - 1:
                     value = value + jnp.where(sub == 7, pltpu.roll(joined[elem + 1], 7, 0), 0.0)
                 final.append(value)
-            pool[face_at(at[i], (7, 0)[i])] = jnp.concatenate(final, axis=0)
-
-    def step(here, after, low, high, shift):
-        def apply(slabs):
-            made = operator([pool[here + at] for at in slabs], [member + at for at in slabs], 1.0 / shift)
-            for at, value in zip(slabs, made):
-                pool[lay.sums + at] = join_depth(join_span(value))
-
-        def advance(at):
-            pool[after + at] = pool[lay.minv + at - 1] * pool[lay.sums + at] - pool[here + at]
-
-        ends((here + low, here + high), (low, high), 1.0 / shift)
-        loop(low + 1, high, apply, 2)
-        loop(low, high, each(join_width))
-        loop(low + 1, high, each(advance))
+            pool[face_at(targets[i], (7, 0)[i])] = jnp.concatenate(final, axis=0)
+
+    def step(chains, low, high, shift):
+        def apply(work):
+            made = operator([pool[here + at] for here, _, at in work], [member + at for _, _, at in work], 1.0 / shift)
+            for (_, sums, at), value in zip(work, made):
+                pool[sums + at] = join_depth(join_span(value))
+
+        for here, sums, _ in chains:
+            ends((here + low, here + high), (sums + low, sums + high), (low, high), 1.0 / shift)
+        if whole:
+            for here, sums, after in chains:
+                loop(low + 1, high, each(lambda at: apply([(here, sums, at)])))
+        else:
+            work = [(here, sums, at) for here, sums, _ in chains for at in range(low + 1, high)]
+            for first in range(0, len(work), 2):
+                apply(work[first : first + 2])
+        for here, sums, after in chains:
+            loop(low, high, each(lambda at: join_width(pool, sums + at)))
+
+            def advance(at):
+                pool[after + at] = pool[lay.minv + at - 1] * pool[sums + at] - pool[here + at]
+
+            loop(low + 1, high, each(advance))
 
     def constant(kind, at):
         layers = [[join_span(coef[member + at + side, kind, elem]) for elem in range(elems)] for side in (-1, 0, 1)]
@@ -287,10 +303,6 @@
             planes += [first] + [inside[elem]] * 6 + [last]
         return jnp.concatenate(planes, axis=0)
 
-    def start_slab(at):
-        cap = jnp.concatenate([tall(coef[member + at, 1, elem], face_ref) for elem in range(elems)], axis=0)
-        pool[lay.sums + at] = join_depth(join_span(cap * pool[lay.cot + member + at]))
-
     def inverse_slab(at):
         quot = jnp.concatenate([quot_ref[...].reshape(64, span)] * elems, axis=0)
         mass = constant(1, at)
@@ -300,21 +312,34 @@
 
     def first_slab(at):
         inverse, _ = inverse_slab(at)
-        pool[lay.basis + at - 1] = inverse * pool[lay.sums + at]
+        pool[lay.basis + at - 1] = inverse * raw[member + at]
 
     def inner_slab(at):
         inverse, mass = inverse_slab(at)
-        pool[lay.basis + at - 1] = inverse * pool[lay.sums + at]
+        pool[lay.basis + at - 1] = inverse * raw[member + at]
         pool[lay.ratio + at - 3] = inverse * mass
 
-    loop(0, wide + 2, each(start_slab))
-    loop(0, wide + 1, each(join_width))
+    def join_blocks(slot):
+        for block in range(1, height):
+            low, high = pl.ds(block * own_rows - 8, 8), pl.ds(block * own_rows, 8)
+            both = raw[slot, low] + raw[slot, high]
+            raw[slot, low] = both
+            raw[slot, high] = both
+
+    loop(0, wide + 2, each(lambda at: join_blocks(member + at)))
+    loop(0, wide + 1, each(lambda at: join_width(raw, member + at)))
     loop(1, 3, each(first_slab))
     loop(3, wide - 1, each(inner_slab))
     loop(wide - 1, wide + 1, each(first_slab))
 
     mid = REACH + 1
-    own = pl.ds(pl.multiple_of(height_pos * own_rows, own_rows), own_rows)
+
+    def own(slot):
+        value = pool[slot, :own_rows]
+        for block in range(1, height):
+            value = jnp.where(height_pos == block, pool[slot, block * own_rows : (block + 1) * own_rows], value)
+        return value
+
     shape = (own_depth, 8, span)
     zpos = lax.broadcasted_iota(jnp.int32, shape, 0) + height_pos * own_depth
     xpos = lax.broadcasted_iota(jnp.int32, shape, 1) + plane_pos * 8
@@ -324,25 +349,32 @@
 
     share = copies(zpos, depth) * copies(xpos, plane * 8) * jnp.where(opens | closes, 0.5, 1.0)
     omega = jnp.concatenate([omega_ref[...].reshape(64, span)] * own_elems, axis=0)
-    weigh[...] = share.reshape(own_rows, span) * omega / pool[lay.minv + REACH, own]
+    weigh[...] = share.reshape(own_rows, span) * omega / own(lay.minv + REACH)
 
     for level in range(2):
-        step(lay.basis + level * wide - 1, lay.basis + (level + 1) * wide - 1, 1 + level, wide - level, SHIFTS[level])
+        step([(lay.basis + level * wide - 1, lay.sums - 1, lay.basis + (level + 1) * wide - 1)], 1 + level, wide - level, SHIFTS[level])
     for vec in range(3):
-        fields_ref[vec] = pool[lay.basis + vec * wide + REACH, own]
-
-    def second(vec):
-        def begin(at):
-            pool[lay.second + at - 3] = pool[lay.ratio + at - 3] * pool[lay.basis + vec * wide + at - 1]
-
-        loop(3, 8, each(begin))
-        step(lay.second - 3, lay.second + 1, 3, 7, SHIFTS[0])
-        step(lay.second + 1, lay.second + 3, 4, 6, SHIFTS[1])
-        fields_ref[3 + vec] = pool[lay.second + 2, own]
-        fields_ref[6 + vec] = pool[lay.second + 6, own]
-        fields_ref[9 + vec] = pool[lay.second + 8, own]
-
-    loop(0, 3, each(second))
+        fields_ref[vec] = own(lay.basis + vec * wide + REACH)
+
+    def second(vecs):
+        homes = [lay.second + wide * i for i in range(lay.at_once)]
+        sums = [lay.sums + 5 * i - 3 for i in range(lay.at_once)]
+        for vec, home in zip(vecs, homes):
+
+            def begin(at):
+                pool[home + at - 3] = pool[lay.ratio + at - 3] * pool[lay.basis + vec * wide + at - 1]
+
+            loop(3, 8, each(begin))
+        step([(h - 3, t, h + 1) for h, t in zip(homes, sums)], 3, 7, SHIFTS[0])
+        step([(h + 1, t, h + 3) for h, t in zip(homes, sums)], 4, 6, SHIFTS[1])
+        for vec, home in zip(vecs, homes):
+            for level, slot in enumerate((2, 6, 8)):
+                fields_ref[3 + 3 * level + vec] = own(home + slot)
+
+    if lay.at_once == 3:
+        second([0, 1, 2])
+    else:
+        loop(0, 3, each(lambda vec: second([vec])))
 
     slot = member + mid
     start = height_pos * own_elems
@@ -464,6 +496,7 @@
         out_shape=(jax.ShapeDtypeStruct((rows, span), F32), jax.ShapeDtypeStruct((depth + coef_rows(elems), span), F32)),
         in_specs=[vmem] * 3,
         out_specs=(vmem, vmem),
+        compiler_params=pltpu.CompilerParams(vmem_limit_bytes=4 * 2**20),
     )(cotangent, conductivity, capacity)
 
     beyond = swap(edge, "plane", [(g * GROUP + GROUP - 1, (g + 1) * GROUP) for g in range(groups - 1)])
@@ -484,9 +517,10 @@
     for turn in range(1, height):
         operands += [lax.ppermute(sent[name], "height", [(h, (h + turn) % height) for h in range(height)]) for name in present]
 
-    lay = Layout()
+    lay = Layout(elems * height > 4)
     consts = tables(span)
     slots = 3 * GROUP + 2
+    slab_bytes = 4 * depth * 8 * height * span
     fields, info = pl.pallas_call(
         functools.partial(basis_kernel, counts, present),
         out_shape=(jax.ShapeDtypeStruct((12, depth * 8, span), F32), jax.ShapeDtypeStruct((devices, 12 * elems * cells // span + 1, span), F32)),
@@ -494,10 +528,11 @@
         out_specs=(vmem, vmem),
         scratch_shapes=[
             pltpu.VMEM((lay.total, depth * 8 * height, span), F32),
+            pltpu.VMEM((slots, depth * 8 * height, span), F32),
             pltpu.VMEM((slots, 2, elems * height, 8, span), F32),
             pltpu.VMEM((depth * 8, span), F32),
         ],
-        compiler_params=pltpu.CompilerParams(vmem_limit_bytes=56 * 1024 * 1024),
+        compiler_params=pltpu.CompilerParams(vmem_limit_bytes=(lay.total + 3 * slots + 14) * slab_bytes + 12 * 2**20),
     )(*operands, *[jnp.asarray(c) for c in consts])
 
     shared = lax.all_to_all(info, ("height", "plane"), 0, 0, tiled=True)
@@ -517,7 +552,7 @@
         ),
         in_specs=[vmem] * 4,
         out_specs=(vmem, vmem, vmem),
-        compiler_params=pltpu.CompilerParams(vmem_limit_bytes=32 * 1024 * 1024),
+        compiler_params=pltpu.CompilerParams(vmem_limit_bytes=8 * 2**20),
     )(shared, fields, owner, place)
 
 

time: 51 us -> 46.8 us (0.918)
  Pallas kernels: 12.2 us -> 8.78 us
  other arithmetic: 0.93 us -> 0.05 us
    pallas_call x1, Pallas kernels: 9.51 us -> 7.59 us  [per_device(): pl.pallas_call(functools.partial(basis_kernel, counts, present), out_shap...]
    pallas_call x1, Pallas kernels: 1.62 us -> 0.14 us  [per_device(): pl.pallas_call(pack_kernel, out_shape=(jax.ShapeDtypeStruct((rows, span),...]
    concatenate x1, other arithmetic: 0.89 us -> 0.01 us  [per_device(): gathered = jnp.concatenate([gathered, other], axis=0)]
    unnamed x21 -> x23, local copies, waits for them, and re-layouts: 2.18 us -> 2.25 us
  transfers between devices with their start and end apart: 9 -> 9, of which waited for: 6 -> 6; matrix products, arithmetic and copies ran while one was open for 2% -> 0% of each run, Pallas kernels for 0% -> 0%
where the time goes in v3:
time: 46.8 us; the launch traced here: 46.5 us
  waiting for transfers between devices  18.1 us (39%)
  starting transfers between devices  16.6 us (35%)
  Pallas kernels  8.78 us (19%)
  local copies, waits for them, and re-layouts  2.26 us (5%)
  between operations  0.8 us (2%)
    ppermute x5, waiting for transfers between devices, swap(): return lax.ppermute(value, axis, [*pairs, *((b, a) for a, b in pairs)])  9.34 us
    ppermute x5, starting transfers between devices, swap(): return lax.ppermute(value, axis, [*pairs, *((b, a) for a, b in pairs)])  9.13 us
    pallas_call x1, Pallas kernels, per_device(): pl.pallas_call(functools.partial(basis_kernel, counts, present), out_shap...  7.59 us
    all_to_all x1, waiting for transfers between devices, per_device(): shared = lax.all_to_all(info, ('height', 'plane'), 0, 0, tiled=True)  7.3 us
    all_to_all x1, starting transfers between devices, per_device(): shared = lax.all_to_all(info, ('height', 'plane'), 0, 0, tiled=True)  6.86 us
    unnamed x23, local copies, waits for them, and re-layouts  2.25 us
    ppermute x3, waiting for transfers between devices, per_device(): lax.ppermute(sent[name], 'height', [(h, (h + turn) % height) for h in ran...  1.44 us
    pallas_call x1, Pallas kernels, per_device(): pl.pallas_call(combine_kernel, out_shape=(jax.ShapeDtypeStruct(cotangent....  1.05 us
  transfers between devices with their start and end apart: 9, of which 6 were waited for; matrix products, arithmetic and copies ran while one was open for 0% of the time, Pallas kernels for 0%

profile of v3, /device:TPU:0, one launch (start us, length us, event | category | flops | bytes accessed | tf_op | source)
XLA Modules:
  0.0 46.5 jit_solution(3537437923734224150)
XLA Ops:
  0.6 0.8 %copy-done.2 = f32[16,8,128]{2,1,0:T(8,128)S(1)} copy-done((f32[16,8,128]{2,1,0:T(8,128)S(1)}, f32[16,8,128]{2,1,0:T(8,128)}, u32[]{:S(2)}) %copy-start.2) | copy-done | bytes 65560
  1.5 0.7 %copy-done.7 = f32[2,1,16]{2,1,0:T(1,128)S(1)} copy-done((f32[2,1,16]{2,1,0:T(1,128)S(1)}, f32[2,1,16]{2,1,0:T(1,128)}, u32[]{:S(2)}) %copy-start.7) | copy-done | bytes 152
  2.2 0.7 %copy-done.8 = f32[2,1,16]{2,1,0:T(1,128)S(1)} copy-done((f32[2,1,16]{2,1,0:T(1,128)S(1)}, f32[2,1,16]{2,1,0:T(1,128)}, u32[]{:S(2)}) %copy-start.8) | copy-done | bytes 152
  2.8 0.1 shard_map.121
  3.0 2.9 %collective-permute-start = (f32[136,128]{1,0:T(8,128)S(1)}, f32[136,128]{1,0:T(8,128)S(1)}, u32[]{:S(2)}, u32[]{:S(2)}) collective-permute-start(f32[136,128]{1,0:T(8,128)S(1)} %get-tuple-element.7), channel_id=1, source_target_pairs={{0,1},{2,3},{4,5},{6,7},{8,9},{10,11},{12,13},{14,15},{1,0},{3,2},... | collective-permute-start | bytes 208904 | tf_op jit(solution)/shard_map/ppermute | solution.py:67
  5.9 0.7 %collective-permute-start.2 = (f32[24,128]{1,0:T(8,128)S(1)}, f32[24,128]{1,0:T(8,128)S(1)}, u32[]{:S(2)}, u32[]{:S(2)}) collective-permute-start(f32[24,128]{1,0:T(8,128)S(1)} %get-tuple-element.8), channel_id=1, source_target_pairs={{3,4},{7,8},{11,12},{4,3},{8,7},{12,11},{19,20},{23,24},{27,28},{2... | collective-permute-start | bytes 36872 | tf_op jit(solution)/shard_map/ppermute | solution.py:67
  6.6 1.6 %collective-permute-done = f32[136,128]{1,0:T(8,128)S(1)} collective-permute-done((f32[136,128]{1,0:T(8,128)S(1)}, f32[136,128]{1,0:T(8,128)S(1)}, u32[]{:S(2)}, u32[]{:S(2)}) %collective-permute-start) | collective-permute-done | bytes 69664 | tf_op jit(solution)/shard_map/ppermute | solution.py:67
  8.2 2.1 %collective-permute-start.1 = (f32[272,128]{1,0:T(8,128)S(1)}, f32[272,128]{1,0:T(8,128)S(1)}, u32[]{:S(2)}, u32[]{:S(2)}) collective-permute-start(f32[272,128]{1,0:T(8,128)S(1)} %pad_maximum_fusion), channel_id=1, source_target_pairs={{0,2},{1,3},{4,6},{5,7},{8,10},{9,11},{12,14},{13,15},{2,0},{3,1},... | collective-permute-start | bytes 417800 | tf_op jit(solution)/shard_map/ppermute | solution.py:67
  10.4 0.0 copy-start.5
  10.4 0.0 copy-start
  10.4 0.0 copy-start.1
  10.4 3.0 %collective-permute-done.1 = f32[272,128]{1,0:T(8,128)S(1)} collective-permute-done((f32[272,128]{1,0:T(8,128)S(1)}, f32[272,128]{1,0:T(8,128)S(1)}, u32[]{:S(2)}, u32[]{:S(2)}) %collective-permute-start.1) | collective-permute-done | bytes 139296 | tf_op jit(solution)/shard_map/ppermute | solution.py:67
  13.4 0.0 copy-start.6
  13.4 2.8 %collective-permute-start.3 = (f32[568,128]{1,0:T(8,128)S(1)}, f32[568,128]{1,0:T(8,128)S(1)}, u32[]{:S(2)}, u32[]{:S(2)}) collective-permute-start(f32[568,128]{1,0:T(8,128)S(1)} %constant_dynamic-update-slice_fusion.refs_0_), channel_id=1, source_target_pairs={{0,4},{1,5},{2,6},{3,7},{8,12},{9,13},{10,14},{11,15},{4,0},{5,1},... | collective-permute-start | bytes 872456 | tf_op jit(solution)/shard_map/ppermute | solution.py:67
  16.2 0.7 %collective-permute-start.4 = (f32[568,128]{1,0:T(8,128)S(1)}, f32[568,128]{1,0:T(8,128)S(1)}, u32[]{:S(2)}, u32[]{:S(2)}) collective-permute-start(f32[568,128]{1,0:T(8,128)S(1)} %constant_dynamic-update-slice_fusion.refs_0_), channel_id=1, source_target_pairs={{4,8},{5,9},{6,10},{7,11},{8,4},{9,5},{10,6},{11,7},{20,24},{21,25... | collective-permute-start | bytes 872456 | tf_op jit(solution)/shard_map/ppermute | solution.py:67
  16.8 0.1 collective-permute-start.5
  16.9 4.8 %collective-permute-done.3.refs_1_ = f32[568,128]{1,0:T(8,128)S(1)} collective-permute-done((f32[568,128]{1,0:T(8,128)S(1)}, f32[568,128]{1,0:T(8,128)S(1)}, u32[]{:S(2)}, u32[]{:S(2)}) %collective-permute-start.3) | collective-permute-done | bytes 290848 | tf_op jit(solution)/shard_map/ppermute | solution.py:67
  21.7 0.5 %collective-permute-start.7 = (f32[568,128]{1,0:T(8,128)S(1)}, f32[568,128]{1,0:T(8,128)S(1)}, u32[]{:S(2)}, u32[]{:S(2)}) collective-permute-start(f32[568,128]{1,0:T(8,128)S(1)} %collective-permute-done.4.refs_2_), channel_id=1, source_target_pairs={{0,16},{16,0},{1,17},{17,1},{2,18},{18,2},{3,19},{19,3},{4,20},{20... | collective-permute-start | bytes 872456 | tf_op jit(solution)/shard_map/ppermute | solution.py:518
  22.2 1.0 %collective-permute-done.6.refs_4_ = f32[568,128]{1,0:T(8,128)S(1)} collective-permute-done((f32[568,128]{1,0:T(8,128)S(1)}, f32[568,128]{1,0:T(8,128)S(1)}, u32[]{:S(2)}, u32[]{:S(2)}) %collective-permute-start.6) | collective-permute-done | bytes 290848 | tf_op jit(solution)/shard_map/ppermute | solution.py:518
  23.3 0.4 collective-permute-done.7.refs_5_
  23.7 7.6 %shard_map.122 = (f32[12,128,128]{2,1,0:T(8,128)S(1)}, f32[32,4,128]{2,1,0:T(4,128)}) custom-call(f32[568,128]{1,0:T(8,128)S(1)} %constant_dynamic-update-slice_fusion.refs_0_, f32[568,128]{1,0:T(8,128)S(1)} %collective-permute-done.3.refs_1_, f32[568,128]{1,0:T(8,128)S(1)} %collective-permute-done.4.refs_2_, f32[568,128]{1,0:T(8,128)S(1)} %collective-permute-done.5.refs_3_, ...), custom_call_target="tpu_custom_call" | custom-call | tf_op jit(solution)/shard_map/pallas_call | solution.py:524
  31.3 6.9 %all-to-all-start = ((f32[32,4,128]{2,1,0:T(4,128)}), f32[32,4,128]{2,1,0:T(4,128)S(1)}, u32[]{:S(2)}, u32[]{:S(2)}) async-start(f32[32,4,128]{2,1,0:T(4,128)} %get-tuple-element.9), calls=%async_computation | async-start | bytes 131072 | tf_op jit(solution)/shard_map/all_to_all | solution.py:538
  38.2 7.3 %all-to-all-done.info_ref = f32[32,4,128]{2,1,0:T(4,128)S(1)} async-done(((f32[32,4,128]{2,1,0:T(4,128)}), f32[32,4,128]{2,1,0:T(4,128)S(1)}, u32[]{:S(2)}, u32[]{:S(2)}) %all-to-all-start) | async-done | bytes 65568 | tf_op jit(solution)/shard_map/all_to_all | solution.py:538
  45.5 1.0 %shard_map.123 = (f32[16,8,128]{2,1,0:T(8,128)}, f32[16,8,128]{2,1,0:T(8,128)}, f32[2,128]{1,0:T(2,128)}) custom-call(f32[32,4,128]{2,1,0:T(4,128)S(1)} %all-to-all-done.info_ref, f32[12,128,128]{2,1,0:T(8,128)S(1)} %get-tuple-element.10.fields_ref, s32[2,128]{1,0:T(2,128)S(1)} %fusion.owner_ref, s32[2,128]{1,0:T(2,128)S(1)} %get-tuple-element.11.place_ref), custom_call_target="tpu_custom_call" | custom-call | tf_op jit(solution)/shard_map/pallas_call | solution.py:546
  (24 shorter events, 0.1 us)
Async XLA Ops:
  0.6 0.8 %copy-start.2 = (f32[16,8,128]{2,1,0:T(8,128)S(1)}, f32[16,8,128]{2,1,0:T(8,128)}, u32[]{:S(2)}) copy-start(f32[16,8,128]{2,1,0:T(8,128)} %cot_ref.1) | copy-start | bytes 196612
  1.5 0.7 %copy-start.7 = (f32[2,1,16]{2,1,0:T(1,128)S(1)}, f32[2,1,16]{2,1,0:T(1,128)}, u32[]{:S(2)}) copy-start(f32[2,1,16]{2,1,0:T(1,128)} %kap_ref.1) | copy-start | bytes 388
  2.2 0.7 %copy-start.8 = (f32[2,1,16]{2,1,0:T(1,128)S(1)}, f32[2,1,16]{2,1,0:T(1,128)}, u32[]{:S(2)}) copy-start(f32[2,1,16]{2,1,0:T(1,128)} %cap_ref.1) | copy-start | bytes 388
  3.0 5.2 %collective-permute-start = (f32[136,128]{1,0:T(8,128)S(1)}, f32[136,128]{1,0:T(8,128)S(1)}, u32[]{:S(2)}, u32[]{:S(2)}) collective-permute-start(f32[136,128]{1,0:T(8,128)S(1)} %get-tuple-element.7), channel_id=1, source_target_pairs={{0,1},{2,3},{4,5},{6,7},{8,9},{10,11},{12,13},{14,15},{1,0},{3,2},... | collective-permute-start | bytes 208904 | tf_op jit(solution)/shard_map/ppermute | solution.py:67
  5.9 7.5 %collective-permute-start.2 = (f32[24,128]{1,0:T(8,128)S(1)}, f32[24,128]{1,0:T(8,128)S(1)}, u32[]{:S(2)}, u32[]{:S(2)}) collective-permute-start(f32[24,128]{1,0:T(8,128)S(1)} %get-tuple-element.8), channel_id=1, source_target_pairs={{3,4},{7,8},{11,12},{4,3},{8,7},{12,11},{19,20},{23,24},{27,28},{2... | collective-permute-start | bytes 36872 | tf_op jit(solution)/shard_map/ppermute | solution.py:67
  8.2 5.2 %collective-permute-start.1 = (f32[272,128]{1,0:T(8,128)S(1)}, f32[272,128]{1,0:T(8,128)S(1)}, u32[]{:S(2)}, u32[]{:S(2)}) collective-permute-start(f32[272,128]{1,0:T(8,128)S(1)} %pad_maximum_fusion), channel_id=1, source_target_pairs={{0,2},{1,3},{4,6},{5,7},{8,10},{9,11},{12,14},{13,15},{2,0},{3,1},... | collective-permute-start | bytes 417800 | tf_op jit(solution)/shard_map/ppermute | solution.py:67
  10.3 11.9 %copy-start.9 = (s32[2,128]{1,0:T(2,128)S(1)}, s32[2,128]{1,0:T(2,128)}, u32[]{:S(2)}) copy-start(s32[2,128]{1,0:T(2,128)} %param.13) | copy-start | bytes 3076
  10.3 13.3 %copy-start.3 = (bf16[64,320]{1,0:T(8,128)(2,1)S(1)}, bf16[64,320]{1,0:T(8,128)(2,1)}, u32[]{:S(2)}) copy-start(bf16[64,320]{1,0:T(8,128)(2,1)} %constant.71.clone.refs_6_) | copy-start | bytes 122884
  10.4 13.3 %copy-start.5 = (f32[8,8,128]{2,1,0:T(8,128)S(1)}, f32[8,8,128]{2,1,0:T(8,128)}, u32[]{:S(2)}) copy-start(f32[8,8,128]{2,1,0:T(8,128)} %constant.76.clone.refs_11_) | copy-start | bytes 98308
  10.4 13.3 %copy-start = (bf16[256,256]{1,0:T(8,128)(2,1)S(1)}, bf16[256,256]{1,0:T(8,128)(2,1)}, u32[]{:S(2)}) copy-start(bf16[256,256]{1,0:T(8,128)(2,1)} %constant.73.clone.refs_8_) | copy-start | bytes 393220
  10.4 13.3 %copy-start.1 = (bf16[256,256]{1,0:T(8,128)(2,1)S(1)}, bf16[256,256]{1,0:T(8,128)(2,1)}, u32[]{:S(2)}) copy-start(bf16[256,256]{1,0:T(8,128)(2,1)} %constant.74.clone.refs_9_) | copy-start | bytes 393220
  13.4 10.3 %copy-start.4 = (f32[8,8,128]{2,1,0:T(8,128)S(1)}, f32[8,8,128]{2,1,0:T(8,128)}, u32[]{:S(2)}) copy-start(f32[8,8,128]{2,1,0:T(8,128)} %constant.75.clone.refs_10_) | copy-start | bytes 98308
  13.4 10.3 %copy-start.6 = (bf16[16,320]{1,0:T(8,128)(2,1)S(1)}, bf16[16,320]{1,0:T(8,128)(2,1)}, u32[]{:S(2)}) copy-start(bf16[16,320]{1,0:T(8,128)(2,1)} %constant.72.clone.refs_7_) | copy-start | bytes 30724
  13.4 8.3 %collective-permute-start.3 = (f32[568,128]{1,0:T(8,128)S(1)}, f32[568,128]{1,0:T(8,128)S(1)}, u32[]{:S(2)}, u32[]{:S(2)}) collective-permute-start(f32[568,128]{1,0:T(8,128)S(1)} %constant_dynamic-update-slice_fusion.refs_0_), channel_id=1, source_target_pairs={{0,4},{1,5},{2,6},{3,7},{8,12},{9,13},{10,14},{11,15},{4,0},{5,1},... | collective-permute-start | bytes 872456 | tf_op jit(solution)/shard_map/ppermute | solution.py:67
  16.2 5.5 %collective-permute-start.4 = (f32[568,128]{1,0:T(8,128)S(1)}, f32[568,128]{1,0:T(8,128)S(1)}, u32[]{:S(2)}, u32[]{:S(2)}) collective-permute-start(f32[568,128]{1,0:T(8,128)S(1)} %constant_dynamic-update-slice_fusion.refs_0_), channel_id=1, source_target_pairs={{4,8},{5,9},{6,10},{7,11},{8,4},{9,5},{10,6},{11,7},{20,24},{21,25... | collective-permute-start | bytes 872456 | tf_op jit(solution)/shard_map/ppermute | solution.py:67
  16.8 5.4 %collective-permute-start.5 = (f32[568,128]{1,0:T(8,128)S(1)}, f32[568,128]{1,0:T(8,128)S(1)}, u32[]{:S(2)}, u32[]{:S(2)}) collective-permute-start(f32[568,128]{1,0:T(8,128)S(1)} %constant_dynamic-update-slice_fusion.refs_0_), channel_id=1, source_target_pairs={{0,16},{16,0},{1,17},{17,1},{2,18},{18,2},{3,19},{19,3},{4,20},{20... | collective-permute-start | bytes 872456 | tf_op jit(solution)/shard_map/ppermute | solution.py:518
  21.7 1.6 %collective-permute-start.6 = (f32[568,128]{1,0:T(8,128)S(1)}, f32[568,128]{1,0:T(8,128)S(1)}, u32[]{:S(2)}, u32[]{:S(2)}) collective-permute-start(f32[568,128]{1,0:T(8,128)S(1)} %collective-permute-done.3.refs_1_), channel_id=1, source_target_pairs={{0,16},{16,0},{1,17},{17,1},{2,18},{18,2},{3,19},{19,3},{4,20},{20... | collective-permute-start | bytes 872456 | tf_op jit(solution)/shard_map/ppermute | solution.py:518
  21.7 2.0 %collective-permute-start.7 = (f32[568,128]{1,0:T(8,128)S(1)}, f32[568,128]{1,0:T(8,128)S(1)}, u32[]{:S(2)}, u32[]{:S(2)}) collective-permute-start(f32[568,128]{1,0:T(8,128)S(1)} %collective-permute-done.4.refs_2_), channel_id=1, source_target_pairs={{0,16},{16,0},{1,17},{17,1},{2,18},{18,2},{3,19},{19,3},{4,20},{20... | collective-permute-start | bytes 872456 | tf_op jit(solution)/shard_map/ppermute | solution.py:518
  31.3 14.2 %all-to-all-start = ((f32[32,4,128]{2,1,0:T(4,128)}), f32[32,4,128]{2,1,0:T(4,128)S(1)}, u32[]{:S(2)}, u32[]{:S(2)}) async-start(f32[32,4,128]{2,1,0:T(4,128)} %get-tuple-element.9), calls=%async_computation | async-start | bytes 131072 | tf_op jit(solution)/shard_map/all_to_all | solution.py:538

commit v4 on v3

--- a/solution.py
+++ b/solution.py
@@ -13,7 +13,6 @@
 SHIFTS = (0.5, 1.5)
 GROUP = 4
 REACH = 4
-TERMS = ((0, 0), (0, 1), (1, 0), (1, 1), (2, 0))
 PAIRS = ((0, 0), (0, 1), (0, 2), (1, 1), (1, 2), (2, 2))
 TINY = 1e-30
 HIGHEST = lax.Precision.HIGHEST
@@ -48,8 +47,8 @@
     line = (derivative.T * weights) @ derivative / weights[:, None]
     eye = np.eye(8)
     face = pieces(np.kron(line, eye) + np.kron(eye, line))
-    face_mat = np.concatenate([face[m] for m, _ in TERMS], axis=1)
-    ends_mat = np.concatenate([face_mat[0::8], face_mat[7::8]], axis=0)
+    face_mat = np.concatenate([np.concatenate([piece, piece], axis=1) for piece in face], axis=0)
+    ends_mat = np.concatenate([np.concatenate([p[0::8], p[7::8]], axis=0) for p in np.split(face_mat, 3)], axis=0)
     row = pieces(np.kron(np.eye(span // 8), line.T))
     row_a = np.concatenate([np.concatenate([row[0], row[1]], 1)] * 2, axis=0)
     none = np.zeros_like(row[2])
@@ -71,19 +70,60 @@
     return -(-(2 * elems) // 8) * 8
 
 
-def pack_kernel(cot_ref, kap_ref, cap_ref, out_ref, edge_ref):
+def seams(span):
+    lane = lax.broadcasted_iota(jnp.int32, (8, span), 1)
+    return (lane % 8 == 0) & (lane > 0), (lane % 8 == 7) & (lane < span - 1)
+
+
+def tall(mask, like):
+    return jnp.concatenate([mask] * (like.shape[0] // 8), axis=0) if like.shape[0] > 8 else mask
+
+
+def join_span(values):
+    span = values.shape[1]
+    opens, closes = seams(span)
+    up, down = pltpu.roll(values, 1, 1), pltpu.roll(values, span - 1, 1)
+    return values + jnp.where(tall(opens, values), up, jnp.where(tall(closes, values), down, 0.0))
+
+
+def join_depth(values):
+    planes = []
+    layers = values.shape[0] // 64
+    for elem in range(layers):
+        top = elem * 64
+        first, last = values[top : top + 8], values[top + 56 : top + 64]
+        if elem > 0:
+            first = first + values[top - 8 : top]
+        if elem < layers - 1:
+            last = last + values[top + 64 : top + 72]
+        planes += [first, values[top + 8 : top + 56], last]
+    return jnp.concatenate(planes, axis=0)
+
+
+def pack_kernel(cot_hbm, kap_hbm, cap_hbm, out_ref, edge_ref, cot_ref, kap_ref, cap_ref, sems):
+    loads = [
+        pltpu.make_async_copy(src, dst, sems.at[i])
+        for i, (src, dst) in enumerate(((cot_hbm, cot_ref), (kap_hbm, kap_ref), (cap_hbm, cap_ref)))
+    ]
+    for load in loads:
+        load.start()
+    for load in loads:
+        load.wait()
     depth, _, span = cot_ref.shape
     elems, _, parts = kap_ref.shape
-    out_ref[: depth * 8, :] = cot_ref[...].reshape(depth * 8, span)
     spread = (lax.broadcasted_iota(jnp.int32, (parts, span), 1) // 8 == lax.broadcasted_iota(jnp.int32, (parts, span), 0)).astype(F32)
     coef = jnp.concatenate([kap_ref[...].reshape(elems, parts) * (1.0 / INV_STEP), cap_ref[...].reshape(elems, parts)], axis=0)
     rows = coef_rows(elems)
     if rows > 2 * elems:
         coef = jnp.concatenate([coef, jnp.zeros((rows - 2 * elems, parts), F32)], axis=0)
     coef = jnp.dot(coef, spread, precision=HIGHEST, preferred_element_type=F32)
+    heavy = jnp.concatenate([jnp.broadcast_to(coef[elems + e : elems + e + 1], (64, span)) for e in range(elems)], axis=0)
+    value = join_depth(join_span(heavy * cot_ref[...].reshape(depth * 8, span)))
+    out_ref[: depth * 8, :] = value
     out_ref[depth * 8 :, :] = coef
     last = lax.rem(lax.axis_index("plane"), GROUP) == GROUP - 1
-    edge_ref[:depth, :] = jnp.where(last, cot_ref[:, 7, :], cot_ref[:, 0, :])
+    faces = [value.reshape(depth, 8, span)[:, node, :] for node in (0, 7)]
+    edge_ref[:depth, :] = jnp.where(last, faces[1], faces[0])
     edge_ref[depth:, :] = coef
 
 
@@ -122,30 +162,8 @@
     lay = Layout(whole)
     wide = lay.wide
 
-    lane = lax.broadcasted_iota(jnp.int32, (8, span), 1)
     sub = lax.broadcasted_iota(jnp.int32, (8, span), 0)
-    opens = (lane % 8 == 0) & (lane > 0)
-    closes = (lane % 8 == 7) & (lane < span - 1)
-
-    def tall(mask, like):
-        return jnp.concatenate([mask] * (like.shape[0] // 8), axis=0) if like.shape[0] > 8 else mask
-
-    def join_span(values):
-        up, down = pltpu.roll(values, 1, 1), pltpu.roll(values, span - 1, 1)
-        return values + jnp.where(tall(opens, values), up, jnp.where(tall(closes, values), down, 0.0))
-
-    def join_depth(values):
-        planes = []
-        layers = values.shape[0] // 64
-        for elem in range(layers):
-            top = elem * 64
-            first, last = values[top : top + 8], values[top + 56 : top + 64]
-            if elem > 0:
-                first = first + values[top - 8 : top]
-            if elem < layers - 1:
-                last = last + values[top + 64 : top + 72]
-            planes += [first, values[top + 8 : top + 56], last]
-        return jnp.concatenate(planes, axis=0)
+    opens, closes = seams(span)
 
     def stage_coef(msg, top, slot, block):
         for kind in range(2):
@@ -153,22 +171,16 @@
                 at = top + kind * own_elems + elem
                 coef[slot, kind, block * own_elems + elem] = jnp.broadcast_to(msg[at : at + 1, :], (8, span))
 
-    def caps(msg, top):
-        return [jnp.broadcast_to(msg[at : at + 1, :], (8, span)) for at in range(top + own_elems, top + 2 * own_elems)]
-
     def stage(msg, piece, slot, block):
         top = piece * slab_rows
-        heavy = jnp.concatenate([c for c in caps(msg, top + own_rows) for _ in range(8)], axis=0)
-        value = join_depth(join_span(heavy * msg[top : top + own_rows, :]))
-        raw[slot, pl.ds(pl.multiple_of(block * own_rows, own_rows), own_rows)] = value
+        raw[slot, pl.ds(pl.multiple_of(block * own_rows, own_rows), own_rows)] = msg[top : top + own_rows, :]
         stage_coef(msg, top + own_rows, slot, block)
 
     def stage_face(msg, slot, block):
         top = GROUP * slab_rows
-        heavy = jnp.concatenate(caps(msg, top + own_depth), axis=0)
-        face = join_span(heavy * msg[top : top + own_depth, :])
-        value = join_depth(jnp.concatenate([jnp.broadcast_to(face[z : z + 1], (8, span)) for z in range(own_depth)], axis=0))
-        raw[slot, pl.ds(pl.multiple_of(block * own_rows, own_rows), own_rows)] = value
+        face = msg[top : top + own_depth, :]
+        spread = jnp.concatenate([jnp.broadcast_to(face[z : z + 1], (8, span)) for z in range(own_depth)], axis=0)
+        raw[slot, pl.ds(pl.multiple_of(block * own_rows, own_rows), own_rows)] = spread
         stage_coef(msg, top + own_depth, slot, block)
 
     def sides(name):
@@ -227,8 +239,10 @@
 
     def along_face(matrix, halves, elem):
         top = elem * 64
-        stacks = [jnp.concatenate([h[f][top : top + 64] for _, f in TERMS], axis=0) for h in halves]
-        return jnp.dot(matrix, stacks[0] if len(stacks) == 1 else jnp.concatenate(stacks, axis=1), preferred_element_type=F32)
+        stacks = [jnp.concatenate([piece[top : top + 64] for piece in h], axis=0) for h in halves]
+        made = jnp.dot(matrix, stacks[0] if len(stacks) == 1 else jnp.concatenate(stacks, axis=1), preferred_element_type=F32)
+        count = made.shape[0] // 3
+        return made[:count] + (made[count : 2 * count] + made[2 * count :])
 
     def scaled(slot, kind, elem, scale):
         value = coef[slot, kind, elem]
@@ -400,7 +414,7 @@
     lines.append(jnp.zeros((span - len(lines), span), F32))
     sums = lax.dot_general(jnp.ones((8, span), F32), jnp.concatenate(lines, axis=0), (((1,), (1,)), ((), ())), precision=HIGHEST, preferred_element_type=F32)
 
-    heavy = jnp.concatenate([tall(coef[slot, 1, start + elem], face_ref) for elem in range(own_elems)], axis=0) * (omega * 0.125)
+    heavy = jnp.concatenate([jnp.concatenate([coef[slot, 1, start + elem]] * 8, axis=0) for elem in range(own_elems)], axis=0) * (omega * 0.125)
     rows_of = []
     for index in range(12):
         mass = heavy * fields_ref[index]
@@ -494,8 +508,9 @@
     message, edge = pl.pallas_call(
         pack_kernel,
         out_shape=(jax.ShapeDtypeStruct((rows, span), F32), jax.ShapeDtypeStruct((depth + coef_rows(elems), span), F32)),
-        in_specs=[vmem] * 3,
+        in_specs=[pl.BlockSpec(memory_space=pl.ANY)] * 3,
         out_specs=(vmem, vmem),
+        scratch_shapes=[pltpu.VMEM(arr.shape, F32) for arr in (cotangent, conductivity, capacity)] + [pltpu.SemaphoreType.DMA((3,))],
         compiler_params=pltpu.CompilerParams(vmem_limit_bytes=4 * 2**20),
     )(cotangent, conductivity, capacity)
 

time: 46.8 us -> 46 us (0.983)
  Pallas kernels: 8.78 us -> 7.86 us
    pallas_call x1, Pallas kernels: 7.59 us -> 6.48 us  [per_device(): pl.pallas_call(functools.partial(basis_kernel, counts, present), out_shap...]
where the time goes in v4:
time: 46 us; the launch traced here: 45.7 us
  waiting for transfers between devices  18.1 us (39%)
  starting transfers between devices  16.6 us (36%)
  Pallas kernels  7.86 us (17%)
  local copies, waits for them, and re-layouts  2.26 us (5%)
  between operations  0.8 us (2%)
    ppermute x5, waiting for transfers between devices, swap(): return lax.ppermute(value, axis, [*pairs, *((b, a) for a, b in pairs)])  9.35 us
    ppermute x5, starting transfers between devices, swap(): return lax.ppermute(value, axis, [*pairs, *((b, a) for a, b in pairs)])  9.19 us
    all_to_all x1, waiting for transfers between devices, per_device(): shared = lax.all_to_all(info, ('height', 'plane'), 0, 0, tiled=True)  7.3 us
    all_to_all x1, starting transfers between devices, per_device(): shared = lax.all_to_all(info, ('height', 'plane'), 0, 0, tiled=True)  6.87 us
    pallas_call x1, Pallas kernels, per_device(): pl.pallas_call(functools.partial(basis_kernel, counts, present), out_shap...  6.48 us
    unnamed x23, local copies, waits for them, and re-layouts  2.25 us
    ppermute x3, waiting for transfers between devices, per_device(): lax.ppermute(sent[name], 'height', [(h, (h + turn) % height) for h in ran...  1.44 us
    pallas_call x1, Pallas kernels, per_device(): pl.pallas_call(combine_kernel, out_shape=(jax.ShapeDtypeStruct(cotangent....  1.05 us
  transfers between devices with their start and end apart: 9, of which 6 were waited for; matrix products, arithmetic and copies ran while one was open for 0% of the time, Pallas kernels for 0%

profile of v4, /device:TPU:0, one launch (start us, length us, event | category | flops | bytes accessed | tf_op | source)
XLA Modules:
  0.0 45.7 jit_solution(18430344247980093606)
XLA Ops:
  0.6 0.8 %copy-done.2 = f32[16,8,128]{2,1,0:T(8,128)S(1)} copy-done((f32[16,8,128]{2,1,0:T(8,128)S(1)}, f32[16,8,128]{2,1,0:T(8,128)}, u32[]{:S(2)}) %copy-start.2) | copy-done | bytes 65560
  1.5 0.7 %copy-done.7 = f32[2,1,16]{2,1,0:T(1,128)S(1)} copy-done((f32[2,1,16]{2,1,0:T(1,128)S(1)}, f32[2,1,16]{2,1,0:T(1,128)}, u32[]{:S(2)}) %copy-start.7) | copy-done | bytes 152
  2.2 0.7 %copy-done.8 = f32[2,1,16]{2,1,0:T(1,128)S(1)} copy-done((f32[2,1,16]{2,1,0:T(1,128)S(1)}, f32[2,1,16]{2,1,0:T(1,128)}, u32[]{:S(2)}) %copy-start.8) | copy-done | bytes 152
  2.8 0.3 shard_map.121
  3.2 3.0 %collective-permute-start = (f32[136,128]{1,0:T(8,128)S(1)}, f32[136,128]{1,0:T(8,128)S(1)}, u32[]{:S(2)}, u32[]{:S(2)}) collective-permute-start(f32[136,128]{1,0:T(8,128)S(1)} %get-tuple-element.7), channel_id=1, source_target_pairs={{0,1},{2,3},{4,5},{6,7},{8,9},{10,11},{12,13},{14,15},{1,0},{3,2},... | collective-permute-start | bytes 208904 | tf_op jit(solution)/shard_map/ppermute | solution.py:66
  6.2 0.7 %collective-permute-start.2 = (f32[24,128]{1,0:T(8,128)S(1)}, f32[24,128]{1,0:T(8,128)S(1)}, u32[]{:S(2)}, u32[]{:S(2)}) collective-permute-start(f32[24,128]{1,0:T(8,128)S(1)} %get-tuple-element.8), channel_id=1, source_target_pairs={{3,4},{7,8},{11,12},{4,3},{8,7},{12,11},{19,20},{23,24},{27,28},{2... | collective-permute-start | bytes 36872 | tf_op jit(solution)/shard_map/ppermute | solution.py:66
  6.8 1.6 %collective-permute-done = f32[136,128]{1,0:T(8,128)S(1)} collective-permute-done((f32[136,128]{1,0:T(8,128)S(1)}, f32[136,128]{1,0:T(8,128)S(1)}, u32[]{:S(2)}, u32[]{:S(2)}) %collective-permute-start) | collective-permute-done | bytes 69664 | tf_op jit(solution)/shard_map/ppermute | solution.py:66
  8.5 2.1 %collective-permute-start.1 = (f32[272,128]{1,0:T(8,128)S(1)}, f32[272,128]{1,0:T(8,128)S(1)}, u32[]{:S(2)}, u32[]{:S(2)}) collective-permute-start(f32[272,128]{1,0:T(8,128)S(1)} %pad_maximum_fusion), channel_id=1, source_target_pairs={{0,2},{1,3},{4,6},{5,7},{8,10},{9,11},{12,14},{13,15},{2,0},{3,1},... | collective-permute-start | bytes 417800 | tf_op jit(solution)/shard_map/ppermute | solution.py:66
  10.6 0.0 copy-start.3
  10.6 0.0 copy-start.5
  10.7 0.0 copy-start.1
  10.7 3.0 %collective-permute-done.1 = f32[272,128]{1,0:T(8,128)S(1)} collective-permute-done((f32[272,128]{1,0:T(8,128)S(1)}, f32[272,128]{1,0:T(8,128)S(1)}, u32[]{:S(2)}, u32[]{:S(2)}) %collective-permute-start.1) | collective-permute-done | bytes 139296 | tf_op jit(solution)/shard_map/ppermute | solution.py:66
  13.6 0.0 copy-start.6
  13.7 2.8 %collective-permute-start.3 = (f32[568,128]{1,0:T(8,128)S(1)}, f32[568,128]{1,0:T(8,128)S(1)}, u32[]{:S(2)}, u32[]{:S(2)}) collective-permute-start(f32[568,128]{1,0:T(8,128)S(1)} %constant_dynamic-update-slice_fusion.refs_0_), channel_id=1, source_target_pairs={{0,4},{1,5},{2,6},{3,7},{8,12},{9,13},{10,14},{11,15},{4,0},{5,1},... | collective-permute-start | bytes 872456 | tf_op jit(solution)/shard_map/ppermute | solution.py:66
  16.4 0.7 %collective-permute-start.4 = (f32[568,128]{1,0:T(8,128)S(1)}, f32[568,128]{1,0:T(8,128)S(1)}, u32[]{:S(2)}, u32[]{:S(2)}) collective-permute-start(f32[568,128]{1,0:T(8,128)S(1)} %constant_dynamic-update-slice_fusion.refs_0_), channel_id=1, source_target_pairs={{4,8},{5,9},{6,10},{7,11},{8,4},{9,5},{10,6},{11,7},{20,24},{21,25... | collective-permute-start | bytes 872456 | tf_op jit(solution)/shard_map/ppermute | solution.py:66
  17.1 0.1 collective-permute-start.5
  17.2 4.8 %collective-permute-done.3.refs_1_ = f32[568,128]{1,0:T(8,128)S(1)} collective-permute-done((f32[568,128]{1,0:T(8,128)S(1)}, f32[568,128]{1,0:T(8,128)S(1)}, u32[]{:S(2)}, u32[]{:S(2)}) %collective-permute-start.3) | collective-permute-done | bytes 290848 | tf_op jit(solution)/shard_map/ppermute | solution.py:66
  21.9 0.5 %collective-permute-start.7 = (f32[568,128]{1,0:T(8,128)S(1)}, f32[568,128]{1,0:T(8,128)S(1)}, u32[]{:S(2)}, u32[]{:S(2)}) collective-permute-start(f32[568,128]{1,0:T(8,128)S(1)} %collective-permute-done.4.refs_2_), channel_id=1, source_target_pairs={{0,16},{16,0},{1,17},{17,1},{2,18},{18,2},{3,19},{19,3},{4,20},{20... | collective-permute-start | bytes 872456 | tf_op jit(solution)/shard_map/ppermute | solution.py:533
  22.5 1.0 %collective-permute-done.6.refs_4_ = f32[568,128]{1,0:T(8,128)S(1)} collective-permute-done((f32[568,128]{1,0:T(8,128)S(1)}, f32[568,128]{1,0:T(8,128)S(1)}, u32[]{:S(2)}, u32[]{:S(2)}) %collective-permute-start.6) | collective-permute-done | bytes 290848 | tf_op jit(solution)/shard_map/ppermute | solution.py:533
  23.5 0.4 collective-permute-done.7.refs_5_
  24.0 6.5 %shard_map.122 = (f32[12,128,128]{2,1,0:T(8,128)S(1)}, f32[32,4,128]{2,1,0:T(4,128)}) custom-call(f32[568,128]{1,0:T(8,128)S(1)} %constant_dynamic-update-slice_fusion.refs_0_, f32[568,128]{1,0:T(8,128)S(1)} %collective-permute-done.3.refs_1_, f32[568,128]{1,0:T(8,128)S(1)} %collective-permute-done.4.refs_2_, f32[568,128]{1,0:T(8,128)S(1)} %collective-permute-done.5.refs_3_, ...), custom_call_target="tpu_custom_call" | custom-call | tf_op jit(solution)/shard_map/pallas_call | solution.py:539
  30.4 6.9 %all-to-all-start = ((f32[32,4,128]{2,1,0:T(4,128)}), f32[32,4,128]{2,1,0:T(4,128)S(1)}, u32[]{:S(2)}, u32[]{:S(2)}) async-start(f32[32,4,128]{2,1,0:T(4,128)} %get-tuple-element.9), calls=%async_computation | async-start | bytes 131072 | tf_op jit(solution)/shard_map/all_to_all | solution.py:553
  37.3 7.3 %all-to-all-done.info_ref = f32[32,4,128]{2,1,0:T(4,128)S(1)} async-done(((f32[32,4,128]{2,1,0:T(4,128)}), f32[32,4,128]{2,1,0:T(4,128)S(1)}, u32[]{:S(2)}, u32[]{:S(2)}) %all-to-all-start) | async-done | bytes 65568 | tf_op jit(solution)/shard_map/all_to_all | solution.py:553
  44.6 1.0 %shard_map.123 = (f32[16,8,128]{2,1,0:T(8,128)}, f32[16,8,128]{2,1,0:T(8,128)}, f32[2,128]{1,0:T(2,128)}) custom-call(f32[32,4,128]{2,1,0:T(4,128)S(1)} %all-to-all-done.info_ref, f32[12,128,128]{2,1,0:T(8,128)S(1)} %get-tuple-element.10.fields_ref, s32[2,128]{1,0:T(2,128)S(1)} %fusion.owner_ref, s32[2,128]{1,0:T(2,128)S(1)} %get-tuple-element.11.place_ref), custom_call_target="tpu_custom_call" | custom-call | tf_op jit(solution)/shard_map/pallas_call | solution.py:561
  (24 shorter events, 0.1 us)
Async XLA Ops:
  0.6 0.8 %copy-start.2 = (f32[16,8,128]{2,1,0:T(8,128)S(1)}, f32[16,8,128]{2,1,0:T(8,128)}, u32[]{:S(2)}) copy-start(f32[16,8,128]{2,1,0:T(8,128)} %cot_hbm.1) | copy-start | bytes 196612
  1.5 0.7 %copy-start.7 = (f32[2,1,16]{2,1,0:T(1,128)S(1)}, f32[2,1,16]{2,1,0:T(1,128)}, u32[]{:S(2)}) copy-start(f32[2,1,16]{2,1,0:T(1,128)} %kap_hbm.1) | copy-start | bytes 388
  2.2 0.7 %copy-start.8 = (f32[2,1,16]{2,1,0:T(1,128)S(1)}, f32[2,1,16]{2,1,0:T(1,128)}, u32[]{:S(2)}) copy-start(f32[2,1,16]{2,1,0:T(1,128)} %cap_hbm.1) | copy-start | bytes 388
  3.2 5.3 %collective-permute-start = (f32[136,128]{1,0:T(8,128)S(1)}, f32[136,128]{1,0:T(8,128)S(1)}, u32[]{:S(2)}, u32[]{:S(2)}) collective-permute-start(f32[136,128]{1,0:T(8,128)S(1)} %get-tuple-element.7), channel_id=1, source_target_pairs={{0,1},{2,3},{4,5},{6,7},{8,9},{10,11},{12,13},{14,15},{1,0},{3,2},... | collective-permute-start | bytes 208904 | tf_op jit(solution)/shard_map/ppermute | solution.py:66
  6.2 7.5 %collective-permute-start.2 = (f32[24,128]{1,0:T(8,128)S(1)}, f32[24,128]{1,0:T(8,128)S(1)}, u32[]{:S(2)}, u32[]{:S(2)}) collective-permute-start(f32[24,128]{1,0:T(8,128)S(1)} %get-tuple-element.8), channel_id=1, source_target_pairs={{3,4},{7,8},{11,12},{4,3},{8,7},{12,11},{19,20},{23,24},{27,28},{2... | collective-permute-start | bytes 36872 | tf_op jit(solution)/shard_map/ppermute | solution.py:66
  8.5 5.1 %collective-permute-start.1 = (f32[272,128]{1,0:T(8,128)S(1)}, f32[272,128]{1,0:T(8,128)S(1)}, u32[]{:S(2)}, u32[]{:S(2)}) collective-permute-start(f32[272,128]{1,0:T(8,128)S(1)} %pad_maximum_fusion), channel_id=1, source_target_pairs={{0,2},{1,3},{4,6},{5,7},{8,10},{9,11},{12,14},{13,15},{2,0},{3,1},... | collective-permute-start | bytes 417800 | tf_op jit(solution)/shard_map/ppermute | solution.py:66
  10.6 11.9 %copy-start.9 = (s32[2,128]{1,0:T(2,128)S(1)}, s32[2,128]{1,0:T(2,128)}, u32[]{:S(2)}) copy-start(s32[2,128]{1,0:T(2,128)} %param.13) | copy-start | bytes 3076
  10.6 13.3 %copy-start.3 = (bf16[192,128]{1,0:T(8,128)(2,1)S(1)}, bf16[192,128]{1,0:T(8,128)(2,1)}, u32[]{:S(2)}) copy-start(bf16[192,128]{1,0:T(8,128)(2,1)} %constant.71.clone.refs_6_) | copy-start | bytes 147460
  10.6 13.3 %copy-start.5 = (f32[8,8,128]{2,1,0:T(8,128)S(1)}, f32[8,8,128]{2,1,0:T(8,128)}, u32[]{:S(2)}) copy-start(f32[8,8,128]{2,1,0:T(8,128)} %constant.76.clone.refs_11_) | copy-start | bytes 98308
  10.6 13.3 %copy-start = (bf16[256,256]{1,0:T(8,128)(2,1)S(1)}, bf16[256,256]{1,0:T(8,128)(2,1)}, u32[]{:S(2)}) copy-start(bf16[256,256]{1,0:T(8,128)(2,1)} %constant.73.clone.refs_8_) | copy-start | bytes 393220
  10.7 13.3 %copy-start.1 = (bf16[256,256]{1,0:T(8,128)(2,1)S(1)}, bf16[256,256]{1,0:T(8,128)(2,1)}, u32[]{:S(2)}) copy-start(bf16[256,256]{1,0:T(8,128)(2,1)} %constant.74.clone.refs_9_) | copy-start | bytes 393220
  13.6 10.3 %copy-start.4 = (f32[8,8,128]{2,1,0:T(8,128)S(1)}, f32[8,8,128]{2,1,0:T(8,128)}, u32[]{:S(2)}) copy-start(f32[8,8,128]{2,1,0:T(8,128)} %constant.75.clone.refs_10_) | copy-start | bytes 98308
  13.6 10.3 %copy-start.6 = (bf16[48,128]{1,0:T(8,128)(2,1)S(1)}, bf16[48,128]{1,0:T(8,128)(2,1)}, u32[]{:S(2)}) copy-start(bf16[48,128]{1,0:T(8,128)(2,1)} %constant.72.clone.refs_7_) | copy-start | bytes 36868
  13.7 8.3 %collective-permute-start.3 = (f32[568,128]{1,0:T(8,128)S(1)}, f32[568,128]{1,0:T(8,128)S(1)}, u32[]{:S(2)}, u32[]{:S(2)}) collective-permute-start(f32[568,128]{1,0:T(8,128)S(1)} %constant_dynamic-update-slice_fusion.refs_0_), channel_id=1, source_target_pairs={{0,4},{1,5},{2,6},{3,7},{8,12},{9,13},{10,14},{11,15},{4,0},{5,1},... | collective-permute-start | bytes 872456 | tf_op jit(solution)/shard_map/ppermute | solution.py:66
  16.4 5.5 %collective-permute-start.4 = (f32[568,128]{1,0:T(8,128)S(1)}, f32[568,128]{1,0:T(8,128)S(1)}, u32[]{:S(2)}, u32[]{:S(2)}) collective-permute-start(f32[568,128]{1,0:T(8,128)S(1)} %constant_dynamic-update-slice_fusion.refs_0_), channel_id=1, source_target_pairs={{4,8},{5,9},{6,10},{7,11},{8,4},{9,5},{10,6},{11,7},{20,24},{21,25... | collective-permute-start | bytes 872456 | tf_op jit(solution)/shard_map/ppermute | solution.py:66
  17.1 5.4 %collective-permute-start.5 = (f32[568,128]{1,0:T(8,128)S(1)}, f32[568,128]{1,0:T(8,128)S(1)}, u32[]{:S(2)}, u32[]{:S(2)}) collective-permute-start(f32[568,128]{1,0:T(8,128)S(1)} %constant_dynamic-update-slice_fusion.refs_0_), channel_id=1, source_target_pairs={{0,16},{16,0},{1,17},{17,1},{2,18},{18,2},{3,19},{19,3},{4,20},{20... | collective-permute-start | bytes 872456 | tf_op jit(solution)/shard_map/ppermute | solution.py:533
  21.9 1.6 %collective-permute-start.6 = (f32[568,128]{1,0:T(8,128)S(1)}, f32[568,128]{1,0:T(8,128)S(1)}, u32[]{:S(2)}, u32[]{:S(2)}) collective-permute-start(f32[568,128]{1,0:T(8,128)S(1)} %collective-permute-done.3.refs_1_), channel_id=1, source_target_pairs={{0,16},{16,0},{1,17},{17,1},{2,18},{18,2},{3,19},{19,3},{4,20},{20... | collective-permute-start | bytes 872456 | tf_op jit(solution)/shard_map/ppermute | solution.py:533
  21.9 2.0 %collective-permute-start.7 = (f32[568,128]{1,0:T(8,128)S(1)}, f32[568,128]{1,0:T(8,128)S(1)}, u32[]{:S(2)}, u32[]{:S(2)}) collective-permute-start(f32[568,128]{1,0:T(8,128)S(1)} %collective-permute-done.4.refs_2_), channel_id=1, source_target_pairs={{0,16},{16,0},{1,17},{17,1},{2,18},{18,2},{3,19},{19,3},{4,20},{20... | collective-permute-start | bytes 872456 | tf_op jit(solution)/shard_map/ppermute | solution.py:533
  30.4 14.2 %all-to-all-start = ((f32[32,4,128]{2,1,0:T(4,128)}), f32[32,4,128]{2,1,0:T(4,128)S(1)}, u32[]{:S(2)}, u32[]{:S(2)}) async-start(f32[32,4,128]{2,1,0:T(4,128)} %get-tuple-element.9), calls=%async_computation | async-start | bytes 131072 | tf_op jit(solution)/shard_map/all_to_all | solution.py:553

commit v5 on v4

--- a/solution.py
+++ b/solution.py
@@ -60,12 +60,6 @@
     return face_mat, ends_mat, row_a, row_b, omega.astype(np.float32), quot.astype(np.float32)
 
 
-def swap(value, axis, pairs):
-    if not pairs:
-        return None
-    return lax.ppermute(value, axis, [*pairs, *((b, a) for a, b in pairs)])
-
-
 def coef_rows(elems):
     return -(-(2 * elems) // 8) * 8
 
@@ -100,31 +94,30 @@
     return jnp.concatenate(planes, axis=0)
 
 
-def pack_kernel(cot_hbm, kap_hbm, cap_hbm, out_ref, edge_ref, cot_ref, kap_ref, cap_ref, sems):
-    loads = [
-        pltpu.make_async_copy(src, dst, sems.at[i])
-        for i, (src, dst) in enumerate(((cot_hbm, cot_ref), (kap_hbm, kap_ref), (cap_hbm, cap_ref)))
-    ]
-    for load in loads:
-        load.start()
-    for load in loads:
-        load.wait()
-    depth, _, span = cot_ref.shape
-    elems, _, parts = kap_ref.shape
+def pack_kernel(shape, raw_ref, out_ref):
+    depth, elems, parts = shape
+    span = raw_ref.shape[1]
     spread = (lax.broadcasted_iota(jnp.int32, (parts, span), 1) // 8 == lax.broadcasted_iota(jnp.int32, (parts, span), 0)).astype(F32)
-    coef = jnp.concatenate([kap_ref[...].reshape(elems, parts) * (1.0 / INV_STEP), cap_ref[...].reshape(elems, parts)], axis=0)
-    rows = coef_rows(elems)
-    if rows > 2 * elems:
-        coef = jnp.concatenate([coef, jnp.zeros((rows - 2 * elems, parts), F32)], axis=0)
+    coef = raw_ref[depth * 8 :, :parts]
+    coef = jnp.where(lax.broadcasted_iota(jnp.int32, coef.shape, 0) < elems, coef * (1.0 / INV_STEP), coef)
     coef = jnp.dot(coef, spread, precision=HIGHEST, preferred_element_type=F32)
     heavy = jnp.concatenate([jnp.broadcast_to(coef[elems + e : elems + e + 1], (64, span)) for e in range(elems)], axis=0)
-    value = join_depth(join_span(heavy * cot_ref[...].reshape(depth * 8, span)))
+    value = join_depth(join_span(heavy * raw_ref[: depth * 8, :]))
     out_ref[: depth * 8, :] = value
     out_ref[depth * 8 :, :] = coef
-    last = lax.rem(lax.axis_index("plane"), GROUP) == GROUP - 1
-    faces = [value.reshape(depth, 8, span)[:, node, :] for node in (0, 7)]
-    edge_ref[:depth, :] = jnp.where(last, faces[1], faces[0])
-    edge_ref[depth:, :] = coef
+
+
+def edge_kernel(depth, msg_ref, out_ref):
+    rows = msg_ref.shape[0] // 2
+    low, high = (msg_ref[pl.ds(rows + node, depth, stride=8), :] for node in (0, 7))
+    out_ref[:depth] = jnp.where(lax.rem(lax.axis_index("plane"), 2) == 0, high, low)
+    out_ref[depth:] = msg_ref[rows + depth * 8 :, :]
+
+
+def widen_kernel(depth, edge_ref, out_ref):
+    span = edge_ref.shape[1]
+    out_ref[: depth * 8] = jnp.concatenate([jnp.broadcast_to(edge_ref[z : z + 1, :], (8, span)) for z in range(depth)], axis=0)
+    out_ref[depth * 8 :] = edge_ref[depth:, :]
 
 
 class Layout:
@@ -140,9 +133,9 @@
         self.total = self.second + wide * self.at_once
 
 
-def basis_kernel(counts, present, *refs):
+def basis_kernel(counts, *refs):
     height, plane = counts
-    n_in = len(present) * height
+    n_in = 6 * height
     msgs = refs[:n_in]
     face_ref, ends_ref, row_a_ref, row_b_ref, omega_ref, quot_ref = refs[n_in : n_in + 6]
     fields_ref, info_ref = refs[n_in + 6 : n_in + 8]
@@ -165,45 +158,34 @@
     sub = lax.broadcasted_iota(jnp.int32, (8, span), 0)
     opens, closes = seams(span)
 
-    def stage_coef(msg, top, slot, block):
-        for kind in range(2):
-            for elem in range(own_elems):
-                at = top + kind * own_elems + elem
-                coef[slot, kind, block * own_elems + elem] = jnp.broadcast_to(msg[at : at + 1, :], (8, span))
-
     def stage(msg, piece, slot, block):
         top = piece * slab_rows
         raw[slot, pl.ds(pl.multiple_of(block * own_rows, own_rows), own_rows)] = msg[top : top + own_rows, :]
-        stage_coef(msg, top + own_rows, slot, block)
-
-    def stage_face(msg, slot, block):
-        top = GROUP * slab_rows
-        face = msg[top : top + own_depth, :]
-        spread = jnp.concatenate([jnp.broadcast_to(face[z : z + 1], (8, span)) for z in range(own_depth)], axis=0)
-        raw[slot, pl.ds(pl.multiple_of(block * own_rows, own_rows), own_rows)] = spread
-        stage_coef(msg, top + own_depth, slot, block)
-
-    def sides(name):
-        after = even if name == "pair" else jnp.logical_not(even)
-        return jnp.where(after, 1 + 2 * GROUP, 1), jnp.where(after, 3 * GROUP + 1, 0)
-
-    for name in ("pair", "cross"):
-        if name not in present:
-            base, beyond = sides(name)
-            for slot in [base + piece for piece in range(GROUP)] + [beyond]:
-                raw[slot] = jnp.zeros((rows, span), F32)
-                coef[slot] = jnp.zeros(coef.shape[1:], F32)
+        for kind in range(2):
+            for elem in range(own_elems):
+                at = top + own_rows + kind * own_elems + elem
+                coef[slot, kind, block * own_elems + elem] = jnp.broadcast_to(msg[at : at + 1, :], (8, span))
+
+    before, here, after = 1, 1 + GROUP, 1 + 2 * GROUP
+    early = member < GROUP // 2
+    lone = jnp.where(
+        early,
+        jnp.where(member == 0, 0, after + jnp.bitwise_xor(member, 3)),
+        jnp.where(member == GROUP - 1, 3 * GROUP + 1, before + jnp.bitwise_xor(member, 3)),
+    )
+    roles = (
+        (here, (0, 1)),
+        (here, (2, 3)),
+        (jnp.where(even, after, before), (0, 1)),
+        (jnp.where(even, before, after), (0, 1)),
+        (jnp.where(early, before, after), (2, 3)),
+        (lone, (None,)),
+    )
     for turn in range(height):
         block = lax.rem(height_pos - turn + height, height)
-        for pos, name in enumerate(present):
-            msg = msgs[turn * len(present) + pos]
-            if name == "own":
-                base = 1 + GROUP
-            else:
-                base, beyond = sides(name)
-                stage_face(msg, beyond, block)
-            for piece in range(GROUP):
-                stage(msg, piece, base + jnp.bitwise_xor(member, piece), block)
+        for msg, (base, owners) in zip(msgs[turn * len(roles) :], roles):
+            for piece, flip in enumerate(owners):
+                stage(msg, piece, base if flip is None else base + jnp.bitwise_xor(member, flip), block)
 
     def face_at(slot, width_node):
         return slot, pl.ds(width_node, depth, stride=8)
@@ -505,39 +487,60 @@
     vmem = pl.BlockSpec(memory_space=pltpu.VMEM)
 
     rows = depth * 8 + coef_rows(elems)
-    message, edge = pl.pallas_call(
-        pack_kernel,
-        out_shape=(jax.ShapeDtypeStruct((rows, span), F32), jax.ShapeDtypeStruct((depth + coef_rows(elems), span), F32)),
-        in_specs=[pl.BlockSpec(memory_space=pl.ANY)] * 3,
-        out_specs=(vmem, vmem),
-        scratch_shapes=[pltpu.VMEM(arr.shape, F32) for arr in (cotangent, conductivity, capacity)] + [pltpu.SemaphoreType.DMA((3,))],
+    lines = [conductivity.reshape(elems, cells), capacity.reshape(elems, cells)]
+    lines = [jnp.pad(line, ((0, 0), (0, span - cells))) for line in lines]
+    filler = jnp.zeros((rows - depth * 8 - 2 * elems, span), F32)
+    raw = jnp.concatenate([cotangent.reshape(depth * 8, span), *lines, filler], axis=0)
+    message = pl.pallas_call(
+        functools.partial(pack_kernel, (depth, elems, cells)),
+        out_shape=jax.ShapeDtypeStruct((rows, span), F32),
+        in_specs=[vmem],
+        out_specs=vmem,
         compiler_params=pltpu.CompilerParams(vmem_limit_bytes=4 * 2**20),
-    )(cotangent, conductivity, capacity)
-
-    beyond = swap(edge, "plane", [(g * GROUP + GROUP - 1, (g + 1) * GROUP) for g in range(groups - 1)])
-    gathered = message
-    width = 1
-    while width < GROUP:
-        other = swap(gathered, "plane", [(p, p ^ width) for p in range(plane) if p & width == 0])
-        gathered = jnp.concatenate([gathered, other], axis=0)
-        width *= 2
-    gathered = jnp.concatenate([gathered, edge if beyond is None else beyond], axis=0)
-
-    def group_pairs(turn):
-        return [(g * GROUP + m, (g + 1) * GROUP + m) for g in range(turn, groups - 1, 2) for m in range(GROUP)]
-
-    sent = {"own": gathered, "pair": swap(gathered, "plane", group_pairs(0)), "cross": swap(gathered, "plane", group_pairs(1))}
-    present = tuple(name for name, arr in sent.items() if arr is not None)
-    operands = [sent[name] for name in present]
+    )(raw)
+
+    def move(value, pairs):
+        return lax.ppermute(value, "plane", pairs) if pairs else jnp.zeros_like(value)
+
+    def both_ways(pairs):
+        return [*pairs, *((b, a) for a, b in pairs)]
+
+    def shift(gap, moving):
+        return [(g * GROUP + m, (g + gap) * GROUP + m) for g in range(groups) for m in moving if 0 <= g + gap < groups]
+
+    half = jnp.concatenate([message, move(message, [(p, p ^ 1) for p in range(plane)])], axis=0)
+    every = range(GROUP)
+    pair = move(half, both_ways([(a, b) for a, b in shift(1, every) if (a // GROUP) % 2 == 0]))
+    cross = move(half, both_ways([(a, b) for a, b in shift(1, every) if (a // GROUP) % 2 == 1]))
+    other = move(half, [(p, p ^ 2) for p in range(plane)])
+    side = move(other, shift(1, (0, 1)) + shift(-1, (2, 3)))
+    edge = pl.pallas_call(
+        functools.partial(edge_kernel, depth),
+        out_shape=jax.ShapeDtypeStruct((rows - depth * 7, span), F32),
+        in_specs=[vmem],
+        out_specs=vmem,
+        compiler_params=pltpu.CompilerParams(vmem_limit_bytes=4 * 2**20),
+    )(other)
+    edge = move(edge, shift(2, (0,)) + shift(-1, (1,)) + shift(1, (2,)) + shift(-2, (3,)))
+    lone = pl.pallas_call(
+        functools.partial(widen_kernel, depth),
+        out_shape=jax.ShapeDtypeStruct((rows, span), F32),
+        in_specs=[vmem],
+        out_specs=vmem,
+        cost_estimate=pl.CostEstimate(flops=1000000, bytes_accessed=1000000, transcendentals=0),
+        compiler_params=pltpu.CompilerParams(vmem_limit_bytes=4 * 2**20),
+    )(edge)
+    sent = (half, other, pair, cross, side, lone)
+    operands = list(sent)
     for turn in range(1, height):
-        operands += [lax.ppermute(sent[name], "height", [(h, (h + turn) % height) for h in range(height)]) for name in present]
+        operands += [lax.ppermute(arr, "height", [(h, (h + turn) % height) for h in range(height)]) for arr in sent]
 
     lay = Layout(elems * height > 4)
     consts = tables(span)
     slots = 3 * GROUP + 2
     slab_bytes = 4 * depth * 8 * height * span
     fields, info = pl.pallas_call(
-        functools.partial(basis_kernel, counts, present),
+        functools.partial(basis_kernel, counts),
         out_shape=(jax.ShapeDtypeStruct((12, depth * 8, span), F32), jax.ShapeDtypeStruct((devices, 12 * elems * cells // span + 1, span), F32)),
         in_specs=[vmem] * (len(operands) + len(consts)),
         out_specs=(vmem, vmem),

time: 46 us -> 43.7 us (0.950)
  waiting for transfers between devices: 18.1 us -> 12.4 us
  starting transfers between devices: 16.6 us -> 20.8 us
  local copies, waits for them, and re-layouts: 2.26 us -> 0.81 us
  other arithmetic: 0.05 us -> 0.97 us
    ppermute x8 -> x12, starting transfers between devices: 9.77 us -> 17.2 us  [the longest x6 16 us: move(): lax.ppermute(value, 'plane', pairs)]
    ppermute x8 -> x12, waiting for transfers between devices: 10.8 us -> 5.05 us  [the longest x6 3.81 us: move(): lax.ppermute(value, 'plane', pairs)]
    all_to_all x1, starting transfers between devices: 6.87 us -> 3.58 us  [per_device(): shared = lax.all_to_all(info, ('height', 'plane'), 0, 0, tiled=True)]
    unnamed x23 -> x18, local copies, waits for them, and re-layouts: 2.25 us -> 0.73 us
    concatenate x1 -> x2, other arithmetic: 0.01 us -> 0.93 us  [the longest x1 0.92 us: per_device(): jnp.concatenate([cotangent.reshape(depth * 8, span), *lines, filler], axi...]
    pallas_call x2 -> x4, Pallas kernels: 6.81 us -> 6.6 us  [the longest x1 6.35 us: per_device(): pl.pallas_call(functools.partial(basis_kernel, counts), out_shape=(jax.Sh...]
  transfers between devices with their start and end apart: 9 -> 13, of which waited for: 6 -> 6; matrix products, arithmetic and copies ran while one was open for 0% -> 0% of each run, Pallas kernels for 0% -> 0%
where the time goes in v5:
time: 43.7 us; the launch traced here: 43.4 us
  starting transfers between devices  20.8 us (48%)
  waiting for transfers between devices  12.4 us (28%)
  Pallas kernels  7.65 us (18%)
  other arithmetic  0.97 us (2%)
  between operations  0.83 us (2%)
  local copies, waits for them, and re-layouts  0.81 us (2%)
    ppermute x6, starting transfers between devices, move(): lax.ppermute(value, 'plane', pairs)  16 us
    all_to_all x1, waiting for transfers between devices, per_device(): shared = lax.all_to_all(info, ('height', 'plane'), 0, 0, tiled=True)  7.3 us
    pallas_call x1, Pallas kernels, per_device(): pl.pallas_call(functools.partial(basis_kernel, counts), out_shape=(jax.Sh...  6.35 us
    ppermute x6, waiting for transfers between devices, move(): lax.ppermute(value, 'plane', pairs)  3.81 us
    all_to_all x1, starting transfers between devices, per_device(): shared = lax.all_to_all(info, ('height', 'plane'), 0, 0, tiled=True)  3.58 us
    ppermute x6, starting transfers between devices, per_device(): lax.ppermute(arr, 'height', [(h, (h + turn) % height) for h in range(heig...  1.29 us
    ppermute x6, waiting for transfers between devices, per_device(): lax.ppermute(arr, 'height', [(h, (h + turn) % height) for h in range(heig...  1.24 us
    pallas_call x1, Pallas kernels, per_device(): pl.pallas_call(combine_kernel, out_shape=(jax.ShapeDtypeStruct(cotangent....  1.05 us
  transfers between devices with their start and end apart: 13, of which 6 were waited for; matrix products, arithmetic and copies ran while one was open for 0% of the time, Pallas kernels for 0%

profile of v5, /device:TPU:0, one launch (start us, length us, event | category | flops | bytes accessed | tf_op | source)
XLA Modules:
  0.0 43.4 jit_solution(1770636710776436498)
XLA Ops:
  0.6 0.1 pad.14.clone
  0.7 0.7 %copy-done.7 = f32[2,1,16]{2,1,0:T(1,128)S(1)} copy-done((f32[2,1,16]{2,1,0:T(1,128)S(1)}, f32[2,1,16]{2,1,0:T(1,128)}, u32[]{:S(2)}) %copy-start.7) | copy-done | bytes 152
  1.4 0.9 %fusion.raw_ref = f32[136,128]{1,0:T(8,128)S(1)} fusion(f32[2,16]{1,0:T(2,128)S(1)} %bitcast.4, f32[2,16]{1,0:T(2,128)S(1)} %bitcast.5, f32[128,128]{1,0:T(8,128)} %bitcast.3, f32[136]{0:T(256)S(1)} %pad.14.clone), kind=kLoop, calls=%fused_computation.6 | loop fusion | flops 191488 | bytes 135968 | tf_op jit(solution)/shard_map/concatenate | solution.py:493
  2.3 0.2 shard_map.121
  2.6 3.0 %collective-permute-start = (f32[136,128]{1,0:T(8,128)S(1)}, f32[136,128]{1,0:T(8,128)S(1)}, u32[]{:S(2)}, u32[]{:S(2)}) collective-permute-start(f32[136,128]{1,0:T(8,128)S(1)} %shard_map.121), channel_id=1, source_target_pairs={{0,1},{1,0},{2,3},{3,2},{4,5},{5,4},{6,7},{7,6},{8,9},{9,8},{10,11... | collective-permute-start | bytes 208904 | tf_op jit(solution)/shard_map/ppermute | solution.py:503
  5.6 2.3 %collective-permute-done = f32[136,128]{1,0:T(8,128)S(1)} collective-permute-done((f32[136,128]{1,0:T(8,128)S(1)}, f32[136,128]{1,0:T(8,128)S(1)}, u32[]{:S(2)}, u32[]{:S(2)}) %collective-permute-start) | collective-permute-done | bytes 69664 | tf_op jit(solution)/shard_map/ppermute | solution.py:503
  7.9 2.1 %collective-permute-start.1 = (f32[272,128]{1,0:T(8,128)S(1)}, f32[272,128]{1,0:T(8,128)S(1)}, u32[]{:S(2)}, u32[]{:S(2)}) collective-permute-start(f32[272,128]{1,0:T(8,128)S(1)} %pad_maximum_fusion.refs_0_), channel_id=1, source_target_pairs={{0,2},{1,3},{2,0},{3,1},{4,6},{5,7},{6,4},{7,5},{8,10},{9,11},{10,... | collective-permute-start | bytes 417800 | tf_op jit(solution)/shard_map/ppermute | solution.py:503
  10.0 1.6 %collective-permute-start.2 = (f32[272,128]{1,0:T(8,128)S(1)}, f32[272,128]{1,0:T(8,128)S(1)}, u32[]{:S(2)}, u32[]{:S(2)}) collective-permute-start(f32[272,128]{1,0:T(8,128)S(1)} %pad_maximum_fusion.refs_0_), channel_id=1, source_target_pairs={{0,4},{1,5},{2,6},{3,7},{8,12},{9,13},{10,14},{11,15},{4,0},{5,1},... | collective-permute-start | bytes 417800 | tf_op jit(solution)/shard_map/ppermute | solution.py:503
  11.6 0.7 %collective-permute-start.3 = (f32[272,128]{1,0:T(8,128)S(1)}, f32[272,128]{1,0:T(8,128)S(1)}, u32[]{:S(2)}, u32[]{:S(2)}) collective-permute-start(f32[272,128]{1,0:T(8,128)S(1)} %pad_maximum_fusion.refs_0_), channel_id=1, source_target_pairs={{4,8},{5,9},{6,10},{7,11},{8,4},{9,5},{10,6},{11,7},{20,24},{21,25... | collective-permute-start | bytes 417800 | tf_op jit(solution)/shard_map/ppermute | solution.py:503
  12.3 0.1 collective-permute-start.6
  12.3 0.7 %collective-permute-done.1.msg_ref.refs_1_ = f32[272,128]{1,0:T(8,128)S(1)} collective-permute-done((f32[272,128]{1,0:T(8,128)S(1)}, f32[272,128]{1,0:T(8,128)S(1)}, u32[]{:S(2)}, u32[]{:S(2)}) %collective-permute-start.1) | collective-permute-done | bytes 139296 | tf_op jit(solution)/shard_map/ppermute | solution.py:503
  13.1 5.6 %collective-permute-start.4 = (f32[272,128]{1,0:T(8,128)S(1)}, f32[272,128]{1,0:T(8,128)S(1)}, u32[]{:S(2)}, u32[]{:S(2)}) collective-permute-start(f32[272,128]{1,0:T(8,128)S(1)} %collective-permute-done.1.msg_ref.refs_1_), channel_id=1, source_target_pairs={{0,4},{1,5},{4,8},{5,9},{8,12},{9,13},{6,2},{7,3},{10,6},{11,7},{1... | collective-permute-start | bytes 417800 | tf_op jit(solution)/shard_map/ppermute | solution.py:503
  18.7 3.0 %collective-permute-start.5 = (f32[24,128]{1,0:T(8,128)S(1)}, f32[24,128]{1,0:T(8,128)S(1)}, u32[]{:S(2)}, u32[]{:S(2)}) collective-permute-start(f32[24,128]{1,0:T(8,128)S(1)} %shard_map.122), channel_id=1, source_target_pairs={{0,8},{4,12},{5,1},{9,5},{13,9},{2,6},{6,10},{10,14},{11,3},{15,7}... | collective-permute-start | bytes 36872 | tf_op jit(solution)/shard_map/ppermute | solution.py:503
  21.7 0.1 collective-permute-start.7
  21.8 0.5 %collective-permute-start.8 = (f32[272,128]{1,0:T(8,128)S(1)}, f32[272,128]{1,0:T(8,128)S(1)}, u32[]{:S(2)}, u32[]{:S(2)}) collective-permute-start(f32[272,128]{1,0:T(8,128)S(1)} %collective-permute-done.2.refs_2_), channel_id=1, source_target_pairs={{0,16},{16,0},{1,17},{17,1},{2,18},{18,2},{3,19},{19,3},{4,20},{20... | collective-permute-start | bytes 417800 | tf_op jit(solution)/shard_map/ppermute | solution.py:536
  22.3 0.8 %collective-permute-done.5.edge_ref = f32[24,128]{1,0:T(8,128)S(1)} collective-permute-done((f32[24,128]{1,0:T(8,128)S(1)}, f32[24,128]{1,0:T(8,128)S(1)}, u32[]{:S(2)}, u32[]{:S(2)}) %collective-permute-start.5) | collective-permute-done | bytes 12320 | tf_op jit(solution)/shard_map/ppermute | solution.py:503
  23.1 0.6 %collective-permute-start.11 = (f32[136,128]{1,0:T(8,128)S(1)}, f32[136,128]{1,0:T(8,128)S(1)}, u32[]{:S(2)}, u32[]{:S(2)}) collective-permute-start(f32[136,128]{1,0:T(8,128)S(1)} %shard_map.123.refs_5_), channel_id=1, source_target_pairs={{0,16},{16,0},{1,17},{17,1},{2,18},{18,2},{3,19},{19,3},{4,20},{20... | collective-permute-start | bytes 208904 | tf_op jit(solution)/shard_map/ppermute | solution.py:536
  23.7 0.1 collective-permute-start.10
  23.8 0.8 %collective-permute-done.11.refs_11_ = f32[136,128]{1,0:T(8,128)S(1)} collective-permute-done((f32[136,128]{1,0:T(8,128)S(1)}, f32[136,128]{1,0:T(8,128)S(1)}, u32[]{:S(2)}, u32[]{:S(2)}) %collective-permute-start.11) | collective-permute-done | bytes 69664 | tf_op jit(solution)/shard_map/ppermute | solution.py:536
  24.6 0.4 %collective-permute-done.10.refs_10_ = f32[272,128]{1,0:T(8,128)S(1)} collective-permute-done((f32[272,128]{1,0:T(8,128)S(1)}, f32[272,128]{1,0:T(8,128)S(1)}, u32[]{:S(2)}, u32[]{:S(2)}) %collective-permute-start.10) | collective-permute-done | bytes 139296 | tf_op jit(solution)/shard_map/ppermute | solution.py:536
  25.1 6.3 %shard_map.124 = (f32[12,128,128]{2,1,0:T(8,128)S(1)}, f32[32,4,128]{2,1,0:T(4,128)}) custom-call(f32[272,128]{1,0:T(8,128)S(1)} %pad_maximum_fusion.refs_0_, f32[272,128]{1,0:T(8,128)S(1)} %collective-permute-done.1.msg_ref.refs_1_, f32[272,128]{1,0:T(8,128)S(1)} %collective-permute-done.2.refs_2_, f32[272,128]{1,0:T(8,128)S(1)} %collective-permute-done.3.refs_3_, ...), custom_call_target="tpu_custom_call" | custom-call | tf_op jit(solution)/shard_map/pallas_call | solution.py:542
  31.5 3.6 %all-to-all-start = ((f32[32,4,128]{2,1,0:T(4,128)}), f32[32,4,128]{2,1,0:T(4,128)S(1)}, u32[]{:S(2)}, u32[]{:S(2)}) async-start(f32[32,4,128]{2,1,0:T(4,128)} %get-tuple-element.5), calls=%async_computation | async-start | bytes 131072 | tf_op jit(solution)/shard_map/all_to_all | solution.py:556
  35.1 7.3 %all-to-all-done.info_ref = f32[32,4,128]{2,1,0:T(4,128)S(1)} async-done(((f32[32,4,128]{2,1,0:T(4,128)}), f32[32,4,128]{2,1,0:T(4,128)S(1)}, u32[]{:S(2)}, u32[]{:S(2)}) %all-to-all-start) | async-done | bytes 65568 | tf_op jit(solution)/shard_map/all_to_all | solution.py:556
  42.4 1.0 %shard_map.125 = (f32[16,8,128]{2,1,0:T(8,128)}, f32[16,8,128]{2,1,0:T(8,128)}, f32[2,128]{1,0:T(2,128)}) custom-call(f32[32,4,128]{2,1,0:T(4,128)S(1)} %all-to-all-done.info_ref, f32[12,128,128]{2,1,0:T(8,128)S(1)} %get-tuple-element.6.fields_ref, s32[2,128]{1,0:T(2,128)S(1)} %fusion.3.owner_ref, s32[2,128]{1,0:T(2,128)S(1)} %get-tuple-element.7.place_ref), custom_call_target="tpu_custom_call" | custom-call | tf_op jit(solution)/shard_map/pallas_call | solution.py:564
  (31 shorter events, 0.2 us)
Async XLA Ops:
  0.7 0.7 %copy-start.7 = (f32[2,1,16]{2,1,0:T(1,128)S(1)}, f32[2,1,16]{2,1,0:T(1,128)}, u32[]{:S(2)}) copy-start(f32[2,1,16]{2,1,0:T(1,128)} %param.11) | copy-start | bytes 388
  0.7 0.7 %copy-start.6 = (f32[2,1,16]{2,1,0:T(1,128)S(1)}, f32[2,1,16]{2,1,0:T(1,128)}, u32[]{:S(2)}) copy-start(f32[2,1,16]{2,1,0:T(1,128)} %param.12) | copy-start | bytes 388
  2.6 5.3 %collective-permute-start = (f32[136,128]{1,0:T(8,128)S(1)}, f32[136,128]{1,0:T(8,128)S(1)}, u32[]{:S(2)}, u32[]{:S(2)}) collective-permute-start(f32[136,128]{1,0:T(8,128)S(1)} %shard_map.121), channel_id=1, source_target_pairs={{0,1},{1,0},{2,3},{3,2},{4,5},{5,4},{6,7},{7,6},{8,9},{9,8},{10,11... | collective-permute-start | bytes 208904 | tf_op jit(solution)/shard_map/ppermute | solution.py:503
  7.9 17.2 %copy-start.1 = (bf16[256,256]{1,0:T(8,128)(2,1)S(1)}, bf16[256,256]{1,0:T(8,128)(2,1)}, u32[]{:S(2)}) copy-start(bf16[256,256]{1,0:T(8,128)(2,1)} %constant.78.clone.refs_15_) | copy-start | bytes 393220
  7.9 17.2 %copy-start.4 = (f32[8,8,128]{2,1,0:T(8,128)S(1)}, f32[8,8,128]{2,1,0:T(8,128)}, u32[]{:S(2)}) copy-start(f32[8,8,128]{2,1,0:T(8,128)} %constant.80.clone.refs_17_) | copy-start | bytes 98308
  7.9 17.2 %copy-start = (bf16[256,256]{1,0:T(8,128)(2,1)S(1)}, bf16[256,256]{1,0:T(8,128)(2,1)}, u32[]{:S(2)}) copy-start(bf16[256,256]{1,0:T(8,128)(2,1)} %constant.77.clone.refs_14_) | copy-start | bytes 393220
  7.9 5.1 %collective-permute-start.1 = (f32[272,128]{1,0:T(8,128)S(1)}, f32[272,128]{1,0:T(8,128)S(1)}, u32[]{:S(2)}, u32[]{:S(2)}) collective-permute-start(f32[272,128]{1,0:T(8,128)S(1)} %pad_maximum_fusion.refs_0_), channel_id=1, source_target_pairs={{0,2},{1,3},{2,0},{3,1},{4,6},{5,7},{6,4},{7,5},{8,10},{9,11},{10,... | collective-permute-start | bytes 417800 | tf_op jit(solution)/shard_map/ppermute | solution.py:503
  10.0 11.7 %collective-permute-start.2 = (f32[272,128]{1,0:T(8,128)S(1)}, f32[272,128]{1,0:T(8,128)S(1)}, u32[]{:S(2)}, u32[]{:S(2)}) collective-permute-start(f32[272,128]{1,0:T(8,128)S(1)} %pad_maximum_fusion.refs_0_), channel_id=1, source_target_pairs={{0,4},{1,5},{2,6},{3,7},{8,12},{9,13},{10,14},{11,15},{4,0},{5,1},... | collective-permute-start | bytes 417800 | tf_op jit(solution)/shard_map/ppermute | solution.py:503
  11.6 10.2 %collective-permute-start.3 = (f32[272,128]{1,0:T(8,128)S(1)}, f32[272,128]{1,0:T(8,128)S(1)}, u32[]{:S(2)}, u32[]{:S(2)}) collective-permute-start(f32[272,128]{1,0:T(8,128)S(1)} %pad_maximum_fusion.refs_0_), channel_id=1, source_target_pairs={{4,8},{5,9},{6,10},{7,11},{8,4},{9,5},{10,6},{11,7},{20,24},{21,25... | collective-permute-start | bytes 417800 | tf_op jit(solution)/shard_map/ppermute | solution.py:503
  12.3 10.9 %collective-permute-start.6 = (f32[272,128]{1,0:T(8,128)S(1)}, f32[272,128]{1,0:T(8,128)S(1)}, u32[]{:S(2)}, u32[]{:S(2)}) collective-permute-start(f32[272,128]{1,0:T(8,128)S(1)} %pad_maximum_fusion.refs_0_), channel_id=1, source_target_pairs={{0,16},{16,0},{1,17},{17,1},{2,18},{18,2},{3,19},{19,3},{4,20},{20... | collective-permute-start | bytes 417800 | tf_op jit(solution)/shard_map/ppermute | solution.py:536
  13.1 10.7 %collective-permute-start.4 = (f32[272,128]{1,0:T(8,128)S(1)}, f32[272,128]{1,0:T(8,128)S(1)}, u32[]{:S(2)}, u32[]{:S(2)}) collective-permute-start(f32[272,128]{1,0:T(8,128)S(1)} %collective-permute-done.1.msg_ref.refs_1_), channel_id=1, source_target_pairs={{0,4},{1,5},{4,8},{5,9},{8,12},{9,13},{6,2},{7,3},{10,6},{11,7},{1... | collective-permute-start | bytes 417800 | tf_op jit(solution)/shard_map/ppermute | solution.py:503
  18.7 5.1 %copy-start.8 = (s32[2,128]{1,0:T(2,128)S(1)}, s32[2,128]{1,0:T(2,128)}, u32[]{:S(2)}) copy-start(s32[2,128]{1,0:T(2,128)} %param.13) | copy-start | bytes 3076
  18.7 6.4 %copy-start.5 = (bf16[48,128]{1,0:T(8,128)(2,1)S(1)}, bf16[48,128]{1,0:T(8,128)(2,1)}, u32[]{:S(2)}) copy-start(bf16[48,128]{1,0:T(8,128)(2,1)} %constant.76.clone.refs_13_) | copy-start | bytes 36868
  18.7 6.4 %copy-start.2 = (bf16[192,128]{1,0:T(8,128)(2,1)S(1)}, bf16[192,128]{1,0:T(8,128)(2,1)}, u32[]{:S(2)}) copy-start(bf16[192,128]{1,0:T(8,128)(2,1)} %constant.75.clone.refs_12_) | copy-start | bytes 147460
  18.7 6.4 %copy-start.3 = (f32[8,8,128]{2,1,0:T(8,128)S(1)}, f32[8,8,128]{2,1,0:T(8,128)}, u32[]{:S(2)}) copy-start(f32[8,8,128]{2,1,0:T(8,128)} %constant.79.clone.refs_16_) | copy-start | bytes 98308
  18.7 4.4 %collective-permute-start.5 = (f32[24,128]{1,0:T(8,128)S(1)}, f32[24,128]{1,0:T(8,128)S(1)}, u32[]{:S(2)}, u32[]{:S(2)}) collective-permute-start(f32[24,128]{1,0:T(8,128)S(1)} %shard_map.122), channel_id=1, source_target_pairs={{0,8},{4,12},{5,1},{9,5},{13,9},{2,6},{6,10},{10,14},{11,3},{15,7}... | collective-permute-start | bytes 36872 | tf_op jit(solution)/shard_map/ppermute | solution.py:503
  21.7 2.9 %collective-permute-start.7 = (f32[272,128]{1,0:T(8,128)S(1)}, f32[272,128]{1,0:T(8,128)S(1)}, u32[]{:S(2)}, u32[]{:S(2)}) collective-permute-start(f32[272,128]{1,0:T(8,128)S(1)} %collective-permute-done.1.msg_ref.refs_1_), channel_id=1, source_target_pairs={{0,16},{16,0},{1,17},{17,1},{2,18},{18,2},{3,19},{19,3},{4,20},{20... | collective-permute-start | bytes 417800 | tf_op jit(solution)/shard_map/ppermute | solution.py:536
  21.8 2.8 %collective-permute-start.8 = (f32[272,128]{1,0:T(8,128)S(1)}, f32[272,128]{1,0:T(8,128)S(1)}, u32[]{:S(2)}, u32[]{:S(2)}) collective-permute-start(f32[272,128]{1,0:T(8,128)S(1)} %collective-permute-done.2.refs_2_), channel_id=1, source_target_pairs={{0,16},{16,0},{1,17},{17,1},{2,18},{18,2},{3,19},{19,3},{4,20},{20... | collective-permute-start | bytes 417800 | tf_op jit(solution)/shard_map/ppermute | solution.py:536
  23.1 1.5 %collective-permute-start.9 = (f32[272,128]{1,0:T(8,128)S(1)}, f32[272,128]{1,0:T(8,128)S(1)}, u32[]{:S(2)}, u32[]{:S(2)}) collective-permute-start(f32[272,128]{1,0:T(8,128)S(1)} %collective-permute-done.3.refs_3_), channel_id=1, source_target_pairs={{0,16},{16,0},{1,17},{17,1},{2,18},{18,2},{3,19},{19,3},{4,20},{20... | collective-permute-start | bytes 417800 | tf_op jit(solution)/shard_map/ppermute | solution.py:536
  23.1 1.5 %collective-permute-start.11 = (f32[136,128]{1,0:T(8,128)S(1)}, f32[136,128]{1,0:T(8,128)S(1)}, u32[]{:S(2)}, u32[]{:S(2)}) collective-permute-start(f32[136,128]{1,0:T(8,128)S(1)} %shard_map.123.refs_5_), channel_id=1, source_target_pairs={{0,16},{16,0},{1,17},{17,1},{2,18},{18,2},{3,19},{19,3},{4,20},{20... | collective-permute-start | bytes 208904 | tf_op jit(solution)/shard_map/ppermute | solution.py:536
  23.7 1.4 %collective-permute-start.10 = (f32[272,128]{1,0:T(8,128)S(1)}, f32[272,128]{1,0:T(8,128)S(1)}, u32[]{:S(2)}, u32[]{:S(2)}) collective-permute-start(f32[272,128]{1,0:T(8,128)S(1)} %collective-permute-done.4.refs_4_), channel_id=1, source_target_pairs={{0,16},{16,0},{1,17},{17,1},{2,18},{18,2},{3,19},{19,3},{4,20},{20... | collective-permute-start | bytes 417800 | tf_op jit(solution)/shard_map/ppermute | solution.py:536
  31.5 10.9 %all-to-all-start = ((f32[32,4,128]{2,1,0:T(4,128)}), f32[32,4,128]{2,1,0:T(4,128)S(1)}, u32[]{:S(2)}, u32[]{:S(2)}) async-start(f32[32,4,128]{2,1,0:T(4,128)} %get-tuple-element.5), calls=%async_computation | async-start | bytes 131072 | tf_op jit(solution)/shard_map/all_to_all | solution.py:556

commit v6 on v5

--- a/solution.py
+++ b/solution.py
@@ -14,6 +14,7 @@
 GROUP = 4
 REACH = 4
 PAIRS = ((0, 0), (0, 1), (0, 2), (1, 1), (1, 2), (2, 2))
+BANDS = ((0, 0), (0, 1), (1, 1), (1, 2), (2, 2))
 TINY = 1e-30
 HIGHEST = lax.Precision.HIGHEST
 F32 = jnp.float32
@@ -99,7 +100,8 @@
     span = raw_ref.shape[1]
     spread = (lax.broadcasted_iota(jnp.int32, (parts, span), 1) // 8 == lax.broadcasted_iota(jnp.int32, (parts, span), 0)).astype(F32)
     coef = raw_ref[depth * 8 :, :parts]
-    coef = jnp.where(lax.broadcasted_iota(jnp.int32, coef.shape, 0) < elems, coef * (1.0 / INV_STEP), coef)
+    pair = [coef[2 * e : 2 * e + 1] * (1.0 / INV_STEP) for e in range(elems)] + [coef[2 * e + 1 : 2 * e + 2] for e in range(elems)]
+    coef = jnp.concatenate([*pair, coef[2 * elems :]], axis=0)
     coef = jnp.dot(coef, spread, precision=HIGHEST, preferred_element_type=F32)
     heavy = jnp.concatenate([jnp.broadcast_to(coef[elems + e : elems + e + 1], (64, span)) for e in range(elems)], axis=0)
     value = join_depth(join_span(heavy * raw_ref[: depth * 8, :]))
@@ -271,8 +273,6 @@
             for (_, sums, at), value in zip(work, made):
                 pool[sums + at] = join_depth(join_span(value))
 
-        for here, sums, _ in chains:
-            ends((here + low, here + high), (sums + low, sums + high), (low, high), 1.0 / shift)
         if whole:
             for here, sums, after in chains:
                 loop(low + 1, high, each(lambda at: apply([(here, sums, at)])))
@@ -280,6 +280,8 @@
             work = [(here, sums, at) for here, sums, _ in chains for at in range(low + 1, high)]
             for first in range(0, len(work), 2):
                 apply(work[first : first + 2])
+        for here, sums, _ in chains:
+            ends((here + low, here + high), (sums + low, sums + high), (low, high), 1.0 / shift)
         for here, sums, after in chains:
             loop(low, high, each(lambda at: join_width(pool, sums + at)))
 
@@ -380,17 +382,16 @@
 
     parts = []
     left = [weigh[...] * fields_ref[i] for i in range(3)]
-    parts += [total(left[i] * fields_ref[j]) for i, j in PAIRS]
+    parts += [total(left[i] * fields_ref[j]) for i, j in BANDS]
     lasts = (2, 9, 10, 11)
     energy = []
     for k in (0, 2):
         energy += operator([fields_ref[i] for i in lasts[k : k + 2]], [slot] * 2, 1.0, start)
     energy = [omega * e for e in energy]
     parts.append(total(fields_ref[2] * energy[0]))
-    for k, l in PAIRS:
-        pairs = PAIRS if k == l else [(i, j) for i in range(3) for j in range(3)]
+    for k, l in BANDS:
         left = [weigh[...] * fields_ref[3 + 3 * k + i] for i in range(3)]
-        parts += [total(left[i] * fields_ref[3 + 3 * l + j]) for i, j in pairs]
+        parts += [total(left[i] * fields_ref[3 + 3 * l + j]) for i, j in PAIRS]
     parts += [total(fields_ref[9 + i] * energy[1 + j]) for i, j in PAIRS]
     lines = [jnp.sum(part, axis=0, keepdims=True) for part in parts]
     lines.append(jnp.zeros((span - len(lines), span), F32))
@@ -414,8 +415,9 @@
 
 
 def galerkin(gram, energy):
-    n00, n01, n02, n11, n12, n22 = gram
+    n00, n01, n11, n12, n22 = gram
     first, later = SHIFTS
+    n02 = (first / later) * (n11 + n01) - n01
     h00, h01, h02 = first * (n01 + n00), first * (n11 + n01), first * (n12 + n02)
     h11, h12 = later * (n12 + n11), later * (n22 + n12)
     low10, low20 = h01 / h00, h02 / h00
@@ -437,16 +439,11 @@
     ones = jnp.ones((devices, span), F32)
     contract = (((0,), (0,)), ((), ()))
     wide = lax.dot_general(info_ref[:, lines - 1, :], ones, contract, precision=HIGHEST, preferred_element_type=F32)
-    take = [wide[i : i + 1, :] for i in range(7 + 45 + 6)]
-    coef = galerkin(take[:6], take[6])
-    at = 7
+    take = [wide[i : i + 1, :] for i in range(6 + 30 + 6)]
+    coef = galerkin(take[:5], take[5])
     double = [(2.0 if i != j else 1.0) * coef[i] * coef[j] for i, j in PAIRS]
-    every = [coef[i] * coef[j] for i in range(3) for j in range(3)]
-    gram = []
-    for k, l in PAIRS:
-        factors = double if k == l else every
-        gram.append(sum(f * t for f, t in zip(factors, take[at : at + len(factors)])))
-        at += len(factors)
+    gram = [sum(f * t for f, t in zip(double, take[at : at + 6])) for at in range(6, 36, 6)]
+    at = 36
     energy = sum(f * t for f, t in zip(double, take[at : at + 6]))
     outer = galerkin(gram, energy)
     factors = list(coef) + [d * c for d in outer for c in coef]
@@ -487,10 +484,9 @@
     vmem = pl.BlockSpec(memory_space=pltpu.VMEM)
 
     rows = depth * 8 + coef_rows(elems)
-    lines = [conductivity.reshape(elems, cells), capacity.reshape(elems, cells)]
-    lines = [jnp.pad(line, ((0, 0), (0, span - cells))) for line in lines]
-    filler = jnp.zeros((rows - depth * 8 - 2 * elems, span), F32)
-    raw = jnp.concatenate([cotangent.reshape(depth * 8, span), *lines, filler], axis=0)
+    lines = jnp.concatenate([conductivity, capacity], axis=1).reshape(elems * 2, cells)
+    lines = jnp.pad(lines, ((0, rows - depth * 8 - 2 * elems), (0, span - cells)))
+    raw = jnp.concatenate([cotangent.reshape(depth * 8, span), lines], axis=0)
     message = pl.pallas_call(
         functools.partial(pack_kernel, (depth, elems, cells)),
         out_shape=jax.ShapeDtypeStruct((rows, span), F32),

time: 43.7 us -> 43.1 us (0.986)
  local copies, waits for them, and re-layouts: 0.81 us -> 0.04 us
  other arithmetic: 0.97 us -> 1.6 us
  Pallas kernels: 7.65 us -> 7.13 us
    unnamed x18 -> x14, local copies, waits for them, and re-layouts: 0.73 us -> 0.04 us
    concatenate x1 -> x2, other arithmetic: 0.92 us -> 1.55 us  [the longest x1 0.84 us: per_device(): raw = jnp.concatenate([cotangent.reshape(depth * 8, span), lines], axis=0)]
    pallas_call x1, Pallas kernels: 6.35 us -> 5.83 us  [per_device(): pl.pallas_call(functools.partial(basis_kernel, counts), out_shape=(jax.Sh...]
where the time goes in v6:
time: 43.1 us; the launch traced here: 42.7 us
  starting transfers between devices  20.8 us (48%)
  waiting for transfers between devices  12.4 us (29%)
  Pallas kernels  7.13 us (17%)
  other arithmetic  1.6 us (4%)
  between operations  0.81 us (2%)
    ppermute x6, starting transfers between devices, move(): lax.ppermute(value, 'plane', pairs)  16 us
    all_to_all x1, waiting for transfers between devices, per_device(): shared = lax.all_to_all(info, ('height', 'plane'), 0, 0, tiled=True)  7.3 us
    pallas_call x1, Pallas kernels, per_device(): pl.pallas_call(functools.partial(basis_kernel, counts), out_shape=(jax.Sh...  5.83 us
    ppermute x6, waiting for transfers between devices, move(): lax.ppermute(value, 'plane', pairs)  3.81 us
    all_to_all x1, starting transfers between devices, per_device(): shared = lax.all_to_all(info, ('height', 'plane'), 0, 0, tiled=True)  3.58 us
    ppermute x6, starting transfers between devices, per_device(): lax.ppermute(arr, 'height', [(h, (h + turn) % height) for h in range(heig...  1.29 us
    ppermute x6, waiting for transfers between devices, per_device(): lax.ppermute(arr, 'height', [(h, (h + turn) % height) for h in range(heig...  1.24 us
    pallas_call x1, Pallas kernels, per_device(): pl.pallas_call(combine_kernel, out_shape=(jax.ShapeDtypeStruct(cotangent....  1.05 us
  transfers between devices with their start and end apart: 13, of which 6 were waited for; matrix products, arithmetic and copies ran while one was open for 0% of the time, Pallas kernels for 0%

profile of v6, /device:TPU:0, one launch (start us, length us, event | category | flops | bytes accessed | tf_op | source)
XLA Modules:
  0.0 42.7 jit_solution(9643765042392766579)
XLA Ops:
  0.6 0.7 %pad_maximum_fusion.1 = f32[2,2,16]{2,1,0:T(2,128)S(1)} fusion(f32[2,1,16]{2,1,0:T(1,128)} %param.12, f32[2,1,16]{2,1,0:T(1,128)} %param.11), kind=kLoop, calls=%fused_computation.3 | loop fusion | flops 64 | bytes 512 | tf_op jit(solution)/shard_map/concatenate | solution.py:487
  1.3 0.8 %select_maximum_fusion.raw_ref = f32[136,128]{1,0:T(8,128)S(1)} fusion(f32[4,16]{1,0:T(4,128)S(1)} %bitcast.3, f32[128,128]{1,0:T(8,128)} %bitcast.2), kind=kLoop, calls=%fused_computation.1 | loop fusion | flops 52224 | bytes 135424 | tf_op jit(solution)/shard_map/concatenate | solution.py:489
  2.2 0.2 shard_map.121
  2.4 3.0 %collective-permute-start = (f32[136,128]{1,0:T(8,128)S(1)}, f32[136,128]{1,0:T(8,128)S(1)}, u32[]{:S(2)}, u32[]{:S(2)}) collective-permute-start(f32[136,128]{1,0:T(8,128)S(1)} %shard_map.121), channel_id=1, source_target_pairs={{0,1},{1,0},{2,3},{3,2},{4,5},{5,4},{6,7},{7,6},{8,9},{9,8},{10,11... | collective-permute-start | bytes 208904 | tf_op jit(solution)/shard_map/ppermute | solution.py:499
  5.4 2.3 %collective-permute-done = f32[136,128]{1,0:T(8,128)S(1)} collective-permute-done((f32[136,128]{1,0:T(8,128)S(1)}, f32[136,128]{1,0:T(8,128)S(1)}, u32[]{:S(2)}, u32[]{:S(2)}) %collective-permute-start) | collective-permute-done | bytes 69664 | tf_op jit(solution)/shard_map/ppermute | solution.py:499
  7.7 0.0 copy-start
  7.7 2.1 %collective-permute-start.1 = (f32[272,128]{1,0:T(8,128)S(1)}, f32[272,128]{1,0:T(8,128)S(1)}, u32[]{:S(2)}, u32[]{:S(2)}) collective-permute-start(f32[272,128]{1,0:T(8,128)S(1)} %pad_maximum_fusion.refs_0_), channel_id=1, source_target_pairs={{0,2},{1,3},{2,0},{3,1},{4,6},{5,7},{6,4},{7,5},{8,10},{9,11},{10,... | collective-permute-start | bytes 417800 | tf_op jit(solution)/shard_map/ppermute | solution.py:499
  9.9 1.6 %collective-permute-start.2 = (f32[272,128]{1,0:T(8,128)S(1)}, f32[272,128]{1,0:T(8,128)S(1)}, u32[]{:S(2)}, u32[]{:S(2)}) collective-permute-start(f32[272,128]{1,0:T(8,128)S(1)} %pad_maximum_fusion.refs_0_), channel_id=1, source_target_pairs={{0,4},{1,5},{2,6},{3,7},{8,12},{9,13},{10,14},{11,15},{4,0},{5,1},... | collective-permute-start | bytes 417800 | tf_op jit(solution)/shard_map/ppermute | solution.py:499
  11.4 0.7 %collective-permute-start.3 = (f32[272,128]{1,0:T(8,128)S(1)}, f32[272,128]{1,0:T(8,128)S(1)}, u32[]{:S(2)}, u32[]{:S(2)}) collective-permute-start(f32[272,128]{1,0:T(8,128)S(1)} %pad_maximum_fusion.refs_0_), channel_id=1, source_target_pairs={{4,8},{5,9},{6,10},{7,11},{8,4},{9,5},{10,6},{11,7},{20,24},{21,25... | collective-permute-start | bytes 417800 | tf_op jit(solution)/shard_map/ppermute | solution.py:499
  12.1 0.1 collective-permute-start.6
  12.2 0.7 %collective-permute-done.1.msg_ref.refs_1_ = f32[272,128]{1,0:T(8,128)S(1)} collective-permute-done((f32[272,128]{1,0:T(8,128)S(1)}, f32[272,128]{1,0:T(8,128)S(1)}, u32[]{:S(2)}, u32[]{:S(2)}) %collective-permute-start.1) | collective-permute-done | bytes 139296 | tf_op jit(solution)/shard_map/ppermute | solution.py:499
  12.9 5.6 %collective-permute-start.4 = (f32[272,128]{1,0:T(8,128)S(1)}, f32[272,128]{1,0:T(8,128)S(1)}, u32[]{:S(2)}, u32[]{:S(2)}) collective-permute-start(f32[272,128]{1,0:T(8,128)S(1)} %collective-permute-done.1.msg_ref.refs_1_), channel_id=1, source_target_pairs={{0,4},{1,5},{4,8},{5,9},{8,12},{9,13},{6,2},{7,3},{10,6},{11,7},{1... | collective-permute-start | bytes 417800 | tf_op jit(solution)/shard_map/ppermute | solution.py:499
  18.6 3.0 %collective-permute-start.5 = (f32[24,128]{1,0:T(8,128)S(1)}, f32[24,128]{1,0:T(8,128)S(1)}, u32[]{:S(2)}, u32[]{:S(2)}) collective-permute-start(f32[24,128]{1,0:T(8,128)S(1)} %shard_map.122), channel_id=1, source_target_pairs={{0,8},{4,12},{5,1},{9,5},{13,9},{2,6},{6,10},{10,14},{11,3},{15,7}... | collective-permute-start | bytes 36872 | tf_op jit(solution)/shard_map/ppermute | solution.py:499
  21.6 0.1 collective-permute-start.7
  21.7 0.5 %collective-permute-start.8 = (f32[272,128]{1,0:T(8,128)S(1)}, f32[272,128]{1,0:T(8,128)S(1)}, u32[]{:S(2)}, u32[]{:S(2)}) collective-permute-start(f32[272,128]{1,0:T(8,128)S(1)} %collective-permute-done.2.refs_2_), channel_id=1, source_target_pairs={{0,16},{16,0},{1,17},{17,1},{2,18},{18,2},{3,19},{19,3},{4,20},{20... | collective-permute-start | bytes 417800 | tf_op jit(solution)/shard_map/ppermute | solution.py:532
  22.2 0.8 %collective-permute-done.5.edge_ref = f32[24,128]{1,0:T(8,128)S(1)} collective-permute-done((f32[24,128]{1,0:T(8,128)S(1)}, f32[24,128]{1,0:T(8,128)S(1)}, u32[]{:S(2)}, u32[]{:S(2)}) %collective-permute-start.5) | collective-permute-done | bytes 12320 | tf_op jit(solution)/shard_map/ppermute | solution.py:499
  23.0 0.6 %collective-permute-start.11 = (f32[136,128]{1,0:T(8,128)S(1)}, f32[136,128]{1,0:T(8,128)S(1)}, u32[]{:S(2)}, u32[]{:S(2)}) collective-permute-start(f32[136,128]{1,0:T(8,128)S(1)} %shard_map.123.refs_5_), channel_id=1, source_target_pairs={{0,16},{16,0},{1,17},{17,1},{2,18},{18,2},{3,19},{19,3},{4,20},{20... | collective-permute-start | bytes 208904 | tf_op jit(solution)/shard_map/ppermute | solution.py:532
  23.6 0.1 collective-permute-start.10
  23.7 0.8 %collective-permute-done.11.refs_11_ = f32[136,128]{1,0:T(8,128)S(1)} collective-permute-done((f32[136,128]{1,0:T(8,128)S(1)}, f32[136,128]{1,0:T(8,128)S(1)}, u32[]{:S(2)}, u32[]{:S(2)}) %collective-permute-start.11) | collective-permute-done | bytes 69664 | tf_op jit(solution)/shard_map/ppermute | solution.py:532
  24.5 0.4 %collective-permute-done.10.refs_10_ = f32[272,128]{1,0:T(8,128)S(1)} collective-permute-done((f32[272,128]{1,0:T(8,128)S(1)}, f32[272,128]{1,0:T(8,128)S(1)}, u32[]{:S(2)}, u32[]{:S(2)}) %collective-permute-start.10) | collective-permute-done | bytes 139296 | tf_op jit(solution)/shard_map/ppermute | solution.py:532
  25.0 5.8 %shard_map.124 = (f32[12,128,128]{2,1,0:T(8,128)S(1)}, f32[32,4,128]{2,1,0:T(4,128)}) custom-call(f32[272,128]{1,0:T(8,128)S(1)} %pad_maximum_fusion.refs_0_, f32[272,128]{1,0:T(8,128)S(1)} %collective-permute-done.1.msg_ref.refs_1_, f32[272,128]{1,0:T(8,128)S(1)} %collective-permute-done.2.refs_2_, f32[272,128]{1,0:T(8,128)S(1)} %collective-permute-done.3.refs_3_, ...), custom_call_target="tpu_custom_call" | custom-call | tf_op jit(solution)/shard_map/pallas_call | solution.py:538
  30.8 3.6 %all-to-all-start = ((f32[32,4,128]{2,1,0:T(4,128)}), f32[32,4,128]{2,1,0:T(4,128)S(1)}, u32[]{:S(2)}, u32[]{:S(2)}) async-start(f32[32,4,128]{2,1,0:T(4,128)} %get-tuple-element.5), calls=%async_computation | async-start | bytes 131072 | tf_op jit(solution)/shard_map/all_to_all | solution.py:552
  34.4 7.3 %all-to-all-done.info_ref = f32[32,4,128]{2,1,0:T(4,128)S(1)} async-done(((f32[32,4,128]{2,1,0:T(4,128)}), f32[32,4,128]{2,1,0:T(4,128)S(1)}, u32[]{:S(2)}, u32[]{:S(2)}) %all-to-all-start) | async-done | bytes 65568 | tf_op jit(solution)/shard_map/all_to_all | solution.py:552
  41.7 1.0 %shard_map.125 = (f32[16,8,128]{2,1,0:T(8,128)}, f32[16,8,128]{2,1,0:T(8,128)}, f32[2,128]{1,0:T(2,128)}) custom-call(f32[32,4,128]{2,1,0:T(4,128)S(1)} %all-to-all-done.info_ref, f32[12,128,128]{2,1,0:T(8,128)S(1)} %get-tuple-element.6.fields_ref, s32[2,128]{1,0:T(2,128)S(1)} %fusion.owner_ref, s32[2,128]{1,0:T(2,128)S(1)} %get-tuple-element.7.place_ref), custom_call_target="tpu_custom_call" | custom-call | tf_op jit(solution)/shard_map/pallas_call | solution.py:560
  (26 shorter events, 0.1 us)
Async XLA Ops:
  2.4 5.3 %collective-permute-start = (f32[136,128]{1,0:T(8,128)S(1)}, f32[136,128]{1,0:T(8,128)S(1)}, u32[]{:S(2)}, u32[]{:S(2)}) collective-permute-start(f32[136,128]{1,0:T(8,128)S(1)} %shard_map.121), channel_id=1, source_target_pairs={{0,1},{1,0},{2,3},{3,2},{4,5},{5,4},{6,7},{7,6},{8,9},{9,8},{10,11... | collective-permute-start | bytes 208904 | tf_op jit(solution)/shard_map/ppermute | solution.py:499
  7.7 17.2 %copy-start.1 = (bf16[256,256]{1,0:T(8,128)(2,1)S(1)}, bf16[256,256]{1,0:T(8,128)(2,1)}, u32[]{:S(2)}) copy-start(bf16[256,256]{1,0:T(8,128)(2,1)} %constant.77.clone.refs_15_) | copy-start | bytes 393220
  7.7 17.2 %copy-start.4 = (f32[8,8,128]{2,1,0:T(8,128)S(1)}, f32[8,8,128]{2,1,0:T(8,128)}, u32[]{:S(2)}) copy-start(f32[8,8,128]{2,1,0:T(8,128)} %constant.79.clone.refs_17_) | copy-start | bytes 98308
  7.7 17.2 %copy-start = (bf16[256,256]{1,0:T(8,128)(2,1)S(1)}, bf16[256,256]{1,0:T(8,128)(2,1)}, u32[]{:S(2)}) copy-start(bf16[256,256]{1,0:T(8,128)(2,1)} %constant.76.clone.refs_14_) | copy-start | bytes 393220
  7.7 5.1 %collective-permute-start.1 = (f32[272,128]{1,0:T(8,128)S(1)}, f32[272,128]{1,0:T(8,128)S(1)}, u32[]{:S(2)}, u32[]{:S(2)}) collective-permute-start(f32[272,128]{1,0:T(8,128)S(1)} %pad_maximum_fusion.refs_0_), channel_id=1, source_target_pairs={{0,2},{1,3},{2,0},{3,1},{4,6},{5,7},{6,4},{7,5},{8,10},{9,11},{10,... | collective-permute-start | bytes 417800 | tf_op jit(solution)/shard_map/ppermute | solution.py:499
  9.9 11.7 %collective-permute-start.2 = (f32[272,128]{1,0:T(8,128)S(1)}, f32[272,128]{1,0:T(8,128)S(1)}, u32[]{:S(2)}, u32[]{:S(2)}) collective-permute-start(f32[272,128]{1,0:T(8,128)S(1)} %pad_maximum_fusion.refs_0_), channel_id=1, source_target_pairs={{0,4},{1,5},{2,6},{3,7},{8,12},{9,13},{10,14},{11,15},{4,0},{5,1},... | collective-permute-start | bytes 417800 | tf_op jit(solution)/shard_map/ppermute | solution.py:499
  11.4 10.2 %collective-permute-start.3 = (f32[272,128]{1,0:T(8,128)S(1)}, f32[272,128]{1,0:T(8,128)S(1)}, u32[]{:S(2)}, u32[]{:S(2)}) collective-permute-start(f32[272,128]{1,0:T(8,128)S(1)} %pad_maximum_fusion.refs_0_), channel_id=1, source_target_pairs={{4,8},{5,9},{6,10},{7,11},{8,4},{9,5},{10,6},{11,7},{20,24},{21,25... | collective-permute-start | bytes 417800 | tf_op jit(solution)/shard_map/ppermute | solution.py:499
  12.1 10.9 %collective-permute-start.6 = (f32[272,128]{1,0:T(8,128)S(1)}, f32[272,128]{1,0:T(8,128)S(1)}, u32[]{:S(2)}, u32[]{:S(2)}) collective-permute-start(f32[272,128]{1,0:T(8,128)S(1)} %pad_maximum_fusion.refs_0_), channel_id=1, source_target_pairs={{0,16},{16,0},{1,17},{17,1},{2,18},{18,2},{3,19},{19,3},{4,20},{20... | collective-permute-start | bytes 417800 | tf_op jit(solution)/shard_map/ppermute | solution.py:532
  12.9 10.7 %collective-permute-start.4 = (f32[272,128]{1,0:T(8,128)S(1)}, f32[272,128]{1,0:T(8,128)S(1)}, u32[]{:S(2)}, u32[]{:S(2)}) collective-permute-start(f32[272,128]{1,0:T(8,128)S(1)} %collective-permute-done.1.msg_ref.refs_1_), channel_id=1, source_target_pairs={{0,4},{1,5},{4,8},{5,9},{8,12},{9,13},{6,2},{7,3},{10,6},{11,7},{1... | collective-permute-start | bytes 417800 | tf_op jit(solution)/shard_map/ppermute | solution.py:499
  18.5 5.1 %copy-start.6 = (s32[2,128]{1,0:T(2,128)S(1)}, s32[2,128]{1,0:T(2,128)}, u32[]{:S(2)}) copy-start(s32[2,128]{1,0:T(2,128)} %param.13) | copy-start | bytes 3076
  18.5 6.4 %copy-start.5 = (bf16[48,128]{1,0:T(8,128)(2,1)S(1)}, bf16[48,128]{1,0:T(8,128)(2,1)}, u32[]{:S(2)}) copy-start(bf16[48,128]{1,0:T(8,128)(2,1)} %constant.75.clone.refs_13_) | copy-start | bytes 36868
  18.6 6.4 %copy-start.2 = (bf16[192,128]{1,0:T(8,128)(2,1)S(1)}, bf16[192,128]{1,0:T(8,128)(2,1)}, u32[]{:S(2)}) copy-start(bf16[192,128]{1,0:T(8,128)(2,1)} %constant.74.clone.refs_12_) | copy-start | bytes 147460
  18.6 6.4 %copy-start.3 = (f32[8,8,128]{2,1,0:T(8,128)S(1)}, f32[8,8,128]{2,1,0:T(8,128)}, u32[]{:S(2)}) copy-start(f32[8,8,128]{2,1,0:T(8,128)} %constant.78.clone.refs_16_) | copy-start | bytes 98308
  18.6 4.4 %collective-permute-start.5 = (f32[24,128]{1,0:T(8,128)S(1)}, f32[24,128]{1,0:T(8,128)S(1)}, u32[]{:S(2)}, u32[]{:S(2)}) collective-permute-start(f32[24,128]{1,0:T(8,128)S(1)} %shard_map.122), channel_id=1, source_target_pairs={{0,8},{4,12},{5,1},{9,5},{13,9},{2,6},{6,10},{10,14},{11,3},{15,7}... | collective-permute-start | bytes 36872 | tf_op jit(solution)/shard_map/ppermute | solution.py:499
  21.6 2.9 %collective-permute-start.7 = (f32[272,128]{1,0:T(8,128)S(1)}, f32[272,128]{1,0:T(8,128)S(1)}, u32[]{:S(2)}, u32[]{:S(2)}) collective-permute-start(f32[272,128]{1,0:T(8,128)S(1)} %collective-permute-done.1.msg_ref.refs_1_), channel_id=1, source_target_pairs={{0,16},{16,0},{1,17},{17,1},{2,18},{18,2},{3,19},{19,3},{4,20},{20... | collective-permute-start | bytes 417800 | tf_op jit(solution)/shard_map/ppermute | solution.py:532
  21.7 2.8 %collective-permute-start.8 = (f32[272,128]{1,0:T(8,128)S(1)}, f32[272,128]{1,0:T(8,128)S(1)}, u32[]{:S(2)}, u32[]{:S(2)}) collective-permute-start(f32[272,128]{1,0:T(8,128)S(1)} %collective-permute-done.2.refs_2_), channel_id=1, source_target_pairs={{0,16},{16,0},{1,17},{17,1},{2,18},{18,2},{3,19},{19,3},{4,20},{20... | collective-permute-start | bytes 417800 | tf_op jit(solution)/shard_map/ppermute | solution.py:532
  23.0 1.5 %collective-permute-start.9 = (f32[272,128]{1,0:T(8,128)S(1)}, f32[272,128]{1,0:T(8,128)S(1)}, u32[]{:S(2)}, u32[]{:S(2)}) collective-permute-start(f32[272,128]{1,0:T(8,128)S(1)} %collective-permute-done.3.refs_3_), channel_id=1, source_target_pairs={{0,16},{16,0},{1,17},{17,1},{2,18},{18,2},{3,19},{19,3},{4,20},{20... | collective-permute-start | bytes 417800 | tf_op jit(solution)/shard_map/ppermute | solution.py:532
  23.0 1.5 %collective-permute-start.11 = (f32[136,128]{1,0:T(8,128)S(1)}, f32[136,128]{1,0:T(8,128)S(1)}, u32[]{:S(2)}, u32[]{:S(2)}) collective-permute-start(f32[136,128]{1,0:T(8,128)S(1)} %shard_map.123.refs_5_), channel_id=1, source_target_pairs={{0,16},{16,0},{1,17},{17,1},{2,18},{18,2},{3,19},{19,3},{4,20},{20... | collective-permute-start | bytes 208904 | tf_op jit(solution)/shard_map/ppermute | solution.py:532
  23.6 1.4 %collective-permute-start.10 = (f32[272,128]{1,0:T(8,128)S(1)}, f32[272,128]{1,0:T(8,128)S(1)}, u32[]{:S(2)}, u32[]{:S(2)}) collective-permute-start(f32[272,128]{1,0:T(8,128)S(1)} %collective-permute-done.4.refs_4_), channel_id=1, source_target_pairs={{0,16},{16,0},{1,17},{17,1},{2,18},{18,2},{3,19},{19,3},{4,20},{20... | collective-permute-start | bytes 417800 | tf_op jit(solution)/shard_map/ppermute | solution.py:532
  30.8 10.9 %all-to-all-start = ((f32[32,4,128]{2,1,0:T(4,128)}), f32[32,4,128]{2,1,0:T(4,128)S(1)}, u32[]{:S(2)}, u32[]{:S(2)}) async-start(f32[32,4,128]{2,1,0:T(4,128)} %get-tuple-element.5), calls=%async_computation | async-start | bytes 131072 | tf_op jit(solution)/shard_map/all_to_all | solution.py:552

commit v7 on v6

--- a/solution.py
+++ b/solution.py
@@ -137,7 +137,7 @@
 
 def basis_kernel(counts, *refs):
     height, plane = counts
-    n_in = 6 * height
+    n_in = 5 * height
     msgs = refs[:n_in]
     face_ref, ends_ref, row_a_ref, row_b_ref, omega_ref, quot_ref = refs[n_in : n_in + 6]
     fields_ref, info_ref = refs[n_in + 6 : n_in + 8]
@@ -175,19 +175,21 @@
         jnp.where(member == 0, 0, after + jnp.bitwise_xor(member, 3)),
         jnp.where(member == GROUP - 1, 3 * GROUP + 1, before + jnp.bitwise_xor(member, 3)),
     )
+    def slots(base, flips):
+        return [base + jnp.bitwise_xor(member, flip) for flip in flips]
+
     roles = (
-        (here, (0, 1)),
-        (here, (2, 3)),
-        (jnp.where(even, after, before), (0, 1)),
-        (jnp.where(even, before, after), (0, 1)),
-        (jnp.where(early, before, after), (2, 3)),
-        (lone, (None,)),
+        slots(here, (0, 1)),
+        slots(here, (2, 3)),
+        slots(jnp.where(even, after, before), (0, 1)),
+        slots(jnp.where(even, before, after), (0, 1)),
+        [*slots(jnp.where(early, before, after), (2, 3)), lone],
     )
     for turn in range(height):
         block = lax.rem(height_pos - turn + height, height)
-        for msg, (base, owners) in zip(msgs[turn * len(roles) :], roles):
-            for piece, flip in enumerate(owners):
-                stage(msg, piece, base if flip is None else base + jnp.bitwise_xor(member, flip), block)
+        for msg, places in zip(msgs[turn * len(roles) :], roles):
+            for piece, slot in enumerate(places):
+                stage(msg, piece, slot, block)
 
     def face_at(slot, width_node):
         return slot, pl.ds(width_node, depth, stride=8)
@@ -523,10 +525,10 @@
         out_shape=jax.ShapeDtypeStruct((rows, span), F32),
         in_specs=[vmem],
         out_specs=vmem,
-        cost_estimate=pl.CostEstimate(flops=1000000, bytes_accessed=1000000, transcendentals=0),
+        cost_estimate=pl.CostEstimate(flops=100000000, bytes_accessed=3000000, transcendentals=0),
         compiler_params=pltpu.CompilerParams(vmem_limit_bytes=4 * 2**20),
     )(edge)
-    sent = (half, other, pair, cross, side, lone)
+    sent = (half, other, pair, cross, jnp.concatenate([side, lone], axis=0))
     operands = list(sent)
     for turn in range(1, height):
         operands += [lax.ppermute(arr, "height", [(h, (h + turn) % height) for h in range(height)]) for arr in sent]

time: 43.1 us -> 42.7 us (level)
    ppermute x6 -> x5, waiting for transfers between devices: 1.24 us -> 1.04 us  [per_device(): lax.ppermute(arr, 'height', [(h, (h + turn) % height) for h in range(heig...]
    ppermute x6 -> x5, starting transfers between devices: 1.29 us -> 1.21 us  [per_device(): lax.ppermute(arr, 'height', [(h, (h + turn) % height) for h in range(heig...]
  transfers between devices with their start and end apart: 13 -> 12, of which waited for: 6 -> 6; matrix products, arithmetic and copies ran while one was open for 0% -> 0% of each run, Pallas kernels for 0% -> 0%
where the time goes in v7:
time: 42.7 us; the launch traced here: 42.5 us
  starting transfers between devices  20.6 us (48%)
  waiting for transfers between devices  12.1 us (28%)
  Pallas kernels  7.19 us (17%)
  other arithmetic  1.61 us (4%)
  between operations  0.83 us (2%)
    ppermute x6, starting transfers between devices, move(): lax.ppermute(value, 'plane', pairs)  15.8 us
    all_to_all x1, waiting for transfers between devices, per_device(): shared = lax.all_to_all(info, ('height', 'plane'), 0, 0, tiled=True)  7.3 us
    pallas_call x1, Pallas kernels, per_device(): pl.pallas_call(functools.partial(basis_kernel, counts), out_shape=(jax.Sh...  5.89 us
    ppermute x6, waiting for transfers between devices, move(): lax.ppermute(value, 'plane', pairs)  3.81 us
    all_to_all x1, starting transfers between devices, per_device(): shared = lax.all_to_all(info, ('height', 'plane'), 0, 0, tiled=True)  3.6 us
    ppermute x5, starting transfers between devices, per_device(): lax.ppermute(arr, 'height', [(h, (h + turn) % height) for h in range(heig...  1.21 us
    pallas_call x1, Pallas kernels, per_device(): pl.pallas_call(combine_kernel, out_shape=(jax.ShapeDtypeStruct(cotangent....  1.05 us
    ppermute x5, waiting for transfers between devices, per_device(): lax.ppermute(arr, 'height', [(h, (h + turn) % height) for h in range(heig...  1.04 us
  transfers between devices with their start and end apart: 12, of which 6 were waited for; matrix products, arithmetic and copies ran while one was open for 0% of the time, Pallas kernels for 0%

profile of v7, /device:TPU:0, one launch (start us, length us, event | category | flops | bytes accessed | tf_op | source)
XLA Modules:
  0.0 42.5 jit_solution(2460415355281520581)
XLA Ops:
  0.6 0.7 %pad_maximum_fusion.2 = f32[2,2,16]{2,1,0:T(2,128)S(1)} fusion(f32[2,1,16]{2,1,0:T(1,128)} %param.12, f32[2,1,16]{2,1,0:T(1,128)} %param.11), kind=kLoop, calls=%fused_computation.4 | loop fusion | flops 64 | bytes 512 | tf_op jit(solution)/shard_map/concatenate | solution.py:489
  1.3 0.8 %select_maximum_fusion.raw_ref = f32[136,128]{1,0:T(8,128)S(1)} fusion(f32[4,16]{1,0:T(4,128)S(1)} %bitcast.3, f32[128,128]{1,0:T(8,128)} %bitcast.2), kind=kLoop, calls=%fused_computation.2 | loop fusion | flops 52224 | bytes 135424 | tf_op jit(solution)/shard_map/concatenate | solution.py:491
  2.2 0.2 shard_map.121
  2.4 3.0 %collective-permute-start = (f32[136,128]{1,0:T(8,128)S(1)}, f32[136,128]{1,0:T(8,128)S(1)}, u32[]{:S(2)}, u32[]{:S(2)}) collective-permute-start(f32[136,128]{1,0:T(8,128)S(1)} %shard_map.121), channel_id=1, source_target_pairs={{0,1},{1,0},{2,3},{3,2},{4,5},{5,4},{6,7},{7,6},{8,9},{9,8},{10,11... | collective-permute-start | bytes 208904 | tf_op jit(solution)/shard_map/ppermute | solution.py:501
  5.4 2.3 %collective-permute-done = f32[136,128]{1,0:T(8,128)S(1)} collective-permute-done((f32[136,128]{1,0:T(8,128)S(1)}, f32[136,128]{1,0:T(8,128)S(1)}, u32[]{:S(2)}, u32[]{:S(2)}) %collective-permute-start) | collective-permute-done | bytes 69664 | tf_op jit(solution)/shard_map/ppermute | solution.py:501
  7.7 2.1 %collective-permute-start.1 = (f32[272,128]{1,0:T(8,128)S(1)}, f32[272,128]{1,0:T(8,128)S(1)}, u32[]{:S(2)}, u32[]{:S(2)}) collective-permute-start(f32[272,128]{1,0:T(8,128)S(1)} %pad_maximum_fusion.1.refs_0_), channel_id=1, source_target_pairs={{0,2},{1,3},{2,0},{3,1},{4,6},{5,7},{6,4},{7,5},{8,10},{9,11},{10,... | collective-permute-start | bytes 417800 | tf_op jit(solution)/shard_map/ppermute | solution.py:501
  9.8 1.6 %collective-permute-start.2 = (f32[272,128]{1,0:T(8,128)S(1)}, f32[272,128]{1,0:T(8,128)S(1)}, u32[]{:S(2)}, u32[]{:S(2)}) collective-permute-start(f32[272,128]{1,0:T(8,128)S(1)} %pad_maximum_fusion.1.refs_0_), channel_id=1, source_target_pairs={{0,4},{1,5},{2,6},{3,7},{8,12},{9,13},{10,14},{11,15},{4,0},{5,1},... | collective-permute-start | bytes 417800 | tf_op jit(solution)/shard_map/ppermute | solution.py:501
  11.4 0.7 %collective-permute-start.3 = (f32[272,128]{1,0:T(8,128)S(1)}, f32[272,128]{1,0:T(8,128)S(1)}, u32[]{:S(2)}, u32[]{:S(2)}) collective-permute-start(f32[272,128]{1,0:T(8,128)S(1)} %pad_maximum_fusion.1.refs_0_), channel_id=1, source_target_pairs={{4,8},{5,9},{6,10},{7,11},{8,4},{9,5},{10,6},{11,7},{20,24},{21,25... | collective-permute-start | bytes 417800 | tf_op jit(solution)/shard_map/ppermute | solution.py:501
  12.1 0.8 %collective-permute-done.1.msg_ref.refs_1_ = f32[272,128]{1,0:T(8,128)S(1)} collective-permute-done((f32[272,128]{1,0:T(8,128)S(1)}, f32[272,128]{1,0:T(8,128)S(1)}, u32[]{:S(2)}, u32[]{:S(2)}) %collective-permute-start.1) | collective-permute-done | bytes 139296 | tf_op jit(solution)/shard_map/ppermute | solution.py:501
  12.9 5.5 %collective-permute-start.4 = (f32[272,128]{1,0:T(8,128)S(1)}, f32[272,128]{1,0:T(8,128)S(1)}, u32[]{:S(2)}, u32[]{:S(2)}) collective-permute-start(f32[272,128]{1,0:T(8,128)S(1)} %collective-permute-done.1.msg_ref.refs_1_), channel_id=1, source_target_pairs={{0,4},{1,5},{4,8},{5,9},{8,12},{9,13},{6,2},{7,3},{10,6},{11,7},{1... | collective-permute-start | bytes 417800 | tf_op jit(solution)/shard_map/ppermute | solution.py:501
  18.4 2.9 %collective-permute-start.5 = (f32[24,128]{1,0:T(8,128)S(1)}, f32[24,128]{1,0:T(8,128)S(1)}, u32[]{:S(2)}, u32[]{:S(2)}) collective-permute-start(f32[24,128]{1,0:T(8,128)S(1)} %shard_map.122), channel_id=1, source_target_pairs={{0,8},{4,12},{5,1},{9,5},{13,9},{2,6},{6,10},{10,14},{11,3},{15,7}... | collective-permute-start | bytes 36872 | tf_op jit(solution)/shard_map/ppermute | solution.py:501
  21.4 0.1 collective-permute-start.6
  21.5 0.5 %collective-permute-start.7 = (f32[272,128]{1,0:T(8,128)S(1)}, f32[272,128]{1,0:T(8,128)S(1)}, u32[]{:S(2)}, u32[]{:S(2)}) collective-permute-start(f32[272,128]{1,0:T(8,128)S(1)} %collective-permute-done.1.msg_ref.refs_1_), channel_id=1, source_target_pairs={{0,16},{16,0},{1,17},{17,1},{2,18},{18,2},{3,19},{19,3},{4,20},{20... | collective-permute-start | bytes 417800 | tf_op jit(solution)/shard_map/ppermute | solution.py:534
  22.0 0.1 collective-permute-start.8
  22.1 0.7 %collective-permute-done.5.edge_ref = f32[24,128]{1,0:T(8,128)S(1)} collective-permute-done((f32[24,128]{1,0:T(8,128)S(1)}, f32[24,128]{1,0:T(8,128)S(1)}, u32[]{:S(2)}, u32[]{:S(2)}) %collective-permute-start.5) | collective-permute-done | bytes 12320 | tf_op jit(solution)/shard_map/ppermute | solution.py:501
  22.8 0.0 copy-start
  22.8 0.0 copy-start.1
  22.9 0.6 %collective-permute-start.10 = (f32[408,128]{1,0:T(8,128)S(1)}, f32[408,128]{1,0:T(8,128)S(1)}, u32[]{:S(2)}, u32[]{:S(2)}) collective-permute-start(f32[408,128]{1,0:T(8,128)S(1)} %pad_maximum_fusion.refs_4_), channel_id=1, source_target_pairs={{0,16},{16,0},{1,17},{17,1},{2,18},{18,2},{3,19},{19,3},{4,20},{20... | collective-permute-start | bytes 626696 | tf_op jit(solution)/shard_map/ppermute | solution.py:534
  23.5 0.6 %collective-permute-done.9.refs_8_ = f32[272,128]{1,0:T(8,128)S(1)} collective-permute-done((f32[272,128]{1,0:T(8,128)S(1)}, f32[272,128]{1,0:T(8,128)S(1)}, u32[]{:S(2)}, u32[]{:S(2)}) %collective-permute-start.9) | collective-permute-done | bytes 139296 | tf_op jit(solution)/shard_map/ppermute | solution.py:534
  24.1 0.4 collective-permute-done.10.refs_9_
  24.6 5.9 %shard_map.124 = (f32[12,128,128]{2,1,0:T(8,128)S(1)}, f32[32,4,128]{2,1,0:T(4,128)}) custom-call(f32[272,128]{1,0:T(8,128)S(1)} %pad_maximum_fusion.1.refs_0_, f32[272,128]{1,0:T(8,128)S(1)} %collective-permute-done.1.msg_ref.refs_1_, f32[272,128]{1,0:T(8,128)S(1)} %collective-permute-done.2.refs_2_, f32[272,128]{1,0:T(8,128)S(1)} %collective-permute-done.3.refs_3_, ...), custom_call_target="tpu_custom_call" | custom-call | tf_op jit(solution)/shard_map/pallas_call | solution.py:540
  30.5 3.6 %all-to-all-start = ((f32[32,4,128]{2,1,0:T(4,128)}), f32[32,4,128]{2,1,0:T(4,128)S(1)}, u32[]{:S(2)}, u32[]{:S(2)}) async-start(f32[32,4,128]{2,1,0:T(4,128)} %get-tuple-element.5), calls=%async_computation | async-start | bytes 131072 | tf_op jit(solution)/shard_map/all_to_all | solution.py:554
  34.1 7.3 %all-to-all-done.info_ref = f32[32,4,128]{2,1,0:T(4,128)S(1)} async-done(((f32[32,4,128]{2,1,0:T(4,128)}), f32[32,4,128]{2,1,0:T(4,128)S(1)}, u32[]{:S(2)}, u32[]{:S(2)}) %all-to-all-start) | async-done | bytes 65568 | tf_op jit(solution)/shard_map/all_to_all | solution.py:554
  41.4 1.0 %shard_map.125 = (f32[16,8,128]{2,1,0:T(8,128)}, f32[16,8,128]{2,1,0:T(8,128)}, f32[2,128]{1,0:T(2,128)}) custom-call(f32[32,4,128]{2,1,0:T(4,128)S(1)} %all-to-all-done.info_ref, f32[12,128,128]{2,1,0:T(8,128)S(1)} %get-tuple-element.6.fields_ref, s32[2,128]{1,0:T(2,128)S(1)} %fusion.owner_ref, s32[2,128]{1,0:T(2,128)S(1)} %get-tuple-element.7.place_ref), custom_call_target="tpu_custom_call" | custom-call | tf_op jit(solution)/shard_map/pallas_call | solution.py:562
  (25 shorter events, 0.1 us)
Async XLA Ops:
  2.4 5.3 %collective-permute-start = (f32[136,128]{1,0:T(8,128)S(1)}, f32[136,128]{1,0:T(8,128)S(1)}, u32[]{:S(2)}, u32[]{:S(2)}) collective-permute-start(f32[136,128]{1,0:T(8,128)S(1)} %shard_map.121), channel_id=1, source_target_pairs={{0,1},{1,0},{2,3},{3,2},{4,5},{5,4},{6,7},{7,6},{8,9},{9,8},{10,11... | collective-permute-start | bytes 208904 | tf_op jit(solution)/shard_map/ppermute | solution.py:501
  7.7 5.1 %collective-permute-start.1 = (f32[272,128]{1,0:T(8,128)S(1)}, f32[272,128]{1,0:T(8,128)S(1)}, u32[]{:S(2)}, u32[]{:S(2)}) collective-permute-start(f32[272,128]{1,0:T(8,128)S(1)} %pad_maximum_fusion.1.refs_0_), channel_id=1, source_target_pairs={{0,2},{1,3},{2,0},{3,1},{4,6},{5,7},{6,4},{7,5},{8,10},{9,11},{10,... | collective-permute-start | bytes 417800 | tf_op jit(solution)/shard_map/ppermute | solution.py:501
  9.8 11.6 %collective-permute-start.2 = (f32[272,128]{1,0:T(8,128)S(1)}, f32[272,128]{1,0:T(8,128)S(1)}, u32[]{:S(2)}, u32[]{:S(2)}) collective-permute-start(f32[272,128]{1,0:T(8,128)S(1)} %pad_maximum_fusion.1.refs_0_), channel_id=1, source_target_pairs={{0,4},{1,5},{2,6},{3,7},{8,12},{9,13},{10,14},{11,15},{4,0},{5,1},... | collective-permute-start | bytes 417800 | tf_op jit(solution)/shard_map/ppermute | solution.py:501
  11.4 10.5 %collective-permute-start.3 = (f32[272,128]{1,0:T(8,128)S(1)}, f32[272,128]{1,0:T(8,128)S(1)}, u32[]{:S(2)}, u32[]{:S(2)}) collective-permute-start(f32[272,128]{1,0:T(8,128)S(1)} %pad_maximum_fusion.1.refs_0_), channel_id=1, source_target_pairs={{4,8},{5,9},{6,10},{7,11},{8,4},{9,5},{10,6},{11,7},{20,24},{21,25... | collective-permute-start | bytes 417800 | tf_op jit(solution)/shard_map/ppermute | solution.py:501
  12.9 10.0 %collective-permute-start.4 = (f32[272,128]{1,0:T(8,128)S(1)}, f32[272,128]{1,0:T(8,128)S(1)}, u32[]{:S(2)}, u32[]{:S(2)}) collective-permute-start(f32[272,128]{1,0:T(8,128)S(1)} %collective-permute-done.1.msg_ref.refs_1_), channel_id=1, source_target_pairs={{0,4},{1,5},{4,8},{5,9},{8,12},{9,13},{6,2},{7,3},{10,6},{11,7},{1... | collective-permute-start | bytes 417800 | tf_op jit(solution)/shard_map/ppermute | solution.py:501
  18.4 4.3 %collective-permute-start.5 = (f32[24,128]{1,0:T(8,128)S(1)}, f32[24,128]{1,0:T(8,128)S(1)}, u32[]{:S(2)}, u32[]{:S(2)}) collective-permute-start(f32[24,128]{1,0:T(8,128)S(1)} %shard_map.122), channel_id=1, source_target_pairs={{0,8},{4,12},{5,1},{9,5},{13,9},{2,6},{6,10},{10,14},{11,3},{15,7}... | collective-permute-start | bytes 36872 | tf_op jit(solution)/shard_map/ppermute | solution.py:501
  21.4 2.1 %collective-permute-start.6 = (f32[272,128]{1,0:T(8,128)S(1)}, f32[272,128]{1,0:T(8,128)S(1)}, u32[]{:S(2)}, u32[]{:S(2)}) collective-permute-start(f32[272,128]{1,0:T(8,128)S(1)} %pad_maximum_fusion.1.refs_0_), channel_id=1, source_target_pairs={{0,16},{16,0},{1,17},{17,1},{2,18},{18,2},{3,19},{19,3},{4,20},{20... | collective-permute-start | bytes 417800 | tf_op jit(solution)/shard_map/ppermute | solution.py:534
  21.5 2.0 %collective-permute-start.7 = (f32[272,128]{1,0:T(8,128)S(1)}, f32[272,128]{1,0:T(8,128)S(1)}, u32[]{:S(2)}, u32[]{:S(2)}) collective-permute-start(f32[272,128]{1,0:T(8,128)S(1)} %collective-permute-done.1.msg_ref.refs_1_), channel_id=1, source_target_pairs={{0,16},{16,0},{1,17},{17,1},{2,18},{18,2},{3,19},{19,3},{4,20},{20... | collective-permute-start | bytes 417800 | tf_op jit(solution)/shard_map/ppermute | solution.py:534
  22.0 1.6 %collective-permute-start.8 = (f32[272,128]{1,0:T(8,128)S(1)}, f32[272,128]{1,0:T(8,128)S(1)}, u32[]{:S(2)}, u32[]{:S(2)}) collective-permute-start(f32[272,128]{1,0:T(8,128)S(1)} %collective-permute-done.2.refs_2_), channel_id=1, source_target_pairs={{0,16},{16,0},{1,17},{17,1},{2,18},{18,2},{3,19},{19,3},{4,20},{20... | collective-permute-start | bytes 417800 | tf_op jit(solution)/shard_map/ppermute | solution.py:534
  22.8 1.4 %collective-permute-start.9 = (f32[272,128]{1,0:T(8,128)S(1)}, f32[272,128]{1,0:T(8,128)S(1)}, u32[]{:S(2)}, u32[]{:S(2)}) collective-permute-start(f32[272,128]{1,0:T(8,128)S(1)} %collective-permute-done.3.refs_3_), channel_id=1, source_target_pairs={{0,16},{16,0},{1,17},{17,1},{2,18},{18,2},{3,19},{19,3},{4,20},{20... | collective-permute-start | bytes 417800 | tf_op jit(solution)/shard_map/ppermute | solution.py:534
  22.8 0.7 %copy-start.6 = (s32[2,128]{1,0:T(2,128)S(1)}, s32[2,128]{1,0:T(2,128)}, u32[]{:S(2)}) copy-start(s32[2,128]{1,0:T(2,128)} %param.13) | copy-start | bytes 3076
  22.8 1.8 %copy-start = (bf16[256,256]{1,0:T(8,128)(2,1)S(1)}, bf16[256,256]{1,0:T(8,128)(2,1)}, u32[]{:S(2)}) copy-start(bf16[256,256]{1,0:T(8,128)(2,1)} %constant.76.clone.refs_12_) | copy-start | bytes 393220
  22.8 1.8 %copy-start.1 = (bf16[256,256]{1,0:T(8,128)(2,1)S(1)}, bf16[256,256]{1,0:T(8,128)(2,1)}, u32[]{:S(2)}) copy-start(bf16[256,256]{1,0:T(8,128)(2,1)} %constant.77.clone.refs_13_) | copy-start | bytes 393220
  22.8 1.7 %copy-start.2 = (bf16[192,128]{1,0:T(8,128)(2,1)S(1)}, bf16[192,128]{1,0:T(8,128)(2,1)}, u32[]{:S(2)}) copy-start(bf16[192,128]{1,0:T(8,128)(2,1)} %constant.74.clone.refs_10_) | copy-start | bytes 147460
  22.8 1.7 %copy-start.3 = (f32[8,8,128]{2,1,0:T(8,128)S(1)}, f32[8,8,128]{2,1,0:T(8,128)}, u32[]{:S(2)}) copy-start(f32[8,8,128]{2,1,0:T(8,128)} %constant.78.clone.refs_14_) | copy-start | bytes 98308
  22.8 1.7 %copy-start.4 = (f32[8,8,128]{2,1,0:T(8,128)S(1)}, f32[8,8,128]{2,1,0:T(8,128)}, u32[]{:S(2)}) copy-start(f32[8,8,128]{2,1,0:T(8,128)} %constant.79.clone.refs_15_) | copy-start | bytes 98308
  22.9 1.7 %copy-start.5 = (bf16[48,128]{1,0:T(8,128)(2,1)S(1)}, bf16[48,128]{1,0:T(8,128)(2,1)}, u32[]{:S(2)}) copy-start(bf16[48,128]{1,0:T(8,128)(2,1)} %constant.75.clone.refs_11_) | copy-start | bytes 36868
  22.9 1.6 %collective-permute-start.10 = (f32[408,128]{1,0:T(8,128)S(1)}, f32[408,128]{1,0:T(8,128)S(1)}, u32[]{:S(2)}, u32[]{:S(2)}) collective-permute-start(f32[408,128]{1,0:T(8,128)S(1)} %pad_maximum_fusion.refs_4_), channel_id=1, source_target_pairs={{0,16},{16,0},{1,17},{17,1},{2,18},{18,2},{3,19},{19,3},{4,20},{20... | collective-permute-start | bytes 626696 | tf_op jit(solution)/shard_map/ppermute | solution.py:534
  30.5 10.9 %all-to-all-start = ((f32[32,4,128]{2,1,0:T(4,128)}), f32[32,4,128]{2,1,0:T(4,128)S(1)}, u32[]{:S(2)}, u32[]{:S(2)}) async-start(f32[32,4,128]{2,1,0:T(4,128)} %get-tuple-element.5), calls=%async_computation | async-start | bytes 131072 | tf_op jit(solution)/shard_map/all_to_all | solution.py:554

commit v8 on v7

--- a/solution.py
+++ b/solution.py
@@ -95,16 +95,16 @@
     return jnp.concatenate(planes, axis=0)
 
 
-def pack_kernel(shape, raw_ref, out_ref):
+def pack_kernel(shape, cot_ref, lines_ref, out_ref):
     depth, elems, parts = shape
-    span = raw_ref.shape[1]
+    span = lines_ref.shape[1]
     spread = (lax.broadcasted_iota(jnp.int32, (parts, span), 1) // 8 == lax.broadcasted_iota(jnp.int32, (parts, span), 0)).astype(F32)
-    coef = raw_ref[depth * 8 :, :parts]
+    coef = lines_ref[:, :parts]
     pair = [coef[2 * e : 2 * e + 1] * (1.0 / INV_STEP) for e in range(elems)] + [coef[2 * e + 1 : 2 * e + 2] for e in range(elems)]
     coef = jnp.concatenate([*pair, coef[2 * elems :]], axis=0)
     coef = jnp.dot(coef, spread, precision=HIGHEST, preferred_element_type=F32)
     heavy = jnp.concatenate([jnp.broadcast_to(coef[elems + e : elems + e + 1], (64, span)) for e in range(elems)], axis=0)
-    value = join_depth(join_span(heavy * raw_ref[: depth * 8, :]))
+    value = join_depth(join_span(heavy * cot_ref[...].reshape(depth * 8, span)))
     out_ref[: depth * 8, :] = value
     out_ref[depth * 8 :, :] = coef
 
@@ -488,14 +488,13 @@
     rows = depth * 8 + coef_rows(elems)
     lines = jnp.concatenate([conductivity, capacity], axis=1).reshape(elems * 2, cells)
     lines = jnp.pad(lines, ((0, rows - depth * 8 - 2 * elems), (0, span - cells)))
-    raw = jnp.concatenate([cotangent.reshape(depth * 8, span), lines], axis=0)
     message = pl.pallas_call(
         functools.partial(pack_kernel, (depth, elems, cells)),
         out_shape=jax.ShapeDtypeStruct((rows, span), F32),
-        in_specs=[vmem],
+        in_specs=[vmem] * 2,
         out_specs=vmem,
         compiler_params=pltpu.CompilerParams(vmem_limit_bytes=4 * 2**20),
-    )(raw)
+    )(cotangent, lines)
 
     def move(value, pairs):
         return lax.ppermute(value, "plane", pairs) if pairs else jnp.zeros_like(value)

time: 42.7 us -> 42.7 us (level)
  other arithmetic: 1.61 us -> 0.77 us
  local copies, waits for them, and re-layouts: 0.05 us -> 0.89 us
    concatenate x1 -> x0, other arithmetic: 0.84 us -> none  [per_device(): raw = jnp.concatenate([cotangent.reshape(depth * 8, span), lines], axis=0)]
    unnamed x14 -> x16, local copies, waits for them, and re-layouts: 0.05 us -> 0.88 us
where the time goes in v8:
time: 42.7 us; the launch traced here: 42.5 us
  starting transfers between devices  20.6 us (48%)
  waiting for transfers between devices  12.1 us (28%)
  Pallas kernels  7.18 us (17%)
  local copies, waits for them, and re-layouts  0.89 us (2%)
  between operations  0.84 us (2%)
  other arithmetic  0.77 us (2%)
    ppermute x6, starting transfers between devices, move(): lax.ppermute(value, 'plane', pairs)  15.8 us
    all_to_all x1, waiting for transfers between devices, per_device(): shared = lax.all_to_all(info, ('height', 'plane'), 0, 0, tiled=True)  7.3 us
    pallas_call x1, Pallas kernels, per_device(): pl.pallas_call(functools.partial(basis_kernel, counts), out_shape=(jax.Sh...  5.88 us
    ppermute x6, waiting for transfers between devices, move(): lax.ppermute(value, 'plane', pairs)  3.81 us
    all_to_all x1, starting transfers between devices, per_device(): shared = lax.all_to_all(info, ('height', 'plane'), 0, 0, tiled=True)  3.6 us
    ppermute x5, starting transfers between devices, per_device(): lax.ppermute(arr, 'height', [(h, (h + turn) % height) for h in range(heig...  1.21 us
    pallas_call x1, Pallas kernels, per_device(): pl.pallas_call(combine_kernel, out_shape=(jax.ShapeDtypeStruct(cotangent....  1.05 us
    ppermute x5, waiting for transfers between devices, per_device(): lax.ppermute(arr, 'height', [(h, (h + turn) % height) for h in range(heig...  1.04 us
  transfers between devices with their start and end apart: 12, of which 6 were waited for; matrix products, arithmetic and copies ran while one was open for 0% of the time, Pallas kernels for 0%

profile of v8, /device:TPU:0, one launch (start us, length us, event | category | flops | bytes accessed | tf_op | source)
XLA Modules:
  0.0 42.5 jit_solution(6537601503130473678)
XLA Ops:
  0.6 0.7 %pad_maximum_fusion.2 = f32[2,2,16]{2,1,0:T(2,128)S(1)} fusion(f32[2,1,16]{2,1,0:T(1,128)} %param.12, f32[2,1,16]{2,1,0:T(1,128)} %param.11), kind=kLoop, calls=%fused_computation.2 | loop fusion | flops 64 | bytes 512 | tf_op jit(solution)/shard_map/concatenate | solution.py:489
  1.4 0.8 %copy-done.2 = f32[16,8,128]{2,1,0:T(8,128)S(1)} copy-done((f32[16,8,128]{2,1,0:T(8,128)S(1)}, f32[16,8,128]{2,1,0:T(8,128)}, u32[]{:S(2)}) %copy-start.2) | copy-done | bytes 65560
  2.2 0.2 shard_map.121
  2.4 3.0 %collective-permute-start = (f32[136,128]{1,0:T(8,128)S(1)}, f32[136,128]{1,0:T(8,128)S(1)}, u32[]{:S(2)}, u32[]{:S(2)}) collective-permute-start(f32[136,128]{1,0:T(8,128)S(1)} %shard_map.121), channel_id=1, source_target_pairs={{0,1},{1,0},{2,3},{3,2},{4,5},{5,4},{6,7},{7,6},{8,9},{9,8},{10,11... | collective-permute-start | bytes 208904 | tf_op jit(solution)/shard_map/ppermute | solution.py:500
  5.4 2.3 %collective-permute-done = f32[136,128]{1,0:T(8,128)S(1)} collective-permute-done((f32[136,128]{1,0:T(8,128)S(1)}, f32[136,128]{1,0:T(8,128)S(1)}, u32[]{:S(2)}, u32[]{:S(2)}) %collective-permute-start) | collective-permute-done | bytes 69664 | tf_op jit(solution)/shard_map/ppermute | solution.py:500
  7.7 2.1 %collective-permute-start.1 = (f32[272,128]{1,0:T(8,128)S(1)}, f32[272,128]{1,0:T(8,128)S(1)}, u32[]{:S(2)}, u32[]{:S(2)}) collective-permute-start(f32[272,128]{1,0:T(8,128)S(1)} %pad_maximum_fusion.1.refs_0_), channel_id=1, source_target_pairs={{0,2},{1,3},{2,0},{3,1},{4,6},{5,7},{6,4},{7,5},{8,10},{9,11},{10,... | collective-permute-start | bytes 417800 | tf_op jit(solution)/shard_map/ppermute | solution.py:500
  9.8 1.6 %collective-permute-start.2 = (f32[272,128]{1,0:T(8,128)S(1)}, f32[272,128]{1,0:T(8,128)S(1)}, u32[]{:S(2)}, u32[]{:S(2)}) collective-permute-start(f32[272,128]{1,0:T(8,128)S(1)} %pad_maximum_fusion.1.refs_0_), channel_id=1, source_target_pairs={{0,4},{1,5},{2,6},{3,7},{8,12},{9,13},{10,14},{11,15},{4,0},{5,1},... | collective-permute-start | bytes 417800 | tf_op jit(solution)/shard_map/ppermute | solution.py:500
  11.4 0.7 %collective-permute-start.3 = (f32[272,128]{1,0:T(8,128)S(1)}, f32[272,128]{1,0:T(8,128)S(1)}, u32[]{:S(2)}, u32[]{:S(2)}) collective-permute-start(f32[272,128]{1,0:T(8,128)S(1)} %pad_maximum_fusion.1.refs_0_), channel_id=1, source_target_pairs={{4,8},{5,9},{6,10},{7,11},{8,4},{9,5},{10,6},{11,7},{20,24},{21,25... | collective-permute-start | bytes 417800 | tf_op jit(solution)/shard_map/ppermute | solution.py:500
  12.1 0.8 %collective-permute-done.1.msg_ref.refs_1_ = f32[272,128]{1,0:T(8,128)S(1)} collective-permute-done((f32[272,128]{1,0:T(8,128)S(1)}, f32[272,128]{1,0:T(8,128)S(1)}, u32[]{:S(2)}, u32[]{:S(2)}) %collective-permute-start.1) | collective-permute-done | bytes 139296 | tf_op jit(solution)/shard_map/ppermute | solution.py:500
  12.9 5.5 %collective-permute-start.4 = (f32[272,128]{1,0:T(8,128)S(1)}, f32[272,128]{1,0:T(8,128)S(1)}, u32[]{:S(2)}, u32[]{:S(2)}) collective-permute-start(f32[272,128]{1,0:T(8,128)S(1)} %collective-permute-done.1.msg_ref.refs_1_), channel_id=1, source_target_pairs={{0,4},{1,5},{4,8},{5,9},{8,12},{9,13},{6,2},{7,3},{10,6},{11,7},{1... | collective-permute-start | bytes 417800 | tf_op jit(solution)/shard_map/ppermute | solution.py:500
  18.4 2.9 %collective-permute-start.5 = (f32[24,128]{1,0:T(8,128)S(1)}, f32[24,128]{1,0:T(8,128)S(1)}, u32[]{:S(2)}, u32[]{:S(2)}) collective-permute-start(f32[24,128]{1,0:T(8,128)S(1)} %shard_map.122), channel_id=1, source_target_pairs={{0,8},{4,12},{5,1},{9,5},{13,9},{2,6},{6,10},{10,14},{11,3},{15,7}... | collective-permute-start | bytes 36872 | tf_op jit(solution)/shard_map/ppermute | solution.py:500
  21.4 0.1 collective-permute-start.6
  21.5 0.5 %collective-permute-start.7 = (f32[272,128]{1,0:T(8,128)S(1)}, f32[272,128]{1,0:T(8,128)S(1)}, u32[]{:S(2)}, u32[]{:S(2)}) collective-permute-start(f32[272,128]{1,0:T(8,128)S(1)} %collective-permute-done.1.msg_ref.refs_1_), channel_id=1, source_target_pairs={{0,16},{16,0},{1,17},{17,1},{2,18},{18,2},{3,19},{19,3},{4,20},{20... | collective-permute-start | bytes 417800 | tf_op jit(solution)/shard_map/ppermute | solution.py:533
  22.0 0.1 collective-permute-start.8
  22.1 0.7 %collective-permute-done.5.edge_ref = f32[24,128]{1,0:T(8,128)S(1)} collective-permute-done((f32[24,128]{1,0:T(8,128)S(1)}, f32[24,128]{1,0:T(8,128)S(1)}, u32[]{:S(2)}, u32[]{:S(2)}) %collective-permute-start.5) | collective-permute-done | bytes 12320 | tf_op jit(solution)/shard_map/ppermute | solution.py:500
  22.8 0.0 copy-start.1
  22.8 0.0 copy-start.3
  22.9 0.6 %collective-permute-start.10 = (f32[408,128]{1,0:T(8,128)S(1)}, f32[408,128]{1,0:T(8,128)S(1)}, u32[]{:S(2)}, u32[]{:S(2)}) collective-permute-start(f32[408,128]{1,0:T(8,128)S(1)} %pad_maximum_fusion.refs_4_), channel_id=1, source_target_pairs={{0,16},{16,0},{1,17},{17,1},{2,18},{18,2},{3,19},{19,3},{4,20},{20... | collective-permute-start | bytes 626696 | tf_op jit(solution)/shard_map/ppermute | solution.py:533
  23.5 0.6 %collective-permute-done.9.refs_8_ = f32[272,128]{1,0:T(8,128)S(1)} collective-permute-done((f32[272,128]{1,0:T(8,128)S(1)}, f32[272,128]{1,0:T(8,128)S(1)}, u32[]{:S(2)}, u32[]{:S(2)}) %collective-permute-start.9) | collective-permute-done | bytes 139296 | tf_op jit(solution)/shard_map/ppermute | solution.py:533
  24.1 0.4 collective-permute-done.10.refs_9_
  24.6 5.9 %shard_map.124 = (f32[12,128,128]{2,1,0:T(8,128)S(1)}, f32[32,4,128]{2,1,0:T(4,128)}) custom-call(f32[272,128]{1,0:T(8,128)S(1)} %pad_maximum_fusion.1.refs_0_, f32[272,128]{1,0:T(8,128)S(1)} %collective-permute-done.1.msg_ref.refs_1_, f32[272,128]{1,0:T(8,128)S(1)} %collective-permute-done.2.refs_2_, f32[272,128]{1,0:T(8,128)S(1)} %collective-permute-done.3.refs_3_, ...), custom_call_target="tpu_custom_call" | custom-call | tf_op jit(solution)/shard_map/pallas_call | solution.py:539
  30.5 3.6 %all-to-all-start = ((f32[32,4,128]{2,1,0:T(4,128)}), f32[32,4,128]{2,1,0:T(4,128)S(1)}, u32[]{:S(2)}, u32[]{:S(2)}) async-start(f32[32,4,128]{2,1,0:T(4,128)} %get-tuple-element.5), calls=%async_computation | async-start | bytes 131072 | tf_op jit(solution)/shard_map/all_to_all | solution.py:553
  34.1 7.3 %all-to-all-done.info_ref = f32[32,4,128]{2,1,0:T(4,128)S(1)} async-done(((f32[32,4,128]{2,1,0:T(4,128)}), f32[32,4,128]{2,1,0:T(4,128)S(1)}, u32[]{:S(2)}, u32[]{:S(2)}) %all-to-all-start) | async-done | bytes 65568 | tf_op jit(solution)/shard_map/all_to_all | solution.py:553
  41.4 1.0 %shard_map.125 = (f32[16,8,128]{2,1,0:T(8,128)}, f32[16,8,128]{2,1,0:T(8,128)}, f32[2,128]{1,0:T(2,128)}) custom-call(f32[32,4,128]{2,1,0:T(4,128)S(1)} %all-to-all-done.info_ref, f32[12,128,128]{2,1,0:T(8,128)S(1)} %get-tuple-element.6.fields_ref, s32[2,128]{1,0:T(2,128)S(1)} %fusion.owner_ref, s32[2,128]{1,0:T(2,128)S(1)} %get-tuple-element.7.place_ref), custom_call_target="tpu_custom_call" | custom-call | tf_op jit(solution)/shard_map/pallas_call | solution.py:561
  (27 shorter events, 0.2 us)
Async XLA Ops:
  1.3 0.8 %copy-start.2 = (f32[16,8,128]{2,1,0:T(8,128)S(1)}, f32[16,8,128]{2,1,0:T(8,128)}, u32[]{:S(2)}) copy-start(f32[16,8,128]{2,1,0:T(8,128)} %cot_ref.1) | copy-start | bytes 196612
  2.4 5.3 %collective-permute-start = (f32[136,128]{1,0:T(8,128)S(1)}, f32[136,128]{1,0:T(8,128)S(1)}, u32[]{:S(2)}, u32[]{:S(2)}) collective-permute-start(f32[136,128]{1,0:T(8,128)S(1)} %shard_map.121), channel_id=1, source_target_pairs={{0,1},{1,0},{2,3},{3,2},{4,5},{5,4},{6,7},{7,6},{8,9},{9,8},{10,11... | collective-permute-start | bytes 208904 | tf_op jit(solution)/shard_map/ppermute | solution.py:500
  7.7 5.1 %collective-permute-start.1 = (f32[272,128]{1,0:T(8,128)S(1)}, f32[272,128]{1,0:T(8,128)S(1)}, u32[]{:S(2)}, u32[]{:S(2)}) collective-permute-start(f32[272,128]{1,0:T(8,128)S(1)} %pad_maximum_fusion.1.refs_0_), channel_id=1, source_target_pairs={{0,2},{1,3},{2,0},{3,1},{4,6},{5,7},{6,4},{7,5},{8,10},{9,11},{10,... | collective-permute-start | bytes 417800 | tf_op jit(solution)/shard_map/ppermute | solution.py:500
  9.8 11.6 %collective-permute-start.2 = (f32[272,128]{1,0:T(8,128)S(1)}, f32[272,128]{1,0:T(8,128)S(1)}, u32[]{:S(2)}, u32[]{:S(2)}) collective-permute-start(f32[272,128]{1,0:T(8,128)S(1)} %pad_maximum_fusion.1.refs_0_), channel_id=1, source_target_pairs={{0,4},{1,5},{2,6},{3,7},{8,12},{9,13},{10,14},{11,15},{4,0},{5,1},... | collective-permute-start | bytes 417800 | tf_op jit(solution)/shard_map/ppermute | solution.py:500
  11.4 10.5 %collective-permute-start.3 = (f32[272,128]{1,0:T(8,128)S(1)}, f32[272,128]{1,0:T(8,128)S(1)}, u32[]{:S(2)}, u32[]{:S(2)}) collective-permute-start(f32[272,128]{1,0:T(8,128)S(1)} %pad_maximum_fusion.1.refs_0_), channel_id=1, source_target_pairs={{4,8},{5,9},{6,10},{7,11},{8,4},{9,5},{10,6},{11,7},{20,24},{21,25... | collective-permute-start | bytes 417800 | tf_op jit(solution)/shard_map/ppermute | solution.py:500
  12.9 10.0 %collective-permute-start.4 = (f32[272,128]{1,0:T(8,128)S(1)}, f32[272,128]{1,0:T(8,128)S(1)}, u32[]{:S(2)}, u32[]{:S(2)}) collective-permute-start(f32[272,128]{1,0:T(8,128)S(1)} %collective-permute-done.1.msg_ref.refs_1_), channel_id=1, source_target_pairs={{0,4},{1,5},{4,8},{5,9},{8,12},{9,13},{6,2},{7,3},{10,6},{11,7},{1... | collective-permute-start | bytes 417800 | tf_op jit(solution)/shard_map/ppermute | solution.py:500
  18.4 4.3 %collective-permute-start.5 = (f32[24,128]{1,0:T(8,128)S(1)}, f32[24,128]{1,0:T(8,128)S(1)}, u32[]{:S(2)}, u32[]{:S(2)}) collective-permute-start(f32[24,128]{1,0:T(8,128)S(1)} %shard_map.122), channel_id=1, source_target_pairs={{0,8},{4,12},{5,1},{9,5},{13,9},{2,6},{6,10},{10,14},{11,3},{15,7}... | collective-permute-start | bytes 36872 | tf_op jit(solution)/shard_map/ppermute | solution.py:500
  21.4 2.1 %collective-permute-start.6 = (f32[272,128]{1,0:T(8,128)S(1)}, f32[272,128]{1,0:T(8,128)S(1)}, u32[]{:S(2)}, u32[]{:S(2)}) collective-permute-start(f32[272,128]{1,0:T(8,128)S(1)} %pad_maximum_fusion.1.refs_0_), channel_id=1, source_target_pairs={{0,16},{16,0},{1,17},{17,1},{2,18},{18,2},{3,19},{19,3},{4,20},{20... | collective-permute-start | bytes 417800 | tf_op jit(solution)/shard_map/ppermute | solution.py:533
  21.5 2.0 %collective-permute-start.7 = (f32[272,128]{1,0:T(8,128)S(1)}, f32[272,128]{1,0:T(8,128)S(1)}, u32[]{:S(2)}, u32[]{:S(2)}) collective-permute-start(f32[272,128]{1,0:T(8,128)S(1)} %collective-permute-done.1.msg_ref.refs_1_), channel_id=1, source_target_pairs={{0,16},{16,0},{1,17},{17,1},{2,18},{18,2},{3,19},{19,3},{4,20},{20... | collective-permute-start | bytes 417800 | tf_op jit(solution)/shard_map/ppermute | solution.py:533
  22.0 1.6 %collective-permute-start.8 = (f32[272,128]{1,0:T(8,128)S(1)}, f32[272,128]{1,0:T(8,128)S(1)}, u32[]{:S(2)}, u32[]{:S(2)}) collective-permute-start(f32[272,128]{1,0:T(8,128)S(1)} %collective-permute-done.2.refs_2_), channel_id=1, source_target_pairs={{0,16},{16,0},{1,17},{17,1},{2,18},{18,2},{3,19},{19,3},{4,20},{20... | collective-permute-start | bytes 417800 | tf_op jit(solution)/shard_map/ppermute | solution.py:533
  22.8 1.4 %collective-permute-start.9 = (f32[272,128]{1,0:T(8,128)S(1)}, f32[272,128]{1,0:T(8,128)S(1)}, u32[]{:S(2)}, u32[]{:S(2)}) collective-permute-start(f32[272,128]{1,0:T(8,128)S(1)} %collective-permute-done.3.refs_3_), channel_id=1, source_target_pairs={{0,16},{16,0},{1,17},{17,1},{2,18},{18,2},{3,19},{19,3},{4,20},{20... | collective-permute-start | bytes 417800 | tf_op jit(solution)/shard_map/ppermute | solution.py:533
  22.8 0.7 %copy-start.7 = (s32[2,128]{1,0:T(2,128)S(1)}, s32[2,128]{1,0:T(2,128)}, u32[]{:S(2)}) copy-start(s32[2,128]{1,0:T(2,128)} %param.13) | copy-start | bytes 3076
  22.8 1.8 %copy-start = (bf16[256,256]{1,0:T(8,128)(2,1)S(1)}, bf16[256,256]{1,0:T(8,128)(2,1)}, u32[]{:S(2)}) copy-start(bf16[256,256]{1,0:T(8,128)(2,1)} %constant.76.clone.refs_12_) | copy-start | bytes 393220
  22.8 1.8 %copy-start.1 = (bf16[256,256]{1,0:T(8,128)(2,1)S(1)}, bf16[256,256]{1,0:T(8,128)(2,1)}, u32[]{:S(2)}) copy-start(bf16[256,256]{1,0:T(8,128)(2,1)} %constant.77.clone.refs_13_) | copy-start | bytes 393220
  22.8 1.7 %copy-start.3 = (bf16[192,128]{1,0:T(8,128)(2,1)S(1)}, bf16[192,128]{1,0:T(8,128)(2,1)}, u32[]{:S(2)}) copy-start(bf16[192,128]{1,0:T(8,128)(2,1)} %constant.74.clone.refs_10_) | copy-start | bytes 147460
  22.8 1.7 %copy-start.4 = (f32[8,8,128]{2,1,0:T(8,128)S(1)}, f32[8,8,128]{2,1,0:T(8,128)}, u32[]{:S(2)}) copy-start(f32[8,8,128]{2,1,0:T(8,128)} %constant.78.clone.refs_14_) | copy-start | bytes 98308
  22.8 1.7 %copy-start.5 = (f32[8,8,128]{2,1,0:T(8,128)S(1)}, f32[8,8,128]{2,1,0:T(8,128)}, u32[]{:S(2)}) copy-start(f32[8,8,128]{2,1,0:T(8,128)} %constant.79.clone.refs_15_) | copy-start | bytes 98308
  22.9 1.7 %copy-start.6 = (bf16[48,128]{1,0:T(8,128)(2,1)S(1)}, bf16[48,128]{1,0:T(8,128)(2,1)}, u32[]{:S(2)}) copy-start(bf16[48,128]{1,0:T(8,128)(2,1)} %constant.75.clone.refs_11_) | copy-start | bytes 36868
  22.9 1.6 %collective-permute-start.10 = (f32[408,128]{1,0:T(8,128)S(1)}, f32[408,128]{1,0:T(8,128)S(1)}, u32[]{:S(2)}, u32[]{:S(2)}) collective-permute-start(f32[408,128]{1,0:T(8,128)S(1)} %pad_maximum_fusion.refs_4_), channel_id=1, source_target_pairs={{0,16},{16,0},{1,17},{17,1},{2,18},{18,2},{3,19},{19,3},{4,20},{20... | collective-permute-start | bytes 626696 | tf_op jit(solution)/shard_map/ppermute | solution.py:533
  30.5 10.9 %all-to-all-start = ((f32[32,4,128]{2,1,0:T(4,128)}), f32[32,4,128]{2,1,0:T(4,128)S(1)}, u32[]{:S(2)}, u32[]{:S(2)}) async-start(f32[32,4,128]{2,1,0:T(4,128)} %get-tuple-element.5), calls=%async_computation | async-start | bytes 131072 | tf_op jit(solution)/shard_map/all_to_all | solution.py:553
